TPU v7x, 32 devices: a whole 2x2x4 slice. The times are simulated.
32 devices in a mesh: dp: 8 (over y, x, core), sub: 4 (over z).
Axes of the slice: x: 2, y: 2, z: 4, core: 2. Of those that a mesh axis runs over, the one named last changes fastest.
Arguments:
- inputs: float32 [147456, 256], P(('dp', 'sub')), may hold values from -6 to 6
- matrices: bfloat16 [2, 3072, 256], P(None, ('dp', 'sub'))
- vectors: bfloat16 [2, 2560], P(None, ('dp', 'sub'))
- lengths: int32 [128], P(('dp', 'sub')), may hold values from 576 to 1152, as said below
- cotangent: float32 [147456, 256], P(('dp', 'sub')), may hold values from -6 to 6
Outputs:
- outputs: float32 [147456, 256], P(('dp', 'sub'))
- grad_inputs: float32 [147456, 256], P(('dp', 'sub'))
- grad_matrices: float32 [2, 3072, 256], P(None, ('dp', 'sub'))
- grad_vectors: float32 [2, 2560], P(None, ('dp', 'sub'))
Inputs may be any that keep to these rules, and one draw needn't show every extreme that they name: `lengths`: real tokens of each image, counted from its start; the rest is padding.
All inputs are finite; a program needn't handle non-finite values.
Results may differ from a plain program's by a relative error of at most 0.015.
The roundings to bfloat16 on the way count: a program that leaves them out, or rounds other values in their place, can miss the bound.
Values may be sent and summed in bfloat16 or wider, within the bound.
A program may use at most 320 MiB of HBM per device.

v0:
```python
from functools import partial

import jax
import jax.numpy as jnp
from jax import lax
from jax.sharding import PartitionSpec as P

HEAD_COUNT = 2
ROW_LENGTH = 96
IMAGE_ROWS = 12


def product(left, right, left_dim, right_dim):
    return lax.dot_general(
        left, right, (((left_dim,), (right_dim,)), ((), ())), preferred_element_type=jnp.float32
    )


def normalize(source, gains, shifts):
    average = jnp.mean(source, -1, keepdims=True)
    centred = source - average
    variance = jnp.mean(centred * centred, -1, keepdims=True)
    return centred * lax.rsqrt(variance + 1e-05) * gains + shifts


def regroup(input_tensor, token_layout):
    grouped_heads = input_tensor.reshape(
        IMAGE_ROWS, ROW_LENGTH, HEAD_COUNT, input_tensor.shape[1] // HEAD_COUNT
    )
    if token_layout == "column":
        grouped_heads = jnp.swapaxes(grouped_heads, 0, 1)
    return grouped_heads


def ungroup(input_tensor, token_layout):
    if token_layout == "column":
        input_tensor = jnp.swapaxes(input_tensor, 0, 1)
    return input_tensor.reshape(IMAGE_ROWS * ROW_LENGTH, -1)


def causal_mask(token_layout):
    token_span = ROW_LENGTH if token_layout == "row" else IMAGE_ROWS
    return jnp.tril(jnp.ones((token_span, token_span), bool))


def unpack(matrix, vector):
    model_width = matrix.shape[1]
    hidden_units = (matrix.shape[0] - 4 * model_width) // 2
    floats = vector.astype(jnp.float32)
    return (
        matrix[: 3 * model_width],
        matrix[3 * model_width : 4 * model_width],
        matrix[4 * model_width : 4 * model_width + hidden_units],
        matrix[4 * model_width + hidden_units :],
        floats[:model_width],
        floats[model_width : 2 * model_width],
        floats[2 * model_width : 3 * model_width],
        floats[3 * model_width : 4 * model_width],
        floats[4 * model_width : 5 * model_width],
        floats[5 * model_width : 6 * model_width],
        floats[6 * model_width :],
    )


def fetch_forward(matrices, vectors, layer_index):
    return (
        lax.all_gather(matrices[layer_index], ("dp", "sub"), axis=0, tiled=True),
        lax.all_gather(vectors[layer_index], ("dp", "sub"), axis=0, tiled=True),
    )


def fetch_backward(matrices, vectors, layer_index):
    return (
        lax.all_gather(matrices[layer_index], ("dp", "sub"), axis=0, tiled=True),
        lax.all_gather(vectors[layer_index], ("dp", "sub"), axis=0, tiled=True),
    )


def split_heads(packed, token_layout):
    model_width = packed.shape[1] // 3
    queries = regroup(packed[:, :model_width], token_layout)
    key_rows = regroup(packed[:, model_width : 2 * model_width], token_layout)
    value_rows = regroup(packed[:, 2 * model_width :], token_layout)
    return (queries, key_rows, value_rows)


def attend_forward(packed, token_layout):
    queries, key_rows, value_rows = split_heads(packed, token_layout)
    head_size = queries.shape[3]
    raw_scores = jnp.einsum(
        "glhd,gmhd->ghlm", queries, key_rows, preferred_element_type=jnp.float32
    )
    scores = jnp.where(causal_mask(token_layout), raw_scores * head_size ** (-0.5), -1e30)
    row_peak = jnp.max(scores, -1, keepdims=True)
    exponent = jnp.exp(scores - row_peak)
    totals = jnp.sum(exponent, -1, keepdims=True)
    attention = (exponent / totals).astype(jnp.bfloat16)
    log_total = row_peak + jnp.log(totals)
    mixture = jnp.einsum(
        "ghlm,gmhd->glhd", attention, value_rows, preferred_element_type=jnp.float32
    )
    return (ungroup(mixture, token_layout), log_total)


def attend_backward(packed, log_total, grad_mixture, token_layout):
    queries, key_rows, value_rows = split_heads(packed, token_layout)
    head_size = queries.shape[3]
    grad_output = regroup(grad_mixture, token_layout)
    raw_scores = jnp.einsum(
        "glhd,gmhd->ghlm", queries, key_rows, preferred_element_type=jnp.float32
    )
    scores = jnp.where(causal_mask(token_layout), raw_scores * head_size ** (-0.5), -1e30)
    attention = jnp.exp(scores - log_total)
    attention_low = attention.astype(jnp.bfloat16)
    grad_attention = jnp.einsum(
        "glhd,gmhd->ghlm", grad_output, value_rows, preferred_element_type=jnp.float32
    )
    grad_values = jnp.einsum(
        "ghlm,glhd->gmhd", attention_low, grad_output, preferred_element_type=jnp.float32
    )
    grad_scores = attention * (
        grad_attention - jnp.sum(attention * grad_attention, -1, keepdims=True)
    )
    grad_raw = (grad_scores * head_size ** (-0.5)).astype(jnp.bfloat16)
    grad_queries = jnp.einsum(
        "ghlm,gmhd->glhd", grad_raw, key_rows, preferred_element_type=jnp.float32
    )
    grad_keys = jnp.einsum("ghlm,glhd->gmhd", grad_raw, queries, preferred_element_type=jnp.float32)
    joined = [
        ungroup(grad_queries, token_layout),
        ungroup(grad_keys, token_layout),
        ungroup(grad_values, token_layout),
    ]
    return jnp.concatenate(joined, axis=1).astype(jnp.bfloat16)


def layer_forward(current, layer_parts, token_layout):
    (
        w_qkv,
        w_out,
        w_up,
        w_down,
        gain_attn,
        shift_attn,
        bias_out,
        gain_ffn,
        shift_ffn,
        bias_down,
        bias_up,
    ) = layer_parts
    normed = normalize(current, gain_attn, shift_attn).astype(jnp.bfloat16)
    packed = product(normed, w_qkv, 1, 1).astype(jnp.bfloat16)
    mixture, log_total = attend_forward(packed, token_layout)
    mixture_low = mixture.astype(jnp.bfloat16)
    middle = current + product(mixture_low, w_out, 1, 1) + bias_out
    normed_two = normalize(middle, gain_ffn, shift_ffn).astype(jnp.bfloat16)
    up_pre = product(normed_two, w_up, 1, 1) + bias_up
    active = jax.nn.gelu(up_pre, approximate=False).astype(jnp.bfloat16)
    result = middle + product(active, w_down, 1, 0) + bias_down
    return (result, (current, packed, log_total, mixture_low, middle, up_pre))


def layer_backward(grad_result, layer_parts, saved_values, token_layout):
    (
        w_qkv,
        w_out,
        w_up,
        w_down,
        gain_attn,
        shift_attn,
        bias_out,
        gain_ffn,
        shift_ffn,
        bias_down,
        bias_up,
    ) = layer_parts
    current, packed, log_total, mixture_low, middle, up_pre = saved_values
    grad_bias_down = jnp.sum(grad_result, 0)
    grad_low = grad_result.astype(jnp.bfloat16)
    active = jax.nn.gelu(up_pre, approximate=False).astype(jnp.bfloat16)
    grad_w_down = product(active, grad_low, 0, 0)
    grad_active = product(grad_low, w_down, 1, 1)
    grad_up = jax.vjp(partial(jax.nn.gelu, approximate=False), up_pre)[1](grad_active)[0]
    grad_bias_up = jnp.sum(grad_up, 0)
    grad_up_low = grad_up.astype(jnp.bfloat16)
    normed_two, second_pull = jax.vjp(normalize, middle, gain_ffn, shift_ffn)
    grad_w_up = product(grad_up_low, normed_two.astype(jnp.bfloat16), 0, 0)
    grad_middle, grad_gain_ffn, grad_shift_ffn = second_pull(product(grad_up_low, w_up, 1, 0))
    grad_middle = grad_result + grad_middle
    grad_bias_out = jnp.sum(grad_middle, 0)
    middle_low = grad_middle.astype(jnp.bfloat16)
    grad_w_out = product(middle_low, mixture_low, 0, 0)
    grad_mixture = product(middle_low, w_out, 1, 0).astype(jnp.bfloat16)
    grad_packed = attend_backward(packed, log_total, grad_mixture, token_layout)
    normed_one, first_pull = jax.vjp(normalize, current, gain_attn, shift_attn)
    grad_w_qkv = product(grad_packed, normed_one.astype(jnp.bfloat16), 0, 0)
    grad_current, grad_gain_attn, grad_shift_attn = first_pull(product(grad_packed, w_qkv, 1, 0))
    grad_current = grad_middle + grad_current
    grad_matrix = jnp.concatenate([grad_w_qkv, grad_w_out, grad_w_up, grad_w_down], axis=0)
    grad_vector = jnp.concatenate(
        [
            grad_gain_attn,
            grad_shift_attn,
            grad_bias_out,
            grad_gain_ffn,
            grad_shift_ffn,
            grad_bias_down,
            grad_bias_up,
        ]
    )
    return (grad_current, grad_matrix, grad_vector)


def run_forward(layer_parts, token_layout, stack):

    def image_step(totals, current):
        result, saved_values = layer_forward(current, layer_parts, token_layout)
        return (totals, (result, saved_values))

    unused, (results, saved_values) = lax.scan(image_step, jnp.zeros((), jnp.float32), stack)
    return (results, saved_values)


def run_backward(layer_parts, token_layout, saved_stack, grad_stack):
    matrix_rows = (
        layer_parts[0].shape[0]
        + layer_parts[1].shape[0]
        + layer_parts[2].shape[0]
        + layer_parts[3].shape[0]
    )
    model_width = layer_parts[0].shape[1]
    vector_len = 6 * model_width + layer_parts[10].shape[0]
    start_totals = (
        jnp.zeros((matrix_rows, model_width), jnp.float32),
        jnp.zeros((vector_len,), jnp.float32),
    )

    def image_step(totals, scan_items):
        saved_values, grad_result = scan_items
        grad_current, grad_matrix, grad_vector = layer_backward(
            grad_result, layer_parts, saved_values, token_layout
        )
        return ((totals[0] + grad_matrix, totals[1] + grad_vector), grad_current)

    (grad_matrix, grad_vector), grad_inputs = lax.scan(
        image_step, start_totals, (saved_stack, grad_stack)
    )
    return (grad_matrix, grad_vector, grad_inputs)


def body(inputs, matrices, vectors, lengths, cotangent):
    image_count = lengths.shape[0]
    seq_len = inputs.shape[0] // image_count
    model_width = inputs.shape[1]
    images = inputs.reshape(image_count, seq_len, model_width)
    live_rows = (jnp.arange(seq_len)[None, :] < lengths[:, None]).astype(jnp.float32)[:, :, None]
    layouts = ("row", "column")
    forward_parts = [
        unpack(*fetch_forward(matrices, vectors, layer_index)) for layer_index in range(2)
    ]
    current = images
    saved_all = []
    for layer_index in range(2):
        current, saved_values = run_forward(
            forward_parts[layer_index], layouts[layer_index], current
        )
        saved_all.append(saved_values)
    outputs = current * live_rows
    backward_parts = [
        unpack(*fetch_backward(matrices, vectors, layer_index)) for layer_index in range(2)
    ]
    upstream = cotangent.reshape(image_count, seq_len, model_width) * live_rows
    grad_pieces = [None, None]
    for layer_index in (1, 0):
        grad_matrix, grad_vector, upstream = run_backward(
            backward_parts[layer_index], layouts[layer_index], saved_all[layer_index], upstream
        )
        grad_pieces[layer_index] = (
            lax.psum_scatter(grad_matrix, ("dp", "sub"), scatter_dimension=0, tiled=True),
            lax.psum_scatter(grad_vector, ("dp", "sub"), scatter_dimension=0, tiled=True),
        )
    stacked_matrix = jnp.stack([grad_pieces[0][0], grad_pieces[1][0]])
    stacked_vector = jnp.stack([grad_pieces[0][1], grad_pieces[1][1]])
    return (
        outputs.reshape(image_count * seq_len, model_width),
        upstream.reshape(image_count * seq_len, model_width),
        stacked_matrix,
        stacked_vector,
    )


def solution(mesh):
    return jax.shard_map(
        body,
        mesh=mesh,
        in_specs=(
            P(("dp", "sub"), None),
            P(None, ("dp", "sub"), None),
            P(None, ("dp", "sub")),
            P(("dp", "sub")),
            P(("dp", "sub"), None),
        ),
        out_specs=(
            P(("dp", "sub"), None),
            P(("dp", "sub"), None),
            P(None, ("dp", "sub"), None),
            P(None, ("dp", "sub")),
        ),
        check_vma=False,
    )
```

profile of v0, /device:TPU:0, one launch (start us, length us, event | category | flops | bytes accessed | tf_op | source)
XLA Modules:
  0.0 1373.2 jit_solution(13195616264849055780)
XLA Ops:
  10.7 42.2 %all-reduce.5 = (bf16[2560]{0:T(1024)(128)(2,1)S(1)}, bf16[2560]{0:T(1024)(128)(2,1)S(1)}) all-reduce(bf16[2560]{0:T(1024)(128)(2,1)S(1)} %dynamic-update-slice, bf16[2560]{0:T(1024)(128)(2,1)S(1)} %dynamic-update-slice.1), channel_id=2, replica_groups=mesh['dp'=8,'sub'=4] {'dp','sub'}, use_global_device_ids=true, to_apply=%add | all-reduce | flops 5120 | bytes 20480
  55.5 13.9 %all-gather.7.cloned.1.call-done = bf16[1,3072,256]{2,1,0:T(8,128)(2,1)} async-done(((bf16[1,96,256]{2,1,0:T(8,128)(2,1)}), bf16[1,3072,256]{2,1,0:T(8,128)(2,1)}) %all-gather.7.cloned.1.call-update) | async-done | bytes 1572880 | tf_op jit(solution)/shard_map/all_gather | solution.py:67
  74.3 8.9 broadcast.869.clone
  93.0 125.2 %while.70 = (s32[]{:T(128)}, f32[4,1152,256]{1,2,0:T(8,128)}, bf16[4,1152,768]{2,1,0:T(8,128)(2,1)}, f32[4,12,2,96,1]{3,2,1,4,0:T(2,128)}, bf16[4,1152,256]{2,1,...) while((s32[]{:T(128)}, f32[4,1152,256]{1,2,0:T(8,128)}, ...), condition=%wide.region_7.8_spmd, body=%wide.region_0.7_spmd.sunk | while | flops 2012488704 | bytes 55406032 | solution.py:220
  104.5 4.2 bitcast_dynamic-update-slice_fusion.33
  108.7 12.6 fusion.563
  135.6 4.3 bitcast_dynamic-update-slice_fusion.33
  139.9 12.7 fusion.563
  166.8 4.2 bitcast_dynamic-update-slice_fusion.33
  171.0 12.6 fusion.563
  197.9 4.2 bitcast_dynamic-update-slice_fusion.33
  202.1 12.6 fusion.563
  223.9 8.9 broadcast.869
  242.8 137.5 %while.71 = (s32[]{:T(128)}, f32[4,1152,256]{2,1,0:T(8,128)}, bf16[4,1152,768]{2,1,0:T(8,128)(2,1)}, f32[4,96,2,12,1]{3,2,1,4,0:T(2,128)}, bf16[4,1152,256]{2,1,...) while((s32[]{:T(128)}, f32[4,1152,256]{2,1,0:T(8,128)}, ...), condition=%wide.region_15.16_spmd, body=%wide.region_8.15_spmd.sunk | while | flops 1911840896 | bytes 51120096 | solution.py:220
  254.8 4.1 bitcast_dynamic-update-slice_fusion.37
  258.9 12.6 fusion.575
  289.1 4.2 bitcast_dynamic-update-slice_fusion.37
  293.2 12.6 fusion.575
  323.5 4.3 bitcast_dynamic-update-slice_fusion.37
  327.7 12.6 fusion.575
  357.9 4.1 bitcast_dynamic-update-slice_fusion.37
  362.0 12.6 fusion.575
  380.4 6.5 broadcast_multiply_fusion.8
  389.4 426.7 %while.72 = (s32[]{:T(128)}, f32[3072,256]{1,0:T(8,128)}, f32[2560]{0:T(1024)}, f32[4,1152,256]{2,1,0:T(8,128)}, bf16[4,1152,768]{2,1,0:T(8,128)(2,1)}, /*index=...) while((s32[]{:T(128)}, f32[3072,256]{1,0:T(8,128)}, ...), condition=%wide.region_33.34_spmd.clone, body=%wide.region_16.33_spmd.clone.sunk | while | flops 3844096512 | bytes 152976240 | solution.py:245
  407.9 13.8 %fusion.600 = (f32[1024]{0:T(1024)}, bf16[1152,1024]{1,0:T(8,128)(2,1)S(1)}) fusion(bf16[1024,256]{1,0:T(8,128)(2,1)} %get-tuple-element.1802, f32[4,1152,256]{2,1,0:T(8,128)} %get-tuple-element.1800, s32[]{:T(128)} %get-tuple-element.1773, f32[4,1152,1024]{2,1,0:T(8,128)} %get-tuple-element.1801), kind=kOutput, calls=%fused_computation.611.clone.1 | convolution fusion | flops 690093056 | bytes 8197120 | tf_op jit(solution)/shard_map/while/body/eval_jaxpr/dot_general | solution.py:14
  444.1 4.8 fusion.610
  450.5 4.9 fusion.609
  458.6 3.6 fusion.612
  489.1 12.8 fusion.599
  506.7 13.8 %fusion.600 = (f32[1024]{0:T(1024)}, bf16[1152,1024]{1,0:T(8,128)(2,1)S(1)}) fusion(bf16[1024,256]{1,0:T(8,128)(2,1)} %get-tuple-element.1802, f32[4,1152,256]{2,1,0:T(8,128)} %get-tuple-element.1800, s32[]{:T(128)} %get-tuple-element.1773, f32[4,1152,1024]{2,1,0:T(8,128)} %get-tuple-element.1801), kind=kOutput, calls=%fused_computation.611.clone.1 | convolution fusion | flops 690093056 | bytes 8197120 | tf_op jit(solution)/shard_map/while/body/eval_jaxpr/dot_general | solution.py:14
  542.9 4.8 fusion.610
  549.3 4.9 fusion.609
  557.4 3.6 fusion.612
  587.9 12.8 fusion.599
  605.5 13.8 %fusion.600 = (f32[1024]{0:T(1024)}, bf16[1152,1024]{1,0:T(8,128)(2,1)S(1)}) fusion(bf16[1024,256]{1,0:T(8,128)(2,1)} %get-tuple-element.1802, f32[4,1152,256]{2,1,0:T(8,128)} %get-tuple-element.1800, s32[]{:T(128)} %get-tuple-element.1773, f32[4,1152,1024]{2,1,0:T(8,128)} %get-tuple-element.1801), kind=kOutput, calls=%fused_computation.611.clone.1 | convolution fusion | flops 690093056 | bytes 8197120 | tf_op jit(solution)/shard_map/while/body/eval_jaxpr/dot_general | solution.py:14
  641.7 4.8 fusion.610
  648.1 4.9 fusion.609
  656.1 3.6 fusion.612
  686.7 12.8 fusion.599
  704.3 13.8 %fusion.600 = (f32[1024]{0:T(1024)}, bf16[1152,1024]{1,0:T(8,128)(2,1)S(1)}) fusion(bf16[1024,256]{1,0:T(8,128)(2,1)} %get-tuple-element.1802, f32[4,1152,256]{2,1,0:T(8,128)} %get-tuple-element.1800, s32[]{:T(128)} %get-tuple-element.1773, f32[4,1152,1024]{2,1,0:T(8,128)} %get-tuple-element.1801), kind=kOutput, calls=%fused_computation.611.clone.1 | convolution fusion | flops 690093056 | bytes 8197120 | tf_op jit(solution)/shard_map/while/body/eval_jaxpr/dot_general | solution.py:14
  740.5 4.8 fusion.610
  746.9 4.9 fusion.609
  755.0 3.6 fusion.612
  785.5 12.8 fusion.599
  818.7 339.9 %while.73 = (s32[]{:T(128)}, f32[3072,256]{1,0:T(8,128)}, f32[2560]{0:T(1024)}, f32[4,1152,256]{2,1,0:T(8,128)}, bf16[4,1152,768]{2,1,0:T(8,128)(2,1)}, /*index=...) while((s32[]{:T(128)}, f32[3072,256]{1,0:T(8,128)}, ...), condition=%wide.region_51.52_spmd.clone, body=%wide.region_34.51_spmd.clone.sunk | while | flops 4094541312 | bytes 153705648 | solution.py:245
  820.9 13.8 %fusion.640 = (f32[1024]{0:T(1024)}, bf16[1152,1024]{1,0:T(8,128)(2,1)S(1)}) fusion(bf16[1024,256]{1,0:T(8,128)(2,1)} %get-tuple-element.1865, f32[4,1152,256]{2,1,0:T(8,128)} %get-tuple-element.1863, s32[]{:T(128)} %get-tuple-element.1836, f32[4,1152,1024]{2,1,0:T(8,128)} %get-tuple-element.1864), kind=kOutput, calls=%fused_computation.613.clone.1 | convolution fusion | flops 690093056 | bytes 8197120 | tf_op jit(solution)/shard_map/while/body/eval_jaxpr/dot_general | solution.py:14
  857.4 4.0 fusion.651
  863.0 4.0 fusion.650
  888.4 12.8 fusion.639
  905.9 13.8 %fusion.640 = (f32[1024]{0:T(1024)}, bf16[1152,1024]{1,0:T(8,128)(2,1)S(1)}) fusion(bf16[1024,256]{1,0:T(8,128)(2,1)} %get-tuple-element.1865, f32[4,1152,256]{2,1,0:T(8,128)} %get-tuple-element.1863, s32[]{:T(128)} %get-tuple-element.1836, f32[4,1152,1024]{2,1,0:T(8,128)} %get-tuple-element.1864), kind=kOutput, calls=%fused_computation.613.clone.1 | convolution fusion | flops 690093056 | bytes 8197120 | tf_op jit(solution)/shard_map/while/body/eval_jaxpr/dot_general | solution.py:14
  942.4 4.0 fusion.651
  948.0 4.0 fusion.650
  973.3 12.8 fusion.639
  990.8 13.8 %fusion.640 = (f32[1024]{0:T(1024)}, bf16[1152,1024]{1,0:T(8,128)(2,1)S(1)}) fusion(bf16[1024,256]{1,0:T(8,128)(2,1)} %get-tuple-element.1865, f32[4,1152,256]{2,1,0:T(8,128)} %get-tuple-element.1863, s32[]{:T(128)} %get-tuple-element.1836, f32[4,1152,1024]{2,1,0:T(8,128)} %get-tuple-element.1864), kind=kOutput, calls=%fused_computation.613.clone.1 | convolution fusion | flops 690093056 | bytes 8197120 | tf_op jit(solution)/shard_map/while/body/eval_jaxpr/dot_general | solution.py:14
  1027.3 4.0 fusion.651
  1033.0 4.0 fusion.650
  1058.3 12.8 fusion.639
  1075.8 13.8 %fusion.640 = (f32[1024]{0:T(1024)}, bf16[1152,1024]{1,0:T(8,128)(2,1)S(1)}) fusion(bf16[1024,256]{1,0:T(8,128)(2,1)} %get-tuple-element.1865, f32[4,1152,256]{2,1,0:T(8,128)} %get-tuple-element.1863, s32[]{:T(128)} %get-tuple-element.1836, f32[4,1152,1024]{2,1,0:T(8,128)} %get-tuple-element.1864), kind=kOutput, calls=%fused_computation.613.clone.1 | convolution fusion | flops 690093056 | bytes 8197120 | tf_op jit(solution)/shard_map/while/body/eval_jaxpr/dot_general | solution.py:14
  1112.3 4.0 fusion.651
  1117.9 4.0 fusion.650
  1143.3 12.8 fusion.639
  1159.3 39.1 %all-reduce.4 = (f32[2560]{0:T(1024)S(1)}, f32[2560]{0:T(1024)S(1)}) all-reduce(f32[2560]{0:T(1024)S(1)} %copy-done.19, f32[2560]{0:T(1024)S(1)} %copy-done.18), channel_id=9, replica_groups=mesh['dp'=8,'sub'=4] {'dp','sub'}, use_global_device_ids=true, to_apply=%region_55.56.clone | all-reduce | flops 5120 | bytes 40960
  1199.1 60.0 %reduce-scatter.3.cloned.1.call-done = f32[96,256]{1,0:T(8,128)} async-done(((f32[3072,256]{1,0:T(8,128)}), f32[96,256]{1,0:T(8,128)}) %reduce-scatter.3.cloned.1.call-update) | async-done | bytes 98320 | tf_op jit(solution)/shard_map/reduce_scatter | solution.py:279
  1259.1 105.8 %reduce-scatter.5.cloned.1.call-done = f32[96,256]{1,0:T(8,128)} async-done(((f32[3072,256]{1,0:T(8,128)}), f32[96,256]{1,0:T(8,128)}) %reduce-scatter.5.cloned.1.call-update) | async-done | bytes 98320 | tf_op jit(solution)/shard_map/reduce_scatter | solution.py:279
  (971 shorter events, 605.2 us)
Async XLA Ops:
  7.2 62.2 %all-gather.7.cloned.1.call-start = ((), (), s32[]{:S(2)}) async-start(), calls=%async_computation.4 | async-start | bytes 1622016 | tf_op jit(solution)/shard_map/all_gather | solution.py:67
  8.7 209.5 %all-gather.9.cloned.1.call-start = ((), (), s32[]{:S(2)}) async-start(), calls=%async_computation.5 | async-start | bytes 1622016 | tf_op jit(solution)/shard_map/all_gather | solution.py:67
  9.5 1249.6 %reduce-scatter.3.cloned.1.call-start = ((), (), s32[]{:S(2)}) async-start(), calls=%async_computation.2 | async-start | bytes 3244032 | tf_op jit(solution)/shard_map/reduce_scatter | solution.py:279
  52.9 30.3 %copy-start.21 = (f32[1,2560]{1,0:T(1,128)}, f32[1,2560]{1,0:T(1,128)S(1)}, u32[]{:S(2)}) copy-start(f32[1,2560]{1,0:T(1,128)S(1)} %reshape.422) | copy-start | bytes 30724
  108.7 12.6 copy-start.12
  139.9 12.7 copy-start.12
  171.0 12.6 copy-start.12
  202.1 12.6 copy-start.12
  218.2 14.6 %copy-start.8 = (bf16[768,256]{1,0:T(8,128)(2,1)}, bf16[768,256]{1,0:T(8,128)(2,1)S(1)}, u32[]{:S(2)}) copy-start(bf16[768,256]{1,0:T(8,128)(2,1)S(1)} %get-tuple-element.1887) | copy-start | bytes 1179652
  218.2 14.6 %copy-start.24 = (f32[256]{0:T(256)}, f32[256]{0:T(256)S(1)}, u32[]{:S(2)}) copy-start(f32[256]{0:T(256)S(1)} %get-tuple-element.1894) | copy-start | bytes 3076
  218.2 14.6 %copy-start.37 = (f32[256]{0:T(256)}, f32[256]{0:T(256)S(1)}, u32[]{:S(2)}) copy-start(f32[256]{0:T(256)S(1)} %get-tuple-element.1900) | copy-start | bytes 3076
  242.8 137.5 %copy-start.32 = (f32[4,1152]{1,0:T(4,128)S(1)}, f32[4,1152]{1,0:T(4,128)}, u32[]{:S(2)}) copy-start(f32[4,1152]{1,0:T(4,128)} %fusion.398) | copy-start | bytes 55300
  405.7 19.0 %copy-start.28 = (f32[256]{0:T(256)}, f32[256]{0:T(256)S(1)}, u32[]{:S(2)}) copy-start(f32[256]{0:T(256)S(1)} %get-tuple-element.1804) | copy-start | bytes 3076 | tf_op jit(solution)/shard_map/while
  407.9 16.8 %copy-start.13 = (f32[1152]{0:T(1024)}, f32[1152]{0:T(1024)S(1)}, u32[]{:S(2)}) copy-start(f32[1152]{0:T(1024)S(1)} %fusion.602) | copy-start | bytes 13828 | tf_op jit(solution)/shard_map/while
  481.6 5.5 copy-start.14
  481.6 5.5 copy-start.39
  481.6 5.5 copy-start.47
  489.1 12.8 copy-start.2
  504.5 19.0 %copy-start.28 = (f32[256]{0:T(256)}, f32[256]{0:T(256)S(1)}, u32[]{:S(2)}) copy-start(f32[256]{0:T(256)S(1)} %get-tuple-element.1804) | copy-start | bytes 3076 | tf_op jit(solution)/shard_map/while
  506.7 16.8 %copy-start.13 = (f32[1152]{0:T(1024)}, f32[1152]{0:T(1024)S(1)}, u32[]{:S(2)}) copy-start(f32[1152]{0:T(1024)S(1)} %fusion.602) | copy-start | bytes 13828 | tf_op jit(solution)/shard_map/while
  580.4 5.5 copy-start.14
  580.4 5.5 copy-start.39
  580.4 5.5 copy-start.47
  587.9 12.8 copy-start.2
  603.2 19.0 %copy-start.28 = (f32[256]{0:T(256)}, f32[256]{0:T(256)S(1)}, u32[]{:S(2)}) copy-start(f32[256]{0:T(256)S(1)} %get-tuple-element.1804) | copy-start | bytes 3076 | tf_op jit(solution)/shard_map/while
  605.4 16.8 %copy-start.13 = (f32[1152]{0:T(1024)}, f32[1152]{0:T(1024)S(1)}, u32[]{:S(2)}) copy-start(f32[1152]{0:T(1024)S(1)} %fusion.602) | copy-start | bytes 13828 | tf_op jit(solution)/shard_map/while
  679.2 5.5 copy-start.14
  679.2 5.5 copy-start.39
  679.2 5.5 copy-start.47
  686.7 12.8 copy-start.2
  702.1 19.0 %copy-start.28 = (f32[256]{0:T(256)}, f32[256]{0:T(256)S(1)}, u32[]{:S(2)}) copy-start(f32[256]{0:T(256)S(1)} %get-tuple-element.1804) | copy-start | bytes 3076 | tf_op jit(solution)/shard_map/while
  704.3 16.8 %copy-start.13 = (f32[1152]{0:T(1024)}, f32[1152]{0:T(1024)S(1)}, u32[]{:S(2)}) copy-start(f32[1152]{0:T(1024)S(1)} %fusion.602) | copy-start | bytes 13828 | tf_op jit(solution)/shard_map/while
  778.0 5.5 copy-start.14
  778.0 5.5 copy-start.39
  778.0 5.5 copy-start.47
  785.5 12.8 copy-start.2
  868.6 6.3 copy-start.9
  868.6 6.3 copy-start.25
  871.0 6.1 copy-start.11
  877.1 4.8 copy-start.16
  877.1 4.8 copy-start.26
  877.1 4.8 copy-start.38
  888.3 12.8 copy-start
  953.6 6.3 copy-start.9
  953.6 6.3 copy-start.25
  956.0 6.1 copy-start.11
  962.0 4.8 copy-start.16
  962.0 4.8 copy-start.26
  962.1 4.8 copy-start.38
  973.3 12.8 copy-start
  1038.5 6.3 copy-start.9
  1038.5 6.3 copy-start.25
  1040.9 6.1 copy-start.11
  1047.0 4.8 copy-start.26
  1047.0 4.8 copy-start.38
  1058.3 12.8 copy-start
  1123.5 6.3 copy-start.9
  1123.5 6.3 copy-start.25
  1125.9 6.1 copy-start.11
  1132.0 4.8 copy-start.16
  1132.0 4.8 copy-start.26
  1132.0 4.8 copy-start.38
  1143.3 12.8 copy-start
  1158.6 206.2 %reduce-scatter.5.cloned.1.call-start = ((), (), s32[]{:S(2)}) async-start(), calls=%async_computation.3 | async-start | bytes 3244032 | tf_op jit(solution)/shard_map/reduce_scatter | solution.py:279
  (109 other events, 385.7 us)
Sparse Core Ops, SparseCore 0:
  11.5 57.8 all-gather.6
  72.2 53.8 all-gather.8
  1158.8 100.2 reduce-scatter.2
  1264.4 100.4 reduce-scatter.4
where the time goes:
time: 1390 us; the launch traced here: 1370 us
  matrix products  626 us (45%)
  local copies, waits for them, and re-layouts  271 us (19%)
  waiting for transfers between devices  181 us (13%)
  other arithmetic  163 us (12%)
  blocking collectives  81.3 us (6%)
  loops' own time  36.2 us (3%)
  between operations  14.1 us (1%)
    dot_general x96, matrix products, product(): lax.dot_general(left, right, (((left_dim,), (right_dim,)), ((), ())), pre...  485 us
    reduce_scatter x2, waiting for transfers between devices, body(): lax.psum_scatter(grad_matrix, ('dp', 'sub'), scatter_dimension=0, tiled=T...  166 us
    unnamed x2, blocking collectives  81.3 us
    reshape x56, local copies, waits for them, and re-layouts, regroup(): input_tensor.reshape(IMAGE_ROWS, ROW_LENGTH, HEAD_COUNT, input_tensor.sha...  55.6 us
    while x376, local copies, waits for them, and re-layouts  46.5 us
    reduce_sum x24, other arithmetic, normalize(): average = jnp.mean(source, -1, keepdims=True)  46.2 us
    another operation x12, local copies, waits for them, and re-layouts  42.7 us
    dot_general x8, matrix products, attend_backward(): jnp.einsum('ghlm,gmhd->glhd', grad_raw, key_rows, preferred_element_type=...  35.7 us
  transfers between devices with their start and end apart: 4, of which 3 were waited for; matrix products, arithmetic and copies ran while one was open for 11% of the time, Pallas kernels for 0%

commit v1 on v0

v1 whole, which is shorter than its diff:
```python
from functools import partial

import jax
import jax.numpy as jnp
from jax import lax
from jax.experimental import pallas as pl
from jax.experimental.pallas import tpu as pltpu
from jax.sharding import PartitionSpec as P

HEADS = 2
COLS = 96
ROWS = 12
SUBL = 8
BLOCK = 96
NBLK = 12
S = COLS * ROWS
LOG2E = 1.4426950408889634
BF = jnp.bfloat16
F32 = jnp.float32


def mm(a, b, ca, cb):
    return lax.dot_general(a, b, (((ca,), (cb,)), ((), ())), preferred_element_type=F32)


def standardize(v):
    c = v - jnp.mean(v, -1, keepdims=True)
    r = lax.rsqrt(jnp.mean(c * c, -1, keepdims=True) + 1e-05)
    return c * r, r


def rowsum8(v):
    return jnp.sum(v.reshape(v.shape[0] // 8, 8, v.shape[1]), axis=0)


def live_mask(length, slab, width):
    row = lax.broadcasted_iota(jnp.int32, (ROWS, SUBL, width), 0)
    col = lax.broadcasted_iota(jnp.int32, (ROWS, SUBL, width), 1)
    return row * COLS + col + slab * SUBL < length


def kernel(
    dims, len_ref, x_ref, cot_ref, w_ref, v_ref,
    out_ref, gin_ref, gwt_ref, gv_ref,
    n1_s, pk_s, pt_s, mix_s, mid_s, n2_s, act_s, dact_s,
    x1_s, gy0_s, gy_s, gup_s, gmid_s, gmidl_s, gmix_s, gpk_s,
):
    d, ff = dims
    hw = d // HEADS
    img = pl.program_id(0)
    length = len_ref[img]
    qs = hw ** -0.5

    @pl.when(img == 0)
    def _():
        gwt_ref[...] = jnp.zeros_like(gwt_ref)
        gv_ref[...] = jnp.zeros_like(gv_ref)

    def wqkv(l):
        return w_ref[l, 0 : 3 * d, :]

    def wout(l):
        return w_ref[l, 3 * d : 4 * d, :]

    def vec(l, i, n=1):
        return v_ref[l, 0:1, i * d : (i + n) * d]

    tril_b = lax.broadcasted_iota(jnp.int32, (BLOCK, BLOCK), 0)
    tril_a = lax.broadcasted_iota(jnp.int32, (BLOCK, BLOCK), 1)
    masks = (
        tril_b <= tril_a,
        (tril_b <= tril_a) & ((tril_b & (SUBL - 1)) == (tril_a & (SUBL - 1))),
    )

    def load_x(l, c, nb):
        if l == 0:
            return x_ref[0, pl.ds(c * nb, nb)].reshape(nb * BLOCK, d)
        return x1_s[pl.ds(c * nb, nb)].reshape(nb * BLOCK, d)

    def store_perm(ref, c, nb, val, lead=()):
        v4 = val.reshape(nb, NBLK, SUBL, d)
        for b in range(nb):
            ref[lead + (slice(None), c * nb + b)] = v4[b]

    def rows(c, nb):
        return pl.ds(pl.multiple_of(c * nb * BLOCK, BLOCK), nb * BLOCK)

    def qkv_fwd(l, nb):
        def step(c, _):
            s = rows(c, nb)
            xh, _r = standardize(load_x(l, c, nb))
            n1 = (xh * vec(l, 0) + vec(l, 1)).astype(BF)
            n1_s[l, s, :] = n1
            pk_s[l, s, :] = mm(n1, wqkv(l), 1, 1).astype(BF)
            return 0

        lax.fori_loop(0, NBLK // nb, step, 0)

    def attn_fwd(l, nb):
        mask = masks[l]

        def step(c, _):
            for b in range(nb):
                s = pl.ds(pl.multiple_of((c * nb + b) * BLOCK, BLOCK), BLOCK)
                pk = pk_s[l, s, :]
                for h in range(HEADS):
                    q = pk[:, h * hw : (h + 1) * hw]
                    k = pk[:, d + h * hw : d + (h + 1) * hw]
                    v = pk[:, 2 * d + h * hw : 2 * d + (h + 1) * hw]
                    st = jnp.where(mask, mm(k, q, 1, 1), -1e30)
                    m = jnp.max(st, 0, keepdims=True)
                    p = jnp.exp2((st - m) * (qs * LOG2E))
                    p = p * (1.0 / jnp.sum(p, 0, keepdims=True))
                    p = p.astype(BF)
                    pt_s[l, c * nb + b, h, :, 0:BLOCK] = p
                    mix_s[l, s, h * hw : (h + 1) * hw] = mm(p, v, 0, 0).astype(BF)
            return 0

        lax.fori_loop(0, NBLK // nb, step, 0)

    def ffn_fwd(l, nb):
        def step(c, _):
            s = rows(c, nb)
            mid = load_x(l, c, nb) + mm(mix_s[l, s, :], wout(l), 1, 1) + vec(l, 2)
            mid_s[l, s, :] = mid
            xh, _r = standardize(mid)
            n2 = (xh * vec(l, 3) + vec(l, 4)).astype(BF)
            n2_s[l, s, :] = n2
            y = mid + vec(l, 5)
            for f in range(ff // d):
                h = mm(n2, w_ref[l, (4 + f) * d : (5 + f) * d, :], 1, 1) + vec(l, 6 + f)
                phi = lax.erf(h * (2 ** -0.5)) * 0.5 + 0.5
                e = jnp.exp2(h * h * (-0.5 * LOG2E)) * 0.3989422804014327
                act = (h * phi).astype(BF)
                act_s[l, s, f * d : (f + 1) * d] = act
                dact_s[l, s, f * d : (f + 1) * d] = (phi + h * e).astype(BF)
                y = y + mm(act, w_ref[l, 4 * d + ff + f * d : 4 * d + ff + (f + 1) * d, :], 1, 0)
            if l == 0:
                store_perm(x1_s, c, nb, y)
            else:
                y4 = y.reshape(nb, NBLK, SUBL, d)
                for b in range(nb):
                    live = live_mask(length, c * nb + b, d)
                    out_ref[0, :, c * nb + b] = jnp.where(live, y4[b], 0.0)
            return 0

        lax.fori_loop(0, NBLK // nb, step, 0)

    def acc_vec(l, i, val, n=1):
        gv_ref[l, :, i * d : (i + n) * d] += rowsum8(val)

    def norm_back(l, gi, v, gn):
        xh, r = standardize(v)
        acc_vec(l, gi, gn * xh)
        acc_vec(l, gi + 1, gn)
        e = gn * vec(l, gi)
        me = jnp.mean(e, -1, keepdims=True)
        mx = jnp.mean(e * xh, -1, keepdims=True)
        return r * (e - me - xh * mx)

    def ffn_bwd(l, nb):
        def step(c, _):
            s = rows(c, nb)
            if l == 0:
                gy = gy0_s[pl.ds(c * nb, nb)].reshape(nb * BLOCK, d)
            else:
                parts = []
                for b in range(nb):
                    live = live_mask(length, c * nb + b, d)
                    part = jnp.where(live, cot_ref[0, :, c * nb + b], 0.0)
                    parts.append(part.reshape(BLOCK, d))
                gy = jnp.concatenate(parts, 0) if nb > 1 else parts[0]
            acc_vec(l, 5, gy)
            gyl = gy.astype(BF)
            gy_s[s, :] = gyl
            gn2 = jnp.zeros((nb * BLOCK, d), F32)
            for f in range(ff // d):
                wd = w_ref[l, 4 * d + ff + f * d : 4 * d + ff + (f + 1) * d, :]
                gup = mm(gyl, wd, 1, 1) * dact_s[l, s, f * d : (f + 1) * d].astype(F32)
                acc_vec(l, 6 + f, gup)
                gupl = gup.astype(BF)
                gup_s[s, f * d : (f + 1) * d] = gupl
                gn2 = gn2 + mm(gupl, w_ref[l, (4 + f) * d : (5 + f) * d, :], 1, 0)
            gmid = gy + norm_back(l, 3, mid_s[l, s, :], gn2)
            gmid_s[s, :] = gmid
            acc_vec(l, 2, gmid)
            gml = gmid.astype(BF)
            gmidl_s[s, :] = gml
            gmix_s[s, :] = mm(gml, wout(l), 1, 0).astype(BF)
            return 0

        lax.fori_loop(0, NBLK // nb, step, 0)

    def attn_bwd(l, nb):
        def step(c, _):
            for b in range(nb):
                s = pl.ds(pl.multiple_of((c * nb + b) * BLOCK, BLOCK), BLOCK)
                pk = pk_s[l, s, :]
                gm2 = gmix_s[s, :]
                for h in range(HEADS):
                    q = pk[:, h * hw : (h + 1) * hw]
                    k = pk[:, d + h * hw : d + (h + 1) * hw]
                    v = pk[:, 2 * d + h * hw : 2 * d + (h + 1) * hw]
                    gm = gm2[:, h * hw : (h + 1) * hw]
                    pt = pt_s[l, c * nb + b, h, :, 0:BLOCK]
                    pf = pt.astype(F32)
                    gp = mm(v, gm, 1, 1)
                    pg = pf * gp
                    gs = (pg - pf * jnp.sum(pg, 0, keepdims=True)) * qs
                    gs = gs.astype(BF)
                    gpk_s[s, h * hw : (h + 1) * hw] = mm(gs, k, 0, 0).astype(BF)
                    gpk_s[s, d + h * hw : d + (h + 1) * hw] = mm(gs, q, 1, 0).astype(BF)
                    gpk_s[s, 2 * d + h * hw : 2 * d + (h + 1) * hw] = mm(pt, gm, 1, 0).astype(BF)
            return 0

        lax.fori_loop(0, NBLK // nb, step, 0)

    def qkv_bwd(l, nb):
        def step(c, _):
            s = rows(c, nb)
            gn1 = mm(gpk_s[s, :], wqkv(l), 1, 0)
            gx = gmid_s[s, :] + norm_back(l, 0, load_x(l, c, nb), gn1)
            if l == 0:
                gin_ref[0, pl.ds(c * nb, nb)] = gx.reshape(nb, NBLK, SUBL, d)
            else:
                store_perm(gy0_s, c, nb, gx)
            return 0

        lax.fori_loop(0, NBLK // nb, step, 0)

    def wgrads(l):
        gwt_ref[l, :, 0 : 3 * d] += mm(n1_s[l], gpk_s[...], 0, 0)
        gwt_ref[l, :, 3 * d : 4 * d] += mm(mix_s[l], gmidl_s[...], 0, 0)
        gwt_ref[l, :, 4 * d : 4 * d + ff] += mm(n2_s[l], gup_s[...], 0, 0)
        gwt_ref[l, :, 4 * d + ff :] += mm(gy_s[...], act_s[l], 0, 0)

    for l in range(2):
        qkv_fwd(l, 4)
        attn_fwd(l, 2)
        ffn_fwd(l, 4)
    for l in (1, 0):
        ffn_bwd(l, 4)
        attn_bwd(l, 2)
        qkv_bwd(l, 4)
        wgrads(l)


def compute(x, cot, w, v, lengths, d, ff):
    n = lengths.shape[0]
    mrows = w.shape[1]
    img = pl.BlockSpec((1, ROWS, NBLK, SUBL, d), lambda i: (i, 0, 0, 0, 0))
    def const(shape):
        return pl.BlockSpec(shape, lambda i: (0,) * len(shape), pipeline_mode=pl.Buffered(1))
    shp = (n, ROWS, NBLK, SUBL, d)
    return pl.pallas_call(
        partial(kernel, (d, ff)),
        grid=(n,),
        in_specs=[
            pl.BlockSpec(memory_space=pltpu.SMEM),
            img,
            img,
            const(w.shape),
            const(v.shape),
        ],
        out_specs=[img, img, const((2, d, mrows)), const((2, 8, v.shape[2]))],
        out_shape=[
            jax.ShapeDtypeStruct(shp, F32),
            jax.ShapeDtypeStruct(shp, F32),
            jax.ShapeDtypeStruct((2, d, mrows), F32),
            jax.ShapeDtypeStruct((2, 8, v.shape[2]), F32),
        ],
        scratch_shapes=[
            pltpu.VMEM((2, S, d), BF),
            pltpu.VMEM((2, S, 3 * d), BF),
            pltpu.VMEM((2, NBLK, HEADS, BLOCK, 128), BF),
            pltpu.VMEM((2, S, d), BF),
            pltpu.VMEM((2, S, d), F32),
            pltpu.VMEM((2, S, d), BF),
            pltpu.VMEM((2, S, ff), BF),
            pltpu.VMEM((2, S, ff), BF),
            pltpu.VMEM((NBLK, ROWS, SUBL, d), F32),
            pltpu.VMEM((ROWS, NBLK, SUBL, d), F32),
            pltpu.VMEM((S, d), BF),
            pltpu.VMEM((S, ff), BF),
            pltpu.VMEM((S, d), F32),
            pltpu.VMEM((S, d), BF),
            pltpu.VMEM((S, d), BF),
            pltpu.VMEM((S, 3 * d), BF),
        ],
        compiler_params=pltpu.CompilerParams(
            dimension_semantics=("arbitrary",), vmem_limit_bytes=63 << 20
        ),
        cost_estimate=pl.CostEstimate(flops=46 * 10**9, bytes_accessed=30 * 10**6, transcendentals=0),
        name="layers",
    )(lengths, x.reshape(shp), cot.reshape(shp), w, v)


def body(inputs, matrices, vectors, lengths, cotangent):
    d = inputs.shape[1]
    w = lax.all_gather(matrices, ("dp", "sub"), axis=1, tiled=True)
    v = lax.all_gather(vectors, ("dp", "sub"), axis=1, tiled=True).astype(F32)
    ff = (w.shape[1] - 4 * d) // 2
    out, gin, gwt, gv = compute(inputs, cotangent, w, v[:, None, :], lengths, d, ff)
    gw = jnp.swapaxes(gwt, 1, 2)
    gw = lax.psum_scatter(gw, ("dp", "sub"), scatter_dimension=1, tiled=True)
    gv = lax.psum_scatter(jnp.sum(gv, 1), ("dp", "sub"), scatter_dimension=1, tiled=True)
    return (out.reshape(inputs.shape), gin.reshape(inputs.shape), gw, gv)


def solution(mesh):
    split = ("dp", "sub")
    return jax.shard_map(
        body,
        mesh=mesh,
        in_specs=(P(split, None), P(None, split, None), P(None, split), P(split), P(split, None)),
        out_specs=(P(split, None), P(split, None), P(None, split, None), P(None, split)),
        check_vma=False,
    )
```

time: 1390 us -> 590 us (0.42); the launches traced: 1370 us -> 590 us
  matrix products: 626 us -> 0 us
  local copies, waits for them, and re-layouts: 271 us -> 15.6 us
  Pallas kernels: 0 us -> 209 us
  other arithmetic: 163 us -> 0.98 us
  waiting for transfers between devices: 181 us -> 281 us
  loops' own time: 36.2 us -> 0 us
    dot_general x152 -> x0, matrix products: 626 us -> none  [the longest x96 485 us: product(): lax.dot_general(left, right, (((left_dim,), (right_dim,)), ((), ())), pre...]
    unnamed x4 -> x5, waiting for transfers between devices: 1.25 us -> 281 us
    pallas_call x0 -> x1, Pallas kernels: none -> 209 us  [compute(): pl.pallas_call(partial(kernel, (d, ff)), grid=(n,), in_specs=[pl.BlockSpe...]
    reduce_scatter x2 -> x0, waiting for transfers between devices: 166 us -> none  [body(): lax.psum_scatter(grad_matrix, ('dp', 'sub'), scatter_dimension=0, tiled=T...]
    reduce_sum x88 -> x1, other arithmetic: 109 us -> 0.97 us  [body(): jnp.sum(gv, 1)]
    unnamed x2 -> x0, blocking collectives: 81.3 us -> none
    all_gather x0 -> x1, blocking collectives: none -> 69.6 us  [body(): v = lax.all_gather(vectors, ('dp', 'sub'), axis=1, tiled=True).astype(F32)]
    reshape x56 -> x0, local copies, waits for them, and re-layouts: 55.6 us -> none  [regroup(): input_tensor.reshape(IMAGE_ROWS, ROW_LENGTH, HEAD_COUNT, input_tensor.sha...]
  transfers between devices with their start and end apart: 4 -> 3, of which waited for: 3 -> 2; matrix products, arithmetic and copies ran while one was open for 11% -> 2% of each run, Pallas kernels for 0% -> 0%
where the time goes in v1:
time: 590 us
  waiting for transfers between devices  281 us (48%)
  Pallas kernels  209 us (35%)
  blocking collectives  69.6 us (12%)
  local copies, waits for them, and re-layouts  15.6 us (3%)
  between operations  13.8 us (2%)
    unnamed x5, waiting for transfers between devices  281 us
    pallas_call x1, Pallas kernels, compute(): pl.pallas_call(partial(kernel, (d, ff)), grid=(n,), in_specs=[pl.BlockSpe...  209 us
    all_gather x1, blocking collectives, body(): v = lax.all_gather(vectors, ('dp', 'sub'), axis=1, tiled=True).astype(F32)  69.6 us
  transfers between devices with their start and end apart: 3, of which 2 were waited for; matrix products, arithmetic and copies ran while one was open for 2% of the time, Pallas kernels for 0%

profile of v1, /device:TPU:0, one launch (start us, length us, event | category | flops | bytes accessed | tf_op | source)
XLA Modules:
  0.0 590.0 jit_solution(8764615730305686844)
XLA Ops:
  7.2 0.0 all-gather.3.cloned.1.call-start
  7.2 0.7 all-gather.3.cloned.1.call-update
  7.9 0.0 reduce-scatter.4.cloned.1.call-start
  7.9 69.6 %all-gather = bf16[32,80,2]{1,2,0:T(2,128)(2,1)S(1)} all-gather(bf16[1,80,2]{1,2,0:T(2,128)(2,1)} %bitcast.17), channel_id=1, replica_groups=mesh['dp'=8,'sub'=4] {'dp','sub'}, dimensions={0}, use_global_device_ids=true | all-gather | bytes 10560 | tf_op jit(solution)/shard_map/all_gather | solution.py:301
  77.5 0.1 reshape.27
  77.6 0.6 reshape.24.v_ref
  78.3 0.0 all-gather.3.cloned.1.call-done.w_ref
  78.3 208.9 %layers.1 = (f32[4,12,12,8,256]{4,3,2,1,0:T(8,128)}, f32[4,12,12,8,256]{4,3,2,1,0:T(8,128)}, f32[2,256,3072]{2,1,0:T(8,128)}, f32[2,8,2560]{2,1,0:T(8,128)}) custom-call(s32[4]{0:T(128)} %len_ref.1, f32[4,12,12,8,256]{4,3,2,1,0:T(8,128)} %bitcast.18, f32[4,12,12,8,256]{4,3,2,1,0:T(8,128)} %bitcast.19, ...), custom_call_target="tpu_custom_call" | custom-call | flops 46000001024 | bytes 30000000 | tf_op jit(solution)/shard_map/layers/pallas_call | solution.py:255
  287.2 1.0 reduce_sum.9
  288.1 1.6 copy.17
  289.7 0.0 reduce-scatter.4.cloned.1.call-update
  289.7 0.0 all-reduce.3.cloned.1.call-start
  289.8 10.2 %copy.15 = f32[2,3072,256]{2,0,1:T(2,128)} copy(f32[2,3072,256]{1,2,0:T(8,128)} %bitcast.13) | data formatting | bytes 12582912 | tf_op jit(solution)/shard_map/transpose | solution.py:304
  300.0 0.0 all-reduce.3.cloned.1.call-update
  300.1 122.5 %reduce-scatter.4.cloned.1.call-done = f32[80,2]{1,0:T(8,128)} async-done(((f32[2560,2]{1,0:T(8,128)}), f32[80,2]{1,0:T(8,128)}) %reduce-scatter.4.cloned.1.call-update) | async-done | bytes 656
  422.6 1.4 copy.18
  424.0 157.9 %all-reduce.3.cloned.1.call-done = f32[2,3072,256]{2,0,1:T(2,128)} async-done(((f32[2,3072,256]{2,0,1:T(2,128)}), f32[2,3072,256]{2,0,1:T(2,128)}) %all-reduce.3.cloned.1.call-update) | async-done | bytes 6291472
  581.9 0.9 constant_dynamic-slice_fusion
  582.8 0.7 copy.16
  (1 shorter events, 0.0 us)
Async XLA Ops:
  7.2 71.1 %all-gather.3.cloned.1.call-start = ((), (), s32[]{:S(2)}) async-start(), calls=%async_computation.1 | async-start | bytes 3244032 | tf_op jit(solution)/shard_map/all_gather | solution.py:300
  7.9 414.7 %reduce-scatter.4.cloned.1.call-start = ((), (), s32[]{:S(2)}) async-start(), calls=%async_computation.2 | async-start | bytes 1351680
  289.7 292.1 %all-reduce.3.cloned.1.call-start = ((), (), s32[]{:S(2)}) async-start(), calls=%async_computation.3 | async-start | bytes 12582912
Sparse Core Ops, SparseCore 0:
  10.9 61.7 all-gather.2
  289.9 132.6 reduce-scatter.3
  429.2 152.6 all-reduce.2

commit v2 on v1

--- a/solution.py
+++ b/solution.py
@@ -40,12 +40,16 @@
 
 
 def kernel(
-    dims, len_ref, x_ref, cot_ref, w_ref, v_ref,
-    out_ref, gin_ref, gwt_ref, gv_ref,
+    dims, len_ref, x_ref, cot_ref, full_ref,
+    out_ref, gin_ref, gb_ref,
+    w_ref, v_ref, gwt_ref, gv_ref,
     n1_s, pk_s, pt_s, mix_s, mid_s, n2_s, act_s, dact_s,
     x1_s, gy0_s, gy_s, gup_s, gmid_s, gmidl_s, gmix_s, gpk_s,
 ):
     d, ff = dims
+    devices, block, _d = full_ref.shape
+    rows_dev, vlen = w_ref.shape[1] // devices, v_ref.shape[2]
+    vrow = vlen // devices
     hw = d // HEADS
     img = pl.program_id(0)
     length = len_ref[img]
@@ -55,6 +59,20 @@
     def _():
         gwt_ref[...] = jnp.zeros_like(gwt_ref)
         gv_ref[...] = jnp.zeros_like(gv_ref)
+        v_ref[...] = jnp.zeros_like(v_ref)
+        for i in range(devices):
+            for l in range(2):
+                w_ref[l, i * rows_dev : (i + 1) * rows_dev] = full_ref[
+                    i, l * rows_dev : (l + 1) * rows_dev
+                ]
+            part = full_ref[i, 2 * rows_dev : block, 0:128].astype(F32)[0:8]
+            at = i * vrow // 128 * 128
+            wide = jnp.concatenate([part, jnp.zeros_like(part)], 1)
+            if i * vrow > at:
+                wide = pltpu.roll(wide, i * vrow - at, 1)
+            n = min(256, vlen - at)
+            for l in range(2):
+                v_ref[l, 0:1, at : at + n] += wide[l : l + 1, 0:n]
 
     def wqkv(l):
         return w_ref[l, 0 : 3 * d, :]
@@ -244,32 +262,451 @@
         qkv_bwd(l, 4)
         wgrads(l)
 
-
-def compute(x, cot, w, v, lengths, d, ff):
+    @pl.when(img == pl.num_programs(0) - 1)
+    def _():
+        zeros = jnp.zeros((block - 2 * rows_dev, d), F32)
+        for l in range(2):
+            g = gwt_ref[l].T.astype(BF)
+            for i in range(devices):
+                gb_ref[i, l * rows_dev : (l + 1) * rows_dev] = g[i * rows_dev : (i + 1) * rows_dev]
+        gv = jnp.concatenate([jnp.sum(gv_ref[l], 0, keepdims=True) for l in range(2)], 0)
+        gv = jnp.concatenate([gv, jnp.zeros((6, vlen), F32)], 0)
+        for i in range(devices):
+            at = i * vrow // 128 * 128
+            n = min(256, vlen - at)
+            wide = gv[:, at : at + n]
+            if n < 256:
+                wide = jnp.concatenate([wide, jnp.zeros_like(wide)], 1)
+            if i * vrow > at:
+                wide = pltpu.roll(wide, 256 - (i * vrow - at), 1)
+            wide = jnp.concatenate([wide, jnp.zeros_like(wide)], 0)
+            gb_ref[i, 2 * rows_dev : block] = wide.astype(BF)
+
+
+MESH = pl.DeviceIdType.MESH
+
+
+def place(z_count):
+    dp, z = lax.axis_index("dp"), lax.axis_index("sub")
+    core = dp % 2
+    x = (dp // 2) % 2
+    y = dp // 4
+    return y, x, core, z
+
+
+def column(y, x, core):
+    return (y * 2 + x) * 2 + core
+
+
+def greet(z, z_count, partners):
+    barrier = pltpu.get_barrier_semaphore()
+    dp = lax.axis_index("dp")
+    for p in partners:
+        pl.semaphore_signal(barrier, inc=1, device_id=(p, z), device_id_type=MESH)
+
+    @pl.when(z > 0)
+    def _():
+        pl.semaphore_signal(barrier, inc=1, device_id=(dp, z - 1), device_id_type=MESH)
+
+    @pl.when(z < z_count - 1)
+    def _():
+        pl.semaphore_signal(barrier, inc=1, device_id=(dp, z + 1), device_id_type=MESH)
+
+    ends = jnp.where(z > 0, 1, 0) + jnp.where(z < z_count - 1, 1, 0)
+    pl.semaphore_wait(barrier, len(partners) + ends)
+
+
+def gather_kernel(z_count, w_ref, v_ref, full_ref, link_sem, core_sem, send_sem):
+    y, x, core, z = place(z_count)
+    dp = lax.axis_index("dp")
+    rows = w_ref.shape[1]
+    block = full_ref.shape[1]
+    half = (block // 2 + 15) // 16 * 16
+    cut = (pl.ds(0, half), pl.ds(half, block - half))
+    dp_x, dp_y, dp_c = column(y, 1 - x, core), column(1 - y, x, core), column(y, x, 1 - core)
+    me = dp * z_count + z
+
+    greet(z, z_count, (dp_x, dp_y, dp_c))
+    full_ref[me, 0:rows] = w_ref[0]
+    full_ref[me, rows : 2 * rows] = w_ref[1]
+    pad = jnp.zeros((block - 2 * rows, full_ref.shape[2]), full_ref.dtype)
+    full_ref[me, 2 * rows : block] = pad
+    full_ref[me, 2 * rows : 2 * rows + 2, 0 : v_ref.shape[1]] = v_ref[...]
+
+    def copy(i, h, slot, target, sem):
+        ref = full_ref.at[i, cut[h], :]
+        return pltpu.make_async_remote_copy(
+            src_ref=ref, dst_ref=ref, send_sem=send_sem.at[i, h, slot], recv_sem=sem.at[i, h],
+            device_id=target, device_id_type=MESH,
+        )
+
+    def to_right(i, h):
+        return copy(i, h, 0, (dp, z + 1), link_sem)
+
+    def to_left(i, h):
+        return copy(i, h, 1, (dp, z - 1), link_sem)
+
+    def to_x(i, h):
+        return copy(i, h, 2, (dp_x, z), link_sem)
+
+    def to_y(i, h):
+        return copy(i, h, 3, (dp_y, z), link_sem)
+
+    def to_core(i, h):
+        return copy(i, h, 4, (dp_c, z), core_sem)
+
+    def spread_column(i):
+        to_x(i, 0).start()
+        to_y(i, 1).start()
+        to_core(i, 0).start()
+        to_core(i, 1).start()
+        to_x(i, 1).start()
+        to_y(i, 0).start()
+
+    def wait_link(i, h):
+        pltpu.make_async_remote_copy(
+            src_ref=full_ref.at[i, cut[h], :], dst_ref=full_ref.at[i, cut[h], :],
+            send_sem=send_sem.at[i, h, 4], recv_sem=link_sem.at[i, h],
+            device_id=(dp_c, z), device_id_type=MESH,
+        ).wait_recv()
+
+    @pl.when(z < z_count - 1)
+    def _():
+        for h in range(2):
+            to_right(me, h).start()
+
+    @pl.when(z > 0)
+    def _():
+        for h in range(2):
+            to_left(me, h).start()
+
+    spread_column(me)
+    for k in range(1, z_count):
+
+        @pl.when(z - k >= 0)
+        def _():
+            i = me - k
+            for h in range(2):
+                wait_link(i, h)
+
+            @pl.when(z < z_count - 1)
+            def _():
+                for h in range(2):
+                    to_right(i, h).start()
+
+            spread_column(i)
+
+        @pl.when(z + k < z_count)
+        def _():
+            i = me + k
+            for h in range(2):
+                wait_link(i, h)
+
+            @pl.when(z > 0)
+            def _():
+                for h in range(2):
+                    to_left(i, h).start()
+
+            spread_column(i)
+
+    order = []
+    for k in range(z_count):
+        order.append(lax.rem(z + k, z_count))
+    for zz in order:
+        i = dp_x * z_count + zz
+        wait_link(i, 0)
+        to_y(i, 0).start()
+        to_core(i, 0).start()
+        i = dp_y * z_count + zz
+        wait_link(i, 1)
+        to_x(i, 1).start()
+        to_core(i, 1).start()
+    for zz in order:
+        i = dp_x * z_count + zz
+        wait_link(i, 1)
+        to_core(i, 1).start()
+        i = dp_y * z_count + zz
+        wait_link(i, 0)
+        to_core(i, 0).start()
+    dp_d = column(1 - y, 1 - x, core)
+    for zz in order:
+        i = dp_d * z_count + zz
+        for h in range(2):
+            wait_link(i, h)
+            to_core(i, h).start()
+    for yy in range(2):
+        for xx in range(2):
+            for zz in range(z_count):
+                i = column(yy, xx, 1 - core) * z_count + zz
+                for h in range(2):
+                    to_core(i, h).wait_recv()
+    for yy in range(2):
+        for xx in range(2):
+            for zz in range(z_count):
+                i = column(yy, xx, core) * z_count + zz
+                for h in range(2):
+                    to_core(i, h).wait_send()
+    for zz in range(z_count):
+        i = dp * z_count + zz
+        for h in range(2):
+            to_x(i, h).wait_send()
+            to_y(i, h).wait_send()
+
+        @pl.when((zz <= z) & (z < z_count - 1))
+        def _():
+            for h in range(2):
+                to_right(i, h).wait_send()
+
+        @pl.when((zz >= z) & (z > 0))
+        def _():
+            for h in range(2):
+                to_left(i, h).wait_send()
+
+        to_y(dp_x * z_count + zz, 0).wait_send()
+        to_x(dp_y * z_count + zz, 1).wait_send()
+
+
+def scatter_kernel(
+    z_count, g_ref, gw_ref, gv_ref,
+    sib_s, acc_s, own_s, xa_s, yb_s, oya_s, oxb_s, oxa_s, oyb_s, zl_s, zr_s,
+    sib_send, sib_recv, xy_send, xy_recv, z_send, z_recv,
+):
+    y, x, core, z = place(z_count)
+    dp = lax.axis_index("dp")
+    block, width = g_ref.shape[1], g_ref.shape[2]
+    half = xa_s.shape[1]
+    top, low = pl.ds(0, half), pl.ds(half, block - half)
+    dp_x, dp_y, dp_c = column(y, 1 - x, core), column(1 - y, x, core), column(y, x, 1 - core)
+    kinds = ((y, x), (y, 1 - x), (1 - y, x), (1 - y, 1 - x))
+    order = []
+    for k in range((z_count + 1) // 2):
+        order.append(z_count - 1 - k)
+        if k != z_count - 1 - k:
+            order.append(k)
+
+    greet(z, z_count, (dp_x, dp_y, dp_c))
+
+    def to_core(kind):
+        yy, xx = kinds[kind]
+        return pltpu.make_async_remote_copy(
+            src_ref=g_ref.at[pl.ds(column(yy, xx, 1 - core) * z_count, z_count)],
+            dst_ref=sib_s.at[kind],
+            send_sem=sib_send.at[kind], recv_sem=sib_recv.at[kind],
+            device_id=(dp_c, z), device_id_type=MESH,
+        )
+
+    def across(kind, rows, dst, slot, target, t):
+        return pltpu.make_async_remote_copy(
+            src_ref=acc_s.at[kind, t, rows, :], dst_ref=dst.at[t],
+            send_sem=xy_send.at[slot, t], recv_sem=xy_recv.at[slot, t],
+            device_id=(target, z), device_id_type=MESH,
+        )
+
+    def diag_top(t):
+        return across(3, top, xa_s, 0, dp_y, t)
+
+    def diag_low(t):
+        return across(3, low, yb_s, 1, dp_x, t)
+
+    def ycol_top(t):
+        return across(2, top, oya_s, 2, dp_y, t)
+
+    def xcol_low(t):
+        return across(1, low, oxb_s, 3, dp_x, t)
+
+    def xcol_top(t):
+        return across(1, top, oxa_s, 4, dp_x, t)
+
+    def ycol_low(t):
+        return across(2, low, oyb_s, 5, dp_y, t)
+
+    def to_right(t):
+        return pltpu.make_async_remote_copy(
+            src_ref=acc_s.at[0, t], dst_ref=zl_s.at[t],
+            send_sem=z_send.at[0, t], recv_sem=z_recv.at[0, t],
+            device_id=(dp, z + 1), device_id_type=MESH,
+        )
+
+    def to_left(t):
+        return pltpu.make_async_remote_copy(
+            src_ref=acc_s.at[0, t], dst_ref=zr_s.at[t],
+            send_sem=z_send.at[1, t], recv_sem=z_recv.at[1, t],
+            device_id=(dp, z - 1), device_id_type=MESH,
+        )
+
+    def chip_sum(kind, t):
+        yy, xx = kinds[kind]
+        mine = g_ref[column(yy, xx, core) * z_count + t].astype(F32)
+        return mine + sib_s[kind, t].astype(F32)
+
+    for kind in (3, 1, 2, 0):
+        to_core(kind).start()
+    to_core(3).wait_recv()
+    for t in order:
+        acc_s[3, t] = chip_sum(3, t).astype(BF)
+        diag_top(t).start()
+        diag_low(t).start()
+    to_core(1).wait_recv()
+    for t in order:
+        acc_s[1, t] = chip_sum(1, t).astype(BF)
+        xcol_low(t).start()
+    to_core(2).wait_recv()
+    for t in order:
+        acc_s[2, t] = chip_sum(2, t).astype(BF)
+        ycol_top(t).start()
+    to_core(0).wait_recv()
+    for t in order:
+        own_s[t] = chip_sum(0, t)
+    for t in order:
+        diag_top(t).wait_recv()
+        acc_s[1, t, top] = (acc_s[1, t, top].astype(F32) + xa_s[t].astype(F32)).astype(BF)
+        xcol_top(t).start()
+        diag_low(t).wait_recv()
+        acc_s[2, t, low] = (acc_s[2, t, low].astype(F32) + yb_s[t].astype(F32)).astype(BF)
+        ycol_low(t).start()
+    for t in order:
+        xcol_low(t).wait_recv()
+        ycol_top(t).wait_recv()
+        xcol_top(t).wait_recv()
+        ycol_low(t).wait_recv()
+        own_s[t, top] += oya_s[t].astype(F32) + oxa_s[t].astype(F32)
+        own_s[t, low] += oxb_s[t].astype(F32) + oyb_s[t].astype(F32)
+
+        @pl.when(t > z)
+        def _():
+            @pl.when(z > 0)
+            def _():
+                to_right(t).wait_recv()
+                acc_s[0, t] = (own_s[t] + zl_s[t].astype(F32)).astype(BF)
+
+            @pl.when(z == 0)
+            def _():
+                acc_s[0, t] = own_s[t].astype(BF)
+
+            to_right(t).start()
+
+        @pl.when(t < z)
+        def _():
+            @pl.when(z < z_count - 1)
+            def _():
+                to_left(t).wait_recv()
+                acc_s[0, t] = (own_s[t] + zr_s[t].astype(F32)).astype(BF)
+
+            @pl.when(z == z_count - 1)
+            def _():
+                acc_s[0, t] = own_s[t].astype(BF)
+
+            to_left(t).start()
+
+    @pl.when(z > 0)
+    def _():
+        to_right(z).wait_recv()
+        own_s[z] += zl_s[z].astype(F32)
+
+    @pl.when(z < z_count - 1)
+    def _():
+        to_left(z).wait_recv()
+        own_s[z] += zr_s[z].astype(F32)
+
+    rows = gw_ref.shape[1]
+    gw_ref[0] = own_s[z, 0:rows]
+    gw_ref[1] = own_s[z, rows : 2 * rows]
+    gv_ref[...] = own_s[z, 2 * rows : 2 * rows + 2, 0 : gv_ref.shape[1]]
+
+    for kind in range(4):
+        to_core(kind).wait_send()
+    for t in range(z_count):
+        for one in (diag_top, diag_low, ycol_top, xcol_low, xcol_top, ycol_low):
+            one(t).wait_send()
+
+        @pl.when(t > z)
+        def _():
+            to_right(t).wait_send()
+
+        @pl.when(t < z)
+        def _():
+            to_left(t).wait_send()
+
+
+def gather(w, v, z_count, devices):
+    rows, d = w.shape[1], w.shape[2]
+    block = 2 * rows + 16
+    return pl.pallas_call(
+        partial(gather_kernel, z_count),
+        in_specs=[pl.BlockSpec(memory_space=pltpu.VMEM)] * 2,
+        out_specs=pl.BlockSpec(memory_space=pltpu.VMEM),
+        out_shape=jax.ShapeDtypeStruct((devices, block, d), BF),
+        scratch_shapes=[
+            pltpu.SemaphoreType.DMA((devices, 2)),
+            pltpu.SemaphoreType.DMA((devices, 2)),
+            pltpu.SemaphoreType.DMA((devices, 2, 5)),
+        ],
+        compiler_params=pltpu.CompilerParams(
+            collective_id=0, has_side_effects=True, vmem_limit_bytes=32 << 20
+        ),
+        name="gather",
+    )(w, v)
+
+
+def scatter(g, z_count, rows, vrow):
+    devices, block, d = g.shape
+    half = (block // 2 + 15) // 16 * 16
+    low = block - half
+    return pl.pallas_call(
+        partial(scatter_kernel, z_count),
+        in_specs=[pl.BlockSpec(memory_space=pltpu.VMEM)],
+        out_specs=[pl.BlockSpec(memory_space=pltpu.VMEM)] * 2,
+        out_shape=[
+            jax.ShapeDtypeStruct((2, rows, d), F32),
+            jax.ShapeDtypeStruct((2, vrow), F32),
+        ],
+        scratch_shapes=[
+            pltpu.VMEM((4, z_count, block, d), BF),
+            pltpu.VMEM((4, z_count, block, d), BF),
+            pltpu.VMEM((z_count, block, d), F32),
+            pltpu.VMEM((z_count, half, d), BF),
+            pltpu.VMEM((z_count, low, d), BF),
+            pltpu.VMEM((z_count, half, d), BF),
+            pltpu.VMEM((z_count, low, d), BF),
+            pltpu.VMEM((z_count, half, d), BF),
+            pltpu.VMEM((z_count, low, d), BF),
+            pltpu.VMEM((z_count, block, d), BF),
+            pltpu.VMEM((z_count, block, d), BF),
+            pltpu.SemaphoreType.DMA((4,)),
+            pltpu.SemaphoreType.DMA((4,)),
+            pltpu.SemaphoreType.DMA((6, z_count)),
+            pltpu.SemaphoreType.DMA((6, z_count)),
+            pltpu.SemaphoreType.DMA((2, z_count)),
+            pltpu.SemaphoreType.DMA((2, z_count)),
+        ],
+        compiler_params=pltpu.CompilerParams(
+            collective_id=1, has_side_effects=True, vmem_limit_bytes=48 << 20
+        ),
+        name="scatter",
+    )(g)
+
+
+def compute(x, cot, full, lengths, d, ff, vlen):
     n = lengths.shape[0]
-    mrows = w.shape[1]
+    mrows = 4 * d + 2 * ff
     img = pl.BlockSpec((1, ROWS, NBLK, SUBL, d), lambda i: (i, 0, 0, 0, 0))
-    def const(shape):
-        return pl.BlockSpec(shape, lambda i: (0,) * len(shape), pipeline_mode=pl.Buffered(1))
+    whole = pl.BlockSpec(full.shape, lambda i: (0, 0, 0), pipeline_mode=pl.Buffered(1))
     shp = (n, ROWS, NBLK, SUBL, d)
     return pl.pallas_call(
         partial(kernel, (d, ff)),
         grid=(n,),
-        in_specs=[
-            pl.BlockSpec(memory_space=pltpu.SMEM),
-            img,
-            img,
-            const(w.shape),
-            const(v.shape),
-        ],
-        out_specs=[img, img, const((2, d, mrows)), const((2, 8, v.shape[2]))],
+        in_specs=[pl.BlockSpec(memory_space=pltpu.SMEM), img, img, whole],
+        out_specs=[img, img, whole],
         out_shape=[
             jax.ShapeDtypeStruct(shp, F32),
             jax.ShapeDtypeStruct(shp, F32),
-            jax.ShapeDtypeStruct((2, d, mrows), F32),
-            jax.ShapeDtypeStruct((2, 8, v.shape[2]), F32),
+            jax.ShapeDtypeStruct(full.shape, BF),
         ],
         scratch_shapes=[
+            pltpu.VMEM((2, mrows, d), BF),
+            pltpu.VMEM((2, 8, vlen), F32),
+            pltpu.VMEM((2, d, mrows), F32),
+            pltpu.VMEM((2, 8, vlen), F32),
             pltpu.VMEM((2, S, d), BF),
             pltpu.VMEM((2, S, 3 * d), BF),
             pltpu.VMEM((2, NBLK, HEADS, BLOCK, 128), BF),
@@ -290,27 +727,41 @@
         compiler_params=pltpu.CompilerParams(
             dimension_semantics=("arbitrary",), vmem_limit_bytes=63 << 20
         ),
-        cost_estimate=pl.CostEstimate(flops=46 * 10**9, bytes_accessed=30 * 10**6, transcendentals=0),
         name="layers",
-    )(lengths, x.reshape(shp), cot.reshape(shp), w, v)
-
-
-def body(inputs, matrices, vectors, lengths, cotangent):
+    )(lengths, x.reshape(shp), cot.reshape(shp), full)
+
+
+def to_blocks(w, v):
+    pad = jnp.pad(v[:, :], ((0, 0), (0, w.shape[2] - v.shape[1])))
+    tail = jnp.pad(pad, ((0, 14), (0, 0)))
+    return jnp.concatenate([w[0], w[1], tail], 0)
+
+
+def body(z_count, dp_count, inputs, matrices, vectors, lengths, cotangent):
     d = inputs.shape[1]
-    w = lax.all_gather(matrices, ("dp", "sub"), axis=1, tiled=True)
-    v = lax.all_gather(vectors, ("dp", "sub"), axis=1, tiled=True).astype(F32)
-    ff = (w.shape[1] - 4 * d) // 2
-    out, gin, gwt, gv = compute(inputs, cotangent, w, v[:, None, :], lengths, d, ff)
-    gw = jnp.swapaxes(gwt, 1, 2)
-    gw = lax.psum_scatter(gw, ("dp", "sub"), scatter_dimension=1, tiled=True)
-    gv = lax.psum_scatter(jnp.sum(gv, 1), ("dp", "sub"), scatter_dimension=1, tiled=True)
+    devices = z_count * dp_count
+    rows, vrow = matrices.shape[1], vectors.shape[1]
+    vlen = vrow * devices
+    ff = (rows * devices - 4 * d) // 2
+    own_kernels = dp_count == 8
+    if own_kernels:
+        full = gather(matrices, vectors, z_count, devices)
+    else:
+        full = lax.all_gather(to_blocks(matrices, vectors), ("dp", "sub"), axis=0)
+    out, gin, gb = compute(inputs, cotangent, full, lengths, d, ff, vlen)
+    if own_kernels:
+        gw, gv = scatter(gb, z_count, rows, vrow)
+    else:
+        g = lax.psum_scatter(gb.astype(F32), ("dp", "sub"), scatter_dimension=0, tiled=True)[0]
+        gw = g[: 2 * rows].reshape(2, rows, d)
+        gv = g[2 * rows : 2 * rows + 2, :vrow]
     return (out.reshape(inputs.shape), gin.reshape(inputs.shape), gw, gv)
 
 
 def solution(mesh):
     split = ("dp", "sub")
     return jax.shard_map(
-        body,
+        partial(body, mesh.shape["sub"], mesh.shape["dp"]),
         mesh=mesh,
         in_specs=(P(split, None), P(None, split, None), P(None, split), P(split), P(split, None)),
         out_specs=(P(split, None), P(split, None), P(None, split, None), P(None, split)),

time: 590 us -> 279 us (0.47)
  waiting for transfers between devices: 281 us -> 0 us
  blocking collectives: 69.6 us -> 0 us
  Pallas kernels: 209 us -> 272 us
  between operations: 13.8 us -> 0.68 us
  local copies, waits for them, and re-layouts: 15.6 us -> 6.46 us
    unnamed x5 -> x0, waiting for transfers between devices: 281 us -> none
    all_gather x1 -> x0, blocking collectives: 69.6 us -> none  [body(): v = lax.all_gather(vectors, ('dp', 'sub'), axis=1, tiled=True).astype(F32)]
    pallas_call x0 -> x2, Pallas kernels: none -> 60.9 us  [the longest x1 32.8 us: scatter(): pl.pallas_call(partial(scatter_kernel, z_count), in_specs=[pl.BlockSpec(m...]
    transpose x1 -> x0, local copies, waits for them, and re-layouts: 10.2 us -> none  [body(): gw = jnp.swapaxes(gwt, 1, 2)]
  transfers between devices with their start and end apart: 3 -> 0, of which waited for: 2 -> 0; matrix products, arithmetic and copies ran while one was open for 2% -> 0% of each run, Pallas kernels for 0% -> 0%
where the time goes in v2:
time: 279 us
  Pallas kernels  272 us (97%)
  local copies, waits for them, and re-layouts  6.46 us (2%)
    pallas_call x1, Pallas kernels, compute(): pl.pallas_call(partial(kernel, (d, ff)), grid=(n,), in_specs=[pl.BlockSpe...  211 us
    pallas_call x1, Pallas kernels, scatter(): pl.pallas_call(partial(scatter_kernel, z_count), in_specs=[pl.BlockSpec(m...  32.8 us
    pallas_call x1, Pallas kernels, gather(): pl.pallas_call(partial(gather_kernel, z_count), in_specs=[pl.BlockSpec(me...  28.2 us
    unnamed x10, local copies, waits for them, and re-layouts  6.46 us

profile of v2, /device:TPU:0, one launch (start us, length us, event | category | flops | bytes accessed | tf_op | source)
XLA Modules:
  0.0 278.9 jit_solution(12523996500344361585)
XLA Ops:
  0.6 0.0 copy-start.2
  0.6 0.9 copy-done.2
  1.5 0.0 copy-start.3
  1.5 0.7 copy-done.3
  2.2 28.2 %gather.1.full_ref = bf16[32,208,256]{2,1,0:T(8,128)(2,1)S(1)} custom-call(bf16[2,96,256]{2,1,0:T(8,128)(2,1)S(1)} %copy-done.2, bf16[2,80]{1,0:T(2,128)(2,1)S(1)} %copy-done.3), custom_call_target="tpu_custom_call" | custom-call | tf_op jit(solution)/shard_map/gather/pallas_call | solution.py:634
  30.4 0.0 copy-start
  30.4 1.7 copy-done
  32.1 210.8 %layers.1 = (f32[4,12,12,8,256]{4,3,2,1,0:T(8,128)}, f32[4,12,12,8,256]{4,3,2,1,0:T(8,128)}, bf16[32,208,256]{2,1,0:T(8,128)(2,1)}) custom-call(s32[4]{0:T(128)} %len_ref.1, f32[4,12,12,8,256]{4,3,2,1,0:T(8,128)} %bitcast.4, f32[4,12,12,8,256]{4,3,2,1,0:T(8,128)} %bitcast.5, bf16[32,208,256]{2,1,0:T(8,128)(2,1)} %copy-done), custom_call_target="tpu_custom_call" | custom-call | tf_op jit(solution)/shard_map/layers/pallas_call | solution.py:695
  242.9 0.0 copy-start.1
  242.9 2.0 copy-done.1
  244.9 32.8 %scatter.1 = (f32[2,96,256]{2,1,0:T(8,128)S(1)}, f32[2,80]{1,0:T(2,128)S(1)}) custom-call(bf16[32,208,256]{2,1,0:T(8,128)(2,1)S(1)} %copy-done.1), custom_call_target="tpu_custom_call" | custom-call | tf_op jit(solution)/shard_map/scatter/pallas_call | solution.py:655
  277.7 0.7 copy.11
  278.3 0.6 copy.12
Async XLA Ops:
  0.6 0.9 copy-start.2
  1.5 0.7 copy-start.3
  30.4 1.7 copy-start
  242.9 2.0 copy-start.1

commit v3 on v2

--- a/solution.py
+++ b/solution.py
@@ -17,6 +17,8 @@
 LOG2E = 1.4426950408889634
 BF = jnp.bfloat16
 F32 = jnp.float32
+STATIC = False
+NB = (12,12,6,6,12,12)
 
 
 def mm(a, b, ca, cb):
@@ -101,7 +103,16 @@
             ref[lead + (slice(None), c * nb + b)] = v4[b]
 
     def rows(c, nb):
+        if isinstance(c, int):
+            return pl.ds(c * nb * BLOCK, nb * BLOCK)
         return pl.ds(pl.multiple_of(c * nb * BLOCK, BLOCK), nb * BLOCK)
+
+    def loop(n, step):
+        if STATIC or n == 1:
+            for c in range(n):
+                step(c, 0)
+        else:
+            lax.fori_loop(0, n, step, 0)
 
     def qkv_fwd(l, nb):
         def step(c, _):
@@ -112,29 +123,35 @@
             pk_s[l, s, :] = mm(n1, wqkv(l), 1, 1).astype(BF)
             return 0
 
-        lax.fori_loop(0, NBLK // nb, step, 0)
+        loop(NBLK // nb, step)
+
+    def heads_of(packed):
+        return [
+            tuple(packed[:, i * d + h * hw : i * d + (h + 1) * hw] for i in range(3))
+            for h in range(HEADS)
+        ]
 
     def attn_fwd(l, nb):
         mask = masks[l]
 
         def step(c, _):
+            each = [(b, h) for b in range(nb) for h in range(HEADS)]
+            qkv = []
             for b in range(nb):
-                s = pl.ds(pl.multiple_of((c * nb + b) * BLOCK, BLOCK), BLOCK)
-                pk = pk_s[l, s, :]
-                for h in range(HEADS):
-                    q = pk[:, h * hw : (h + 1) * hw]
-                    k = pk[:, d + h * hw : d + (h + 1) * hw]
-                    v = pk[:, 2 * d + h * hw : 2 * d + (h + 1) * hw]
-                    st = jnp.where(mask, mm(k, q, 1, 1), -1e30)
-                    m = jnp.max(st, 0, keepdims=True)
-                    p = jnp.exp2((st - m) * (qs * LOG2E))
-                    p = p * (1.0 / jnp.sum(p, 0, keepdims=True))
-                    p = p.astype(BF)
-                    pt_s[l, c * nb + b, h, :, 0:BLOCK] = p
-                    mix_s[l, s, h * hw : (h + 1) * hw] = mm(p, v, 0, 0).astype(BF)
+                qkv += heads_of(pk_s[l, rows(c * nb + b, 1), :])
+            scores = [mm(k, q, 1, 1) for q, k, v in qkv]
+            ps = []
+            for st in scores:
+                st = jnp.where(mask, st, -1e30)
+                p = jnp.exp2((st - jnp.max(st, 0, keepdims=True)) * (qs * LOG2E))
+                ps.append((p * (1.0 / jnp.sum(p, 0, keepdims=True))).astype(BF))
+            mixed = [mm(p, v, 0, 0).astype(BF) for p, (q, k, v) in zip(ps, qkv)]
+            for (b, h), p, m in zip(each, ps, mixed):
+                pt_s[l, c * nb + b, h, :, 0:BLOCK] = p
+                mix_s[l, rows(c * nb + b, 1), h * hw : (h + 1) * hw] = m
             return 0
 
-        lax.fori_loop(0, NBLK // nb, step, 0)
+        loop(NBLK // nb, step)
 
     def ffn_fwd(l, nb):
         def step(c, _):
@@ -152,7 +169,7 @@
                 act = (h * phi).astype(BF)
                 act_s[l, s, f * d : (f + 1) * d] = act
                 dact_s[l, s, f * d : (f + 1) * d] = (phi + h * e).astype(BF)
-                y = y + mm(act, w_ref[l, 4 * d + ff + f * d : 4 * d + ff + (f + 1) * d, :], 1, 0)
+            y = y + mm(act_s[l, s, :], w_ref[l, 4 * d + ff :, :], 1, 0)
             if l == 0:
                 store_perm(x1_s, c, nb, y)
             else:
@@ -162,7 +179,7 @@
                     out_ref[0, :, c * nb + b] = jnp.where(live, y4[b], 0.0)
             return 0
 
-        lax.fori_loop(0, NBLK // nb, step, 0)
+        loop(NBLK // nb, step)
 
     def acc_vec(l, i, val, n=1):
         gv_ref[l, :, i * d : (i + n) * d] += rowsum8(val)
@@ -191,14 +208,13 @@
             acc_vec(l, 5, gy)
             gyl = gy.astype(BF)
             gy_s[s, :] = gyl
-            gn2 = jnp.zeros((nb * BLOCK, d), F32)
             for f in range(ff // d):
                 wd = w_ref[l, 4 * d + ff + f * d : 4 * d + ff + (f + 1) * d, :]
                 gup = mm(gyl, wd, 1, 1) * dact_s[l, s, f * d : (f + 1) * d].astype(F32)
                 acc_vec(l, 6 + f, gup)
                 gupl = gup.astype(BF)
                 gup_s[s, f * d : (f + 1) * d] = gupl
-                gn2 = gn2 + mm(gupl, w_ref[l, (4 + f) * d : (5 + f) * d, :], 1, 0)
+            gn2 = mm(gup_s[s, :], w_ref[l, 4 * d : 4 * d + ff, :], 1, 0)
             gmid = gy + norm_back(l, 3, mid_s[l, s, :], gn2)
             gmid_s[s, :] = gmid
             acc_vec(l, 2, gmid)
@@ -207,31 +223,33 @@
             gmix_s[s, :] = mm(gml, wout(l), 1, 0).astype(BF)
             return 0
 
-        lax.fori_loop(0, NBLK // nb, step, 0)
+        loop(NBLK // nb, step)
 
     def attn_bwd(l, nb):
         def step(c, _):
+            each = [(b, h) for b in range(nb) for h in range(HEADS)]
+            qkv, gms = [], []
             for b in range(nb):
-                s = pl.ds(pl.multiple_of((c * nb + b) * BLOCK, BLOCK), BLOCK)
-                pk = pk_s[l, s, :]
-                gm2 = gmix_s[s, :]
-                for h in range(HEADS):
-                    q = pk[:, h * hw : (h + 1) * hw]
-                    k = pk[:, d + h * hw : d + (h + 1) * hw]
-                    v = pk[:, 2 * d + h * hw : 2 * d + (h + 1) * hw]
-                    gm = gm2[:, h * hw : (h + 1) * hw]
-                    pt = pt_s[l, c * nb + b, h, :, 0:BLOCK]
-                    pf = pt.astype(F32)
-                    gp = mm(v, gm, 1, 1)
-                    pg = pf * gp
-                    gs = (pg - pf * jnp.sum(pg, 0, keepdims=True)) * qs
-                    gs = gs.astype(BF)
-                    gpk_s[s, h * hw : (h + 1) * hw] = mm(gs, k, 0, 0).astype(BF)
-                    gpk_s[s, d + h * hw : d + (h + 1) * hw] = mm(gs, q, 1, 0).astype(BF)
-                    gpk_s[s, 2 * d + h * hw : 2 * d + (h + 1) * hw] = mm(pt, gm, 1, 0).astype(BF)
+                at = rows(c * nb + b, 1)
+                qkv += heads_of(pk_s[l, at, :])
+                gm = gmix_s[at, :]
+                gms += [gm[:, h * hw : (h + 1) * hw] for h in range(HEADS)]
+            pts = [pt_s[l, c * nb + b, h, :, 0:BLOCK] for b, h in each]
+            gps = [mm(v, gm, 1, 1) for (q, k, v), gm in zip(qkv, gms)]
+            gss = []
+            for pt, gp in zip(pts, gps):
+                pf = pt.astype(F32)
+                pg = pf * gp
+                gss.append(((pg - pf * jnp.sum(pg, 0, keepdims=True)) * qs).astype(BF))
+            gv = [mm(pt, gm, 1, 0).astype(BF) for pt, gm in zip(pts, gms)]
+            gk = [mm(gs, q, 1, 0).astype(BF) for gs, (q, k, v) in zip(gss, qkv)]
+            gq = [mm(gs, k, 0, 0).astype(BF) for gs, (q, k, v) in zip(gss, qkv)]
+            for n, (b, h) in enumerate(each):
+                for i, g in enumerate((gq, gk, gv)):
+                    gpk_s[rows(c * nb + b, 1), i * d + h * hw : i * d + (h + 1) * hw] = g[n]
             return 0
 
-        lax.fori_loop(0, NBLK // nb, step, 0)
+        loop(NBLK // nb, step)
 
     def qkv_bwd(l, nb):
         def step(c, _):
@@ -244,7 +262,7 @@
                 store_perm(gy0_s, c, nb, gx)
             return 0
 
-        lax.fori_loop(0, NBLK // nb, step, 0)
+        loop(NBLK // nb, step)
 
     def wgrads(l):
         gwt_ref[l, :, 0 : 3 * d] += mm(n1_s[l], gpk_s[...], 0, 0)
@@ -253,13 +271,13 @@
         gwt_ref[l, :, 4 * d + ff :] += mm(gy_s[...], act_s[l], 0, 0)
 
     for l in range(2):
-        qkv_fwd(l, 4)
-        attn_fwd(l, 2)
-        ffn_fwd(l, 4)
+        qkv_fwd(l, NB[0])
+        attn_fwd(l, NB[1])
+        ffn_fwd(l, NB[2])
     for l in (1, 0):
-        ffn_bwd(l, 4)
-        attn_bwd(l, 2)
-        qkv_bwd(l, 4)
+        ffn_bwd(l, NB[3])
+        attn_bwd(l, NB[4])
+        qkv_bwd(l, NB[5])
         wgrads(l)
 
     @pl.when(img == pl.num_programs(0) - 1)

time: 279 us -> 169 us (0.61)
  Pallas kernels: 272 us -> 162 us
    pallas_call x1, Pallas kernels: 211 us -> 101 us  [compute(): pl.pallas_call(partial(kernel, (d, ff)), grid=(n,), in_specs=[pl.BlockSpe...]
where the time goes in v3:
time: 169 us
  Pallas kernels  162 us (96%)
  local copies, waits for them, and re-layouts  6.46 us (4%)
    pallas_call x1, Pallas kernels, compute(): pl.pallas_call(partial(kernel, (d, ff)), grid=(n,), in_specs=[pl.BlockSpe...  101 us
    pallas_call x1, Pallas kernels, scatter(): pl.pallas_call(partial(scatter_kernel, z_count), in_specs=[pl.BlockSpec(m...  32.7 us
    pallas_call x1, Pallas kernels, gather(): pl.pallas_call(partial(gather_kernel, z_count), in_specs=[pl.BlockSpec(me...  28.2 us
    unnamed x10, local copies, waits for them, and re-layouts  6.46 us

profile of v3, /device:TPU:0, one launch (start us, length us, event | category | flops | bytes accessed | tf_op | source)
XLA Modules:
  0.0 169.0 jit_solution(67852389056809758)
XLA Ops:
  0.6 0.0 copy-start.2
  0.6 0.9 copy-done.2
  1.5 0.0 copy-start.3
  1.5 0.7 copy-done.3
  2.2 28.2 %gather.1.full_ref = bf16[32,208,256]{2,1,0:T(8,128)(2,1)S(1)} custom-call(bf16[2,96,256]{2,1,0:T(8,128)(2,1)S(1)} %copy-done.2, bf16[2,80]{1,0:T(2,128)(2,1)S(1)} %copy-done.3), custom_call_target="tpu_custom_call" | custom-call | tf_op jit(solution)/shard_map/gather/pallas_call | solution.py:652
  30.4 0.0 copy-start
  30.4 1.7 %copy-done = bf16[32,208,256]{2,1,0:T(8,128)(2,1)} copy-done((bf16[32,208,256]{2,1,0:T(8,128)(2,1)}, bf16[32,208,256]{2,1,0:T(8,128)(2,1)S(1)}, u32[]{:S(2)}) %copy-start) | copy-done | bytes 3407896
  32.1 100.9 %layers.1 = (f32[4,12,12,8,256]{4,3,2,1,0:T(8,128)}, f32[4,12,12,8,256]{4,3,2,1,0:T(8,128)}, bf16[32,208,256]{2,1,0:T(8,128)(2,1)}) custom-call(s32[4]{0:T(128)} %len_ref.1, f32[4,12,12,8,256]{4,3,2,1,0:T(8,128)} %bitcast.4, f32[4,12,12,8,256]{4,3,2,1,0:T(8,128)} %bitcast.5, bf16[32,208,256]{2,1,0:T(8,128)(2,1)} %copy-done), custom_call_target="tpu_custom_call" | custom-call | tf_op jit(solution)/shard_map/layers/pallas_call | solution.py:713
  133.0 0.0 copy-start.1
  133.0 2.0 %copy-done.1 = bf16[32,208,256]{2,1,0:T(8,128)(2,1)S(1)} copy-done((bf16[32,208,256]{2,1,0:T(8,128)(2,1)S(1)}, bf16[32,208,256]{2,1,0:T(8,128)(2,1)}, u32[]{:S(2)}) %copy-start.1) | copy-done | bytes 3407896
  135.0 32.7 %scatter.1 = (f32[2,96,256]{2,1,0:T(8,128)S(1)}, f32[2,80]{1,0:T(2,128)S(1)}) custom-call(bf16[32,208,256]{2,1,0:T(8,128)(2,1)S(1)} %copy-done.1), custom_call_target="tpu_custom_call" | custom-call | tf_op jit(solution)/shard_map/scatter/pallas_call | solution.py:673
  167.7 0.7 copy.11
  168.4 0.6 copy.12
Async XLA Ops:
  0.6 0.9 copy-start.2
  1.5 0.7 copy-start.3
  30.4 1.7 %copy-start = (bf16[32,208,256]{2,1,0:T(8,128)(2,1)}, bf16[32,208,256]{2,1,0:T(8,128)(2,1)S(1)}, u32[]{:S(2)}) copy-start(bf16[32,208,256]{2,1,0:T(8,128)(2,1)S(1)} %gather.1.full_ref) | copy-start | bytes 10223620
  133.0 2.0 %copy-start.1 = (bf16[32,208,256]{2,1,0:T(8,128)(2,1)S(1)}, bf16[32,208,256]{2,1,0:T(8,128)(2,1)}, u32[]{:S(2)}) copy-start(bf16[32,208,256]{2,1,0:T(8,128)(2,1)} %get-tuple-element.11.g_ref) | copy-start | bytes 10223620

commit v4 on v1

v4 whole, which is shorter than its diff:
```python
from functools import partial

import jax
import jax.numpy as jnp
from jax import lax
from jax.experimental import pallas as pl
from jax.experimental.pallas import tpu as pltpu
from jax.sharding import PartitionSpec as P

HEADS = 2
COLS = 96
ROWS = 12
SUBL = 8
BLOCK = 96
NBLK = 12
S = COLS * ROWS
LOG2E = 1.4426950408889634
BF = jnp.bfloat16
F32 = jnp.float32
STATIC = False
NB = (12,12,6,6,12,12)


def mm(a, b, ca, cb):
    return lax.dot_general(a, b, (((ca,), (cb,)), ((), ())), preferred_element_type=F32)


def standardize(v):
    c = v - jnp.mean(v, -1, keepdims=True)
    r = lax.rsqrt(jnp.mean(c * c, -1, keepdims=True) + 1e-05)
    return c * r, r


def rowsum8(v):
    return jnp.sum(v.reshape(v.shape[0] // 8, 8, v.shape[1]), axis=0)


def live_mask(length, slab, width):
    row = lax.broadcasted_iota(jnp.int32, (ROWS, SUBL, width), 0)
    col = lax.broadcasted_iota(jnp.int32, (ROWS, SUBL, width), 1)
    return row * COLS + col + slab * SUBL < length


def kernel(dims, own, z_count, *refs):
    d, ff = dims
    len_ref, x_ref, cot_ref, w_ref, v_ref, out_ref, gin_ref, gw_ref, gvo_ref = refs[:9]
    (
        vs_s, gwt_ref, gv_ref, n1_s, pk_s, pt_s, mix_s, mid_s, n2_s, act_s, dact_s,
        x1_s, gy0_s, gy_s, gup_s, gmid_s, gmidl_s, gmix_s, gpk_s,
    ) = refs[9:28]
    img = pl.program_id(0)
    last = img == pl.num_programs(0) - 1
    length = len_ref[img]
    hw = d // HEADS
    qs = hw ** -0.5
    if own:
        move = Moves(z_count, w_ref, v_ref, gwt_ref, gv_ref, vs_s, gw_ref, gvo_ref, refs[28:])
        wpart = move.weights
    else:

        def wpart(l, a, b):
            return w_ref[l, a:b, :]

    @pl.when(img == 0)
    def _():
        gwt_ref[...] = jnp.zeros_like(gwt_ref)
        gv_ref[...] = jnp.zeros_like(gv_ref)
        if own:
            move.gather_first()
        else:
            vs_s[:, 0:1, :] = v_ref[...]

    def wqkv(l):
        return wpart(l, 0, 3 * d)

    def wout(l):
        return wpart(l, 3 * d, 4 * d)

    def vec(l, i, n=1):
        return vs_s[l, 0:1, i * d : (i + n) * d]

    tril_b = lax.broadcasted_iota(jnp.int32, (BLOCK, BLOCK), 0)
    tril_a = lax.broadcasted_iota(jnp.int32, (BLOCK, BLOCK), 1)
    masks = (
        tril_b <= tril_a,
        (tril_b <= tril_a) & ((tril_b & (SUBL - 1)) == (tril_a & (SUBL - 1))),
    )

    def load_x(l, c, nb):
        if l == 0:
            return x_ref[0, pl.ds(c * nb, nb)].reshape(nb * BLOCK, d)
        return x1_s[pl.ds(c * nb, nb)].reshape(nb * BLOCK, d)

    def store_perm(ref, c, nb, val, lead=()):
        v4 = val.reshape(nb, NBLK, SUBL, d)
        for b in range(nb):
            ref[lead + (slice(None), c * nb + b)] = v4[b]

    def rows(c, nb):
        if isinstance(c, int):
            return pl.ds(c * nb * BLOCK, nb * BLOCK)
        return pl.ds(pl.multiple_of(c * nb * BLOCK, BLOCK), nb * BLOCK)

    def loop(n, step):
        if STATIC or n == 1:
            for c in range(n):
                step(c, 0)
        else:
            lax.fori_loop(0, n, step, 0)

    def qkv_fwd(l, nb):
        def step(c, _):
            s = rows(c, nb)
            xh, _r = standardize(load_x(l, c, nb))
            n1 = (xh * vec(l, 0) + vec(l, 1)).astype(BF)
            n1_s[l, s, :] = n1
            pk_s[l, s, :] = mm(n1, wqkv(l), 1, 1).astype(BF)
            return 0

        loop(NBLK // nb, step)

    def heads_of(packed):
        return [
            tuple(packed[:, i * d + h * hw : i * d + (h + 1) * hw] for i in range(3))
            for h in range(HEADS)
        ]

    def attn_fwd(l, nb):
        mask = masks[l]

        def step(c, _):
            each = [(b, h) for b in range(nb) for h in range(HEADS)]
            qkv = []
            for b in range(nb):
                qkv += heads_of(pk_s[l, rows(c * nb + b, 1), :])
            scores = [mm(k, q, 1, 1) for q, k, v in qkv]
            ps = []
            for st in scores:
                st = jnp.where(mask, st, -1e30)
                p = jnp.exp2((st - jnp.max(st, 0, keepdims=True)) * (qs * LOG2E))
                ps.append((p * (1.0 / jnp.sum(p, 0, keepdims=True))).astype(BF))
            mixed = [mm(p, v, 0, 0).astype(BF) for p, (q, k, v) in zip(ps, qkv)]
            for (b, h), p, m in zip(each, ps, mixed):
                pt_s[l, c * nb + b, h, :, 0:BLOCK] = p
                mix_s[l, rows(c * nb + b, 1), h * hw : (h + 1) * hw] = m
            return 0

        loop(NBLK // nb, step)

    def ffn_fwd(l, nb):
        def step(c, _):
            s = rows(c, nb)
            mid = load_x(l, c, nb) + mm(mix_s[l, s, :], wout(l), 1, 1) + vec(l, 2)
            mid_s[l, s, :] = mid
            xh, _r = standardize(mid)
            n2 = (xh * vec(l, 3) + vec(l, 4)).astype(BF)
            n2_s[l, s, :] = n2
            y = mid + vec(l, 5)
            for f in range(ff // d):
                h = mm(n2, wpart(l, (4 + f) * d, (5 + f) * d), 1, 1) + vec(l, 6 + f)
                phi = lax.erf(h * (2 ** -0.5)) * 0.5 + 0.5
                e = jnp.exp2(h * h * (-0.5 * LOG2E)) * 0.3989422804014327
                act = (h * phi).astype(BF)
                act_s[l, s, f * d : (f + 1) * d] = act
                dact_s[l, s, f * d : (f + 1) * d] = (phi + h * e).astype(BF)
            y = y + mm(act_s[l, s, :], wpart(l, 4 * d + ff, 4 * d + 2 * ff), 1, 0)
            if l == 0:
                store_perm(x1_s, c, nb, y)
            else:
                y4 = y.reshape(nb, NBLK, SUBL, d)
                for b in range(nb):
                    live = live_mask(length, c * nb + b, d)
                    out_ref[0, :, c * nb + b] = jnp.where(live, y4[b], 0.0)
            return 0

        loop(NBLK // nb, step)

    def acc_vec(l, i, val, n=1):
        gv_ref[l, :, i * d : (i + n) * d] += rowsum8(val)

    def norm_back(l, gi, v, gn):
        xh, r = standardize(v)
        acc_vec(l, gi, gn * xh)
        acc_vec(l, gi + 1, gn)
        e = gn * vec(l, gi)
        me = jnp.mean(e, -1, keepdims=True)
        mx = jnp.mean(e * xh, -1, keepdims=True)
        return r * (e - me - xh * mx)

    def ffn_bwd(l, nb):
        def step(c, _):
            s = rows(c, nb)
            if l == 0:
                gy = gy0_s[pl.ds(c * nb, nb)].reshape(nb * BLOCK, d)
            else:
                parts = []
                for b in range(nb):
                    live = live_mask(length, c * nb + b, d)
                    part = jnp.where(live, cot_ref[0, :, c * nb + b], 0.0)
                    parts.append(part.reshape(BLOCK, d))
                gy = jnp.concatenate(parts, 0) if nb > 1 else parts[0]
            acc_vec(l, 5, gy)
            gyl = gy.astype(BF)
            gy_s[s, :] = gyl
            for f in range(ff // d):
                wd = wpart(l, 4 * d + ff + f * d, 4 * d + ff + (f + 1) * d)
                gup = mm(gyl, wd, 1, 1) * dact_s[l, s, f * d : (f + 1) * d].astype(F32)
                acc_vec(l, 6 + f, gup)
                gupl = gup.astype(BF)
                gup_s[s, f * d : (f + 1) * d] = gupl
            gn2 = mm(gup_s[s, :], wpart(l, 4 * d, 4 * d + ff), 1, 0)
            gmid = gy + norm_back(l, 3, mid_s[l, s, :], gn2)
            gmid_s[s, :] = gmid
            acc_vec(l, 2, gmid)
            gml = gmid.astype(BF)
            gmidl_s[s, :] = gml
            gmix_s[s, :] = mm(gml, wout(l), 1, 0).astype(BF)
            return 0

        loop(NBLK // nb, step)

    def attn_bwd(l, nb):
        def step(c, _):
            each = [(b, h) for b in range(nb) for h in range(HEADS)]
            qkv, gms = [], []
            for b in range(nb):
                at = rows(c * nb + b, 1)
                qkv += heads_of(pk_s[l, at, :])
                gm = gmix_s[at, :]
                gms += [gm[:, h * hw : (h + 1) * hw] for h in range(HEADS)]
            pts = [pt_s[l, c * nb + b, h, :, 0:BLOCK] for b, h in each]
            gps = [mm(v, gm, 1, 1) for (q, k, v), gm in zip(qkv, gms)]
            gss = []
            for pt, gp in zip(pts, gps):
                pf = pt.astype(F32)
                pg = pf * gp
                gss.append(((pg - pf * jnp.sum(pg, 0, keepdims=True)) * qs).astype(BF))
            gv = [mm(pt, gm, 1, 0).astype(BF) for pt, gm in zip(pts, gms)]
            gk = [mm(gs, q, 1, 0).astype(BF) for gs, (q, k, v) in zip(gss, qkv)]
            gq = [mm(gs, k, 0, 0).astype(BF) for gs, (q, k, v) in zip(gss, qkv)]
            for n, (b, h) in enumerate(each):
                for i, g in enumerate((gq, gk, gv)):
                    gpk_s[rows(c * nb + b, 1), i * d + h * hw : i * d + (h + 1) * hw] = g[n]
            return 0

        loop(NBLK // nb, step)

    def qkv_bwd(l, nb):
        def step(c, _):
            s = rows(c, nb)
            gn1 = mm(gpk_s[s, :], wqkv(l), 1, 0)
            gx = gmid_s[s, :] + norm_back(l, 0, load_x(l, c, nb), gn1)
            if l == 0:
                gin_ref[0, pl.ds(c * nb, nb)] = gx.reshape(nb, NBLK, SUBL, d)
            else:
                store_perm(gy0_s, c, nb, gx)
            return 0

        loop(NBLK // nb, step)

    def wgrads(l):
        gwt_ref[l, :, 0 : 3 * d] += mm(n1_s[l], gpk_s[...], 0, 0)
        gwt_ref[l, :, 3 * d : 4 * d] += mm(mix_s[l], gmidl_s[...], 0, 0)
        gwt_ref[l, :, 4 * d : 4 * d + ff] += mm(n2_s[l], gup_s[...], 0, 0)
        gwt_ref[l, :, 4 * d + ff :] += mm(gy_s[...], act_s[l], 0, 0)

    def between(first, step):
        if own:
            pl.when(img == 0 if first else last)(step)

    for l in range(2):
        qkv_fwd(l, NB[0])
        if l == 0:
            between(True, lambda: move.gather_across(1))
        attn_fwd(l, NB[1])
        if l == 0:
            between(True, lambda: move.gather_diagonal(1))
        ffn_fwd(l, NB[2])
        if l == 0:
            between(True, lambda: move.gather_end(1))
    for l in (1, 0):
        ffn_bwd(l, NB[3])
        if l == 0:
            between(False, lambda: move.sum_chip(1))
        attn_bwd(l, NB[4])
        if l == 0:
            between(False, lambda: move.sum_across(1))
        qkv_bwd(l, NB[5])
        if l == 0:
            between(False, lambda: move.sum_column(1))
        wgrads(l)
        between(False, lambda: move.sum_start(l))

    @pl.when(last)
    def _():
        if own:
            move.sum_chip(0)
            move.sum_end(1)
            move.sum_across(0)
            move.sum_column(0)
            move.sum_end(0)
            move.drain()
        else:
            for l in range(2):
                gw_ref[l] = gwt_ref[l].T
                gvo_ref[l] = jnp.sum(gv_ref[l], 0, keepdims=True)


MESH = pl.DeviceIdType.MESH


def column(y, x, core):
    return (y * 2 + x) * 2 + core


class Moves:
    def __init__(self, z_count, w_ref, v_ref, gwt_ref, gv_ref, vs_s, gw_ref, gvo_ref, refs):
        self.z_count = z_count
        self.w_ref, self.v_ref, self.gwt_ref, self.gv_ref = w_ref, v_ref, gwt_ref, gv_ref
        self.vs_s, self.gw_ref, self.gvo_ref = vs_s, gw_ref, gvo_ref
        (
            self.full_s, self.gb_s, self.sib_s, self.own_s, self.diag_top_s, self.diag_low_s,
            self.cols_s, self.zr_s,
            self.ag_link, self.ag_core, self.ag_z, self.ag_x, self.ag_y, self.ag_c,
            self.rs_core_send, self.rs_core_recv, self.rs_send, self.rs_recv,
            self.rs_z_send, self.rs_z_recv,
        ) = refs
        self.rows, self.d = w_ref.shape[1], w_ref.shape[2]
        self.block = self.full_s.shape[2]
        self.half = self.diag_top_s.shape[2]
        self.devices = self.full_s.shape[1]
        self.vrow = v_ref.shape[1]
        self.vlen = self.vrow * self.devices
        dp, z = lax.axis_index("dp"), lax.axis_index("sub")
        self.dp, self.z = dp, z
        self.core = dp % 2
        self.x = dp // 2 % 2
        self.y = dp // 4
        y, x = self.y, self.x
        self.chips = ((y, x), (y, 1 - x), (1 - y, x), (1 - y, 1 - x))
        self.dp_x = column(y, 1 - x, self.core)
        self.dp_y = column(1 - y, x, self.core)
        self.dp_c = column(y, x, 1 - self.core)
        self.cut = (pl.ds(0, self.half), pl.ds(self.half, self.block - self.half))
        near = [0]
        for k in range(1, z_count // 2 + 1):
            near.append(k)
            if z_count - k != k:
                near.append(z_count - k)
        self.near = near

    def zz(self, k):
        return lax.rem(self.z + k, self.z_count)

    def index(self, kind, t, core=None):
        yy, xx = self.chips[kind]
        return column(yy, xx, self.core if core is None else core) * self.z_count + t

    def slot(self, kind, t):
        yy, xx = self.chips[kind]
        return (yy * 2 + xx) * self.z_count + t

    def weights(self, l, a, b):
        parts, rows = [], self.rows
        while a < b:
            i = a // rows
            e = min(b, (i + 1) * rows)
            parts.append(self.full_s[l, i, a - i * rows : e - i * rows, :])
            a = e
        return jnp.concatenate(parts, 0)

    def remote(self, src, dst, send, recv, target):
        return pltpu.make_async_remote_copy(
            src_ref=src, dst_ref=dst, send_sem=send, recv_sem=recv,
            device_id=target, device_id_type=MESH,
        )

    def ag_copy(self, l, kind, t, way, part=None):
        i, s = self.index(kind, t), self.slot(kind, t)
        ref = self.full_s.at[l, i] if part is None else self.full_s.at[l, i, self.cut[part], :]
        if way == "c":
            return self.remote(
                ref, ref, self.ag_c.at[l, s], self.ag_core.at[l, s], (self.dp_c, self.z)
            )
        send = self.ag_x if way == "x" else self.ag_y
        target = (self.dp_x if way == "x" else self.dp_y, self.z)
        return self.remote(ref, ref, send.at[l, s], self.ag_link.at[l, 1 if part else 0, s], target)

    def ag_along(self, l, k):
        ref = self.full_s.at[l, self.index(0, self.z)]
        s = self.slot(0, self.z)
        return self.remote(
            ref, ref, self.ag_z.at[l, k], self.ag_link.at[l, 0, s], (self.dp, self.zz(k))
        )

    def ag_wait(self, l, kind, t, part=None):
        i, s = self.index(kind, t), self.slot(kind, t)
        ref = self.full_s.at[l, i] if part is None else self.full_s.at[l, i, self.cut[part], :]
        self.remote(
            ref, ref, self.ag_c.at[l, s], self.ag_link.at[l, 1 if part else 0, s],
            (self.dp_c, self.z),
        ).wait_recv()

    def gather_along(self, l):
        for k in self.near[1:]:
            self.ag_along(l, k).start()

    def gather_spread(self, l):
        for k in self.near:
            t = self.zz(k)
            if k:
                self.ag_wait(l, 0, t)
            for way in "xyc":
                self.ag_copy(l, 0, t, way).start()

    def gather_across(self, l):
        for k in self.near:
            t = self.zz(k)
            self.ag_wait(l, 1, t)
            self.ag_copy(l, 1, t, "y", 0).start()
            self.ag_copy(l, 1, t, "c").start()
            self.ag_wait(l, 2, t)
            self.ag_copy(l, 2, t, "x", 1).start()
            self.ag_copy(l, 2, t, "c").start()

    def gather_diagonal(self, l):
        for k in self.near:
            t = self.zz(k)
            self.ag_wait(l, 3, t, 0)
            self.ag_wait(l, 3, t, 1)
            self.ag_copy(l, 3, t, "c").start()

    def gather_end(self, l):
        for kind in range(4):
            for t in range(self.z_count):
                i, s = self.index(kind, t, 1 - self.core), self.slot(kind, t)
                ref = self.full_s.at[l, i]
                self.remote(
                    ref, ref, self.ag_c.at[l, s], self.ag_core.at[l, s], (self.dp_c, self.z)
                ).wait_recv()
        vrow, vlen, rows = self.vrow, self.vlen, self.rows
        self.vs_s[l] = jnp.zeros((8, vlen), F32)
        for i in range(self.devices):
            part = self.full_s[l, i, rows : self.block, 0:128].astype(F32)[0:8]
            at = i * vrow // 128 * 128
            wide = jnp.concatenate([part, jnp.zeros_like(part)], 1)
            if i * vrow > at:
                wide = pltpu.roll(wide, i * vrow - at, 1)
            n = min(256, vlen - at)
            self.vs_s[l, 0:1, at : at + n] += wide[0:1, 0:n]

    def gather_first(self):
        barrier = pltpu.get_barrier_semaphore()
        partners = [(p, self.z) for p in (self.dp_x, self.dp_y, self.dp_c)]
        partners += [(self.dp, self.zz(k)) for k in self.near[1:]]
        for p in partners:
            pl.semaphore_signal(barrier, inc=1, device_id=p, device_id_type=MESH)
        me, rows = self.index(0, self.z), self.rows
        for l in range(2):
            self.full_s[l, me, 0:rows] = self.w_ref[l]
            tail = jnp.zeros((self.block - rows, self.d - self.vrow), BF)
            v = self.v_ref[l : l + 1, :].astype(F32)
            v = jnp.concatenate([v, jnp.zeros((self.block - rows - 1, self.vrow), F32)], 0)
            self.full_s[l, me, rows : self.block, :] = jnp.concatenate([v.astype(BF), tail], 1)
        pl.semaphore_wait(barrier, len(partners))
        self.gather_along(0)
        self.gather_spread(0)
        self.gather_along(1)
        self.gather_across(0)
        self.gather_spread(1)
        self.gather_diagonal(0)
        self.gather_end(0)

    def rs_core(self, l, kind):
        i = self.index(kind, 0, 1 - self.core)
        return self.remote(
            self.gb_s.at[l, pl.ds(i, self.z_count)], self.sib_s.at[l, kind],
            self.rs_core_send.at[l, kind], self.rs_core_recv.at[l, kind], (self.dp_c, self.z),
        )

    def rs_across(self, l, slot, t):
        kind, half, target, dst = (
            (3, 0, self.dp_y, self.diag_top_s.at[l, t]),
            (3, 1, self.dp_x, self.diag_low_s.at[l, t]),
            (2, 0, self.dp_y, self.cols_s.at[l, 0, t, self.cut[0], :]),
            (1, 1, self.dp_x, self.cols_s.at[l, 0, t, self.cut[1], :]),
            (1, 0, self.dp_x, self.cols_s.at[l, 1, t, self.cut[0], :]),
            (2, 1, self.dp_y, self.cols_s.at[l, 1, t, self.cut[1], :]),
        )[slot]
        return self.remote(
            self.gb_s.at[l, self.index(kind, t), self.cut[half], :], dst,
            self.rs_send.at[l, slot, t], self.rs_recv.at[l, slot, t], (target, self.z),
        )

    def rs_along(self, l, k):
        return self.remote(
            self.gb_s.at[l, self.index(0, self.zz(k))], self.zr_s.at[l, k - 1],
            self.rs_z_send.at[l, k], self.rs_z_recv.at[l, k], (self.dp, self.zz(k)),
        )

    def sum_start(self, l):
        rows, vrow, vlen = self.rows, self.vrow, self.vlen
        g = self.gwt_ref[l].T.astype(BF)
        gv = jnp.sum(self.gv_ref[l], 0, keepdims=True)
        gv = jnp.concatenate([gv, jnp.zeros((7, vlen), F32)], 0)
        for i in range(self.devices):
            self.gb_s[l, i, 0:rows] = g[i * rows : (i + 1) * rows]
            at = i * vrow // 128 * 128
            n = min(256, vlen - at)
            wide = gv[:, at : at + n]
            if n < 256:
                wide = jnp.concatenate([wide, jnp.zeros_like(wide)], 1)
            if i * vrow > at:
                wide = pltpu.roll(wide, 256 - (i * vrow - at), 1)
            wide = jnp.concatenate([wide, jnp.zeros_like(wide)], 0)
            self.gb_s[l, i, rows : self.block] = wide.astype(BF)
        for kind in (3, 1, 2, 0):
            self.rs_core(l, kind).start()

    def sum_chip(self, l):
        for kind, slots in ((3, (0, 1)), (1, (3,)), (2, (2,)), (0, ())):
            self.rs_core(l, kind).wait_recv()
            for t in range(self.z_count):
                i = self.index(kind, t)
                both = self.gb_s[l, i].astype(F32) + self.sib_s[l, kind, t].astype(F32)
                if kind == 0:
                    self.own_s[l, t] = both
                else:
                    self.gb_s[l, i] = both.astype(BF)
                for slot in slots:
                    self.rs_across(l, slot, t).start()

    def sum_across(self, l):
        for t in range(self.z_count):
            for slot, kind, half, ref in (
                (0, 1, 0, self.diag_top_s), (1, 2, 1, self.diag_low_s),
            ):
                self.rs_across(l, slot, t).wait_recv()
                i, cut = self.index(kind, t), self.cut[half]
                both = self.gb_s[l, i, cut].astype(F32) + ref[l, t].astype(F32)
                self.gb_s[l, i, cut] = both.astype(BF)
                self.rs_across(l, 4 if half == 0 else 5, t).start()

    def sum_column(self, l):
        for k in self.near[1:] + [0]:
            t = self.zz(k)
            for slot in (2, 3, 4, 5):
                self.rs_across(l, slot, t).wait_recv()
            total = self.own_s[l, t]
            for a in range(2):
                total = total + self.cols_s[l, a, t].astype(F32)
            if k:
                self.gb_s[l, self.index(0, t)] = total.astype(BF)
                self.rs_along(l, k).start()
            else:
                self.own_s[l, t] = total

    def sum_end(self, l):
        for k in self.near[1:]:
            self.rs_along(l, k).wait_recv()
        total = self.own_s[l, self.z]
        for k in self.near[1:]:
            total = total + self.zr_s[l, k - 1].astype(F32)
        self.gw_ref[l] = total[0 : self.rows]
        self.gvo_ref[l : l + 1, :] = total[self.rows : self.rows + 1, 0 : self.vrow]

    def drain(self):
        for l in range(2):
            for k in self.near[1:]:
                self.ag_along(l, k).wait_send()
                self.rs_along(l, k).wait_send()
            for t in range(self.z_count):
                for kind in range(4):
                    self.ag_copy(l, kind, t, "c").wait_send()
                self.ag_copy(l, 0, t, "x").wait_send()
                self.ag_copy(l, 0, t, "y").wait_send()
                self.ag_copy(l, 1, t, "y", 0).wait_send()
                self.ag_copy(l, 2, t, "x", 1).wait_send()
                for slot in range(6):
                    self.rs_across(l, slot, t).wait_send()
            for kind in range(4):
                self.rs_core(l, kind).wait_send()


def compute(x, cot, w, v, lengths, dims, own, z_count):
    d, ff = dims
    n = lengths.shape[0]
    mrows, vlen = 4 * d + 2 * ff, 6 * d + ff
    img = pl.BlockSpec((1, ROWS, NBLK, SUBL, d), lambda i: (i, 0, 0, 0, 0))
    shp = (n, ROWS, NBLK, SUBL, d)

    def whole(shape):
        zero = (0,) * len(shape)
        return pl.BlockSpec(shape, lambda i: zero, pipeline_mode=pl.Buffered(1))

    scratch = [
        pltpu.VMEM((2, 8, vlen), F32),
        pltpu.VMEM((2, d, mrows), F32),
        pltpu.VMEM((2, 8, vlen), F32),
        pltpu.VMEM((2, S, d), BF),
        pltpu.VMEM((2, S, 3 * d), BF),
        pltpu.VMEM((2, NBLK, HEADS, BLOCK, 128), BF),
        pltpu.VMEM((2, S, d), BF),
        pltpu.VMEM((2, S, d), F32),
        pltpu.VMEM((2, S, d), BF),
        pltpu.VMEM((2, S, ff), BF),
        pltpu.VMEM((2, S, ff), BF),
        pltpu.VMEM((NBLK, ROWS, SUBL, d), F32),
        pltpu.VMEM((ROWS, NBLK, SUBL, d), F32),
        pltpu.VMEM((S, d), BF),
        pltpu.VMEM((S, ff), BF),
        pltpu.VMEM((S, d), F32),
        pltpu.VMEM((S, d), BF),
        pltpu.VMEM((S, d), BF),
        pltpu.VMEM((S, 3 * d), BF),
    ]
    if own:
        rows, vrow = w.shape[1], v.shape[1]
        devices = mrows // rows
        block = rows + 16
        half = (block // 2 + 15) // 16 * 16
        zc = z_count
        dma = pltpu.SemaphoreType.DMA
        scratch += [
            pltpu.VMEM((2, devices, block, d), BF),
            pltpu.VMEM((2, devices, block, d), BF),
            pltpu.VMEM((2, 4, zc, block, d), BF),
            pltpu.VMEM((2, zc, block, d), F32),
            pltpu.VMEM((2, zc, half, d), BF),
            pltpu.VMEM((2, zc, block - half, d), BF),
            pltpu.VMEM((2, 2, zc, block, d), BF),
            pltpu.VMEM((2, zc - 1, block, d), BF),
            dma((2, 2, 4 * zc)), dma((2, 4 * zc)), dma((2, zc)),
            dma((2, 4 * zc)), dma((2, 4 * zc)), dma((2, 4 * zc)),
            dma((2, 4)), dma((2, 4)), dma((2, 6, zc)), dma((2, 6, zc)),
            dma((2, zc)), dma((2, zc)),
        ]
        gw_shape, gv_shape = (2, rows, d), (2, vrow)
    else:
        gw_shape, gv_shape = (2, mrows, d), (2, 1, vlen)
    return pl.pallas_call(
        partial(kernel, dims, own, z_count),
        grid=(n,),
        in_specs=[pl.BlockSpec(memory_space=pltpu.SMEM), img, img, whole(w.shape), whole(v.shape)],
        out_specs=[img, img, whole(gw_shape), whole(gv_shape)],
        out_shape=[
            jax.ShapeDtypeStruct(shp, F32),
            jax.ShapeDtypeStruct(shp, F32),
            jax.ShapeDtypeStruct(gw_shape, F32),
            jax.ShapeDtypeStruct(gv_shape, F32),
        ],
        scratch_shapes=scratch,
        compiler_params=pltpu.CompilerParams(
            dimension_semantics=("arbitrary",),
            vmem_limit_bytes=63 << 20,
            collective_id=0 if own else None,
            has_side_effects=own,
        ),
        name="layers",
    )(lengths, x.reshape(shp), cot.reshape(shp), w, v)


def body(z_count, dp_count, inputs, matrices, vectors, lengths, cotangent):
    d = inputs.shape[1]
    devices = z_count * dp_count
    ff = (matrices.shape[1] * devices - 4 * d) // 2
    own = dp_count == 8
    split = ("dp", "sub")
    if own:
        w, v = matrices, vectors
    else:
        w = lax.all_gather(matrices, split, axis=1, tiled=True)
        v = lax.all_gather(vectors, split, axis=1, tiled=True).astype(F32)[:, None, :]
    out, gin, gw, gv = compute(inputs, cotangent, w, v, lengths, (d, ff), own, z_count)
    if not own:
        gw = lax.psum_scatter(gw, split, scatter_dimension=1, tiled=True)
        gv = lax.psum_scatter(gv[:, 0], split, scatter_dimension=1, tiled=True)
    return (out.reshape(inputs.shape), gin.reshape(inputs.shape), gw, gv)


def solution(mesh):
    split = ("dp", "sub")
    return jax.shard_map(
        partial(body, mesh.shape["sub"], mesh.shape["dp"]),
        mesh=mesh,
        in_specs=(P(split, None), P(None, split, None), P(None, split), P(split), P(split, None)),
        out_specs=(P(split, None), P(split, None), P(None, split, None), P(None, split)),
        check_vma=False,
    )
```

time: 590 us -> 166 us (0.28)
  waiting for transfers between devices: 281 us -> 0 us
  blocking collectives: 69.6 us -> 0 us
  Pallas kernels: 209 us -> 157 us
  between operations: 13.8 us -> 0.65 us
  local copies, waits for them, and re-layouts: 15.6 us -> 8.43 us
    unnamed x5 -> x0, waiting for transfers between devices: 281 us -> none
    all_gather x1 -> x0, blocking collectives: 69.6 us -> none  [body(): v = lax.all_gather(vectors, ('dp', 'sub'), axis=1, tiled=True).astype(F32)]
    pallas_call x1, Pallas kernels: 209 us -> 157 us  [compute(): pl.pallas_call(partial(kernel, dims, own, z_count), grid=(n,), in_specs=[...]
    transpose x1 -> x0, local copies, waits for them, and re-layouts: 10.2 us -> none  [body(): gw = jnp.swapaxes(gwt, 1, 2)]
  transfers between devices with their start and end apart: 3 -> 0, of which waited for: 2 -> 0; matrix products, arithmetic and copies ran while one was open for 2% -> 0% of each run, Pallas kernels for 0% -> 0%
where the time goes in v4:
time: 166 us
  Pallas kernels  157 us (95%)
  local copies, waits for them, and re-layouts  8.43 us (5%)
    pallas_call x1, Pallas kernels, compute(): pl.pallas_call(partial(kernel, dims, own, z_count), grid=(n,), in_specs=[...  157 us
    unnamed x10, local copies, waits for them, and re-layouts  8.43 us

profile of v4, /device:TPU:0, one launch (start us, length us, event | category | flops | bytes accessed | tf_op | source)
XLA Modules:
  0.0 166.0 jit_solution(14980514369678999678)
XLA Ops:
  0.6 156.9 %layers.1 = (f32[4,12,12,8,256]{4,3,2,1,0:T(8,128)}, f32[4,12,12,8,256]{4,3,2,1,0:T(8,128)}, f32[2,96,256]{2,1,0:T(8,128)}, f32[2,80]{1,0:T(2,128)}) custom-call(s32[4]{0:T(128)} %refs_0_.1, f32[4,12,12,8,256]{4,3,2,1,0:T(8,128)} %bitcast.4, f32[4,12,12,8,256]{4,3,2,1,0:T(8,128)} %bitcast.5, bf16[2,96,256]{2,1,0:T(8,128)(2,1)} %refs_3_.1, bf16[2,80]{1,0:T(2,128)(2,1)} %refs_4_.1), custom_call_target="tpu_custom_call" | custom-call | tf_op jit(solution)/shard_map/layers/pallas_call | solution.py:641
  157.6 0.0 copy-start
  157.6 5.0 %copy.13 = f32[4608,256]{1,0:T(8,128)} copy(f32[4608,256]{1,0:T(8,128)} %bitcast.7) | data formatting | bytes 9437184
  162.6 0.0 copy-done
  162.6 0.0 copy-start.1
  162.6 0.0 copy-start.2
  162.6 2.2 %copy.14 = f32[4608,256]{1,0:T(8,128)} copy(f32[4608,256]{1,0:T(8,128)S(1)} %bitcast.6) | data formatting | bytes 9437184
  164.8 0.0 copy-done.1
  164.8 0.7 copy.15
  165.4 0.0 copy-done.2
  165.4 0.6 copy.16
Async XLA Ops:
  157.6 5.0 %copy-start = (f32[4,12,12,8,256]{4,3,2,1,0:T(8,128)S(1)}, f32[4,12,12,8,256]{4,3,2,1,0:T(8,128)}, u32[]{:S(2)}) copy-start(f32[4,12,12,8,256]{4,3,2,1,0:T(8,128)} %get-tuple-element.9) | copy-start | bytes 14155780
  162.6 2.2 %copy-start.1 = (f32[2,96,256]{2,1,0:T(8,128)S(1)}, f32[2,96,256]{2,1,0:T(8,128)}, u32[]{:S(2)}) copy-start(f32[2,96,256]{2,1,0:T(8,128)} %get-tuple-element.18) | copy-start | bytes 589828
  162.6 2.9 %copy-start.2 = (f32[2,80]{1,0:T(2,128)S(1)}, f32[2,80]{1,0:T(2,128)}, u32[]{:S(2)}) copy-start(f32[2,80]{1,0:T(2,128)} %get-tuple-element.19) | copy-start | bytes 1924

commit v5 on v4

--- a/solution.py
+++ b/solution.py
@@ -18,7 +18,7 @@
 BF = jnp.bfloat16
 F32 = jnp.float32
 STATIC = False
-NB = (12,12,6,6,12,12)
+SIZE = (288, 576, 576, 576)
 
 
 def mm(a, b, ca, cb):
@@ -147,33 +147,118 @@
 
         loop(NBLK // nb, step)
 
-    def ffn_fwd(l, nb):
-        def step(c, _):
-            s = rows(c, nb)
-            mid = load_x(l, c, nb) + mm(mix_s[l, s, :], wout(l), 1, 1) + vec(l, 2)
-            mid_s[l, s, :] = mid
-            xh, _r = standardize(mid)
-            n2 = (xh * vec(l, 3) + vec(l, 4)).astype(BF)
-            n2_s[l, s, :] = n2
-            y = mid + vec(l, 5)
-            for f in range(ff // d):
-                h = mm(n2, wpart(l, (4 + f) * d, (5 + f) * d), 1, 1) + vec(l, 6 + f)
-                phi = lax.erf(h * (2 ** -0.5)) * 0.5 + 0.5
-                e = jnp.exp2(h * h * (-0.5 * LOG2E)) * 0.3989422804014327
-                act = (h * phi).astype(BF)
-                act_s[l, s, f * d : (f + 1) * d] = act
-                dact_s[l, s, f * d : (f + 1) * d] = (phi + h * e).astype(BF)
-            y = y + mm(act_s[l, s, :], wpart(l, 4 * d + ff, 4 * d + 2 * ff), 1, 0)
+    def wup(l, f):
+        return wpart(l, (4 + f) * d, (5 + f) * d)
+
+    def wdown(l, f):
+        return wpart(l, 4 * d + ff + f * d, 4 * d + ff + (f + 1) * d)
+
+    def cols(f):
+        return slice(f * d, (f + 1) * d)
+
+    def mid_stage(l):
+        mid = load_x(l, 0, NBLK) + mm(mix_s[l], wout(l), 1, 1) + vec(l, 2)
+        mid_s[l] = mid
+        xh, _r = standardize(mid)
+        n2_s[l] = (xh * vec(l, 3) + vec(l, 4)).astype(BF)
+
+    def gelu_parts(h):
+        t = lax.erf(h * (2 ** -0.5)) + 1.0
+        act = ((0.5 * h) * t).astype(BF)
+        hb = h.astype(BF)
+        e = jnp.exp2(hb * hb * BF(-0.5 * LOG2E))
+        return act, t.astype(BF) + hb * e * BF(2 * 0.3989422804014327)
+
+    def chunks(size):
+        return [slice(r, r + size) for r in range(0, S, size)]
+
+    def ffn_fwd0():
+        l = 0
+        h = mm(n2_s[l], wup(l, 0), 1, 1)
+        for f in range(ff // d):
+            ahead = mm(n2_s[l], wup(l, f + 1), 1, 1) if f + 1 < ff // d else None
+            act, dact = gelu_parts(h + vec(l, 6 + f))
+            act_s[l, :, cols(f)] = act
+            dact_s[:, cols(f)] = dact
+            h = ahead
+        y = mid_s[l] + vec(l, 5) + mm(act_s[l], wpart(l, 4 * d + ff, 4 * d + 2 * ff), 1, 0)
+        store_perm(x1_s, 0, NBLK, y)
+
+    def load_gy1():
+        for b in range(NBLK):
+            live = live_mask(length, b, d)
+            part = jnp.where(live, cot_ref[0, :, b], 0.0).reshape(BLOCK, d)
+            acc_vec(1, 5, part)
+            gy_s[b * BLOCK : (b + 1) * BLOCK] = (0.5 * part).astype(BF)
+
+    def ffn_both1(size):
+        l, n = 1, ff // d
+
+        def products(f, s):
+            return mm(n2_s[l, s], wup(l, f), 1, 1), mm(gy_s[s], wdown(l, f), 1, 1)
+
+        ahead = {s.start: products(0, s) for s in chunks(size)}
+        for f in range(n + 1):
+            for i, s in enumerate(chunks(size)):
+                if f < n:
+                    h, ga = ahead[s.start]
+                    if f + 1 < n:
+                        ahead[s.start] = products(f + 1, s)
+                    act, dact = gelu_parts(h + vec(l, 6 + f))
+                    act_s[l, s, cols(f)] = act
+                    gup = ga * dact.astype(F32)
+                    acc_vec(l, 6 + f, gup)
+                    gup_s[s, cols(f)] = gup.astype(BF)
+                if f > 0 and i == 0:
+                    wgrad(l, 4 * d + ff + (f - 1) * d, gy_s[...], act_s[l, :, cols(f - 1)])
+                if f > 0 and i == min(1, S // size - 1):
+                    wgrad(l, 4 * d + (f - 1) * d, n2_s[l], gup_s[:, cols(f - 1)])
+
+    def ffn_end1():
+        l = 1
+        y = mid_s[l] + vec(l, 5) + mm(act_s[l], wpart(l, 4 * d + ff, 4 * d + 2 * ff), 1, 0)
+        y4 = y.reshape(NBLK, NBLK, SUBL, d)
+        for b in range(NBLK):
+            out_ref[0, :, b] = jnp.where(live_mask(length, b, d), y4[b], 0.0)
+
+    def ffn_bwd0(size):
+        l, n = 0, ff // d
+        for s in chunks(size):
+            gy = gy0_s[s.start // BLOCK : s.stop // BLOCK].reshape(size, d)
+            acc_vec(l, 5, gy)
+            gy_s[s] = (0.5 * gy).astype(BF)
+        ahead = {s.start: mm(gy_s[s], wdown(l, 0), 1, 1) for s in chunks(size)}
+        for f in range(n + 1):
+            for i, s in enumerate(chunks(size)):
+                if f < n:
+                    ga = ahead[s.start]
+                    if f + 1 < n:
+                        ahead[s.start] = mm(gy_s[s], wdown(l, f + 1), 1, 1)
+                    gup = ga * dact_s[s, cols(f)].astype(F32)
+                    acc_vec(l, 6 + f, gup)
+                    gup_s[s, cols(f)] = gup.astype(BF)
+                if f > 0 and i == 0:
+                    wgrad(l, 4 * d + ff + (f - 1) * d, gy_s[...], act_s[l, :, cols(f - 1)])
+                if f > 0 and i == min(1, S // size - 1):
+                    wgrad(l, 4 * d + (f - 1) * d, n2_s[l], gup_s[:, cols(f - 1)])
+
+    def mid_bwd(l, size):
+        for s in chunks(size):
+            gn2 = mm(gup_s[s], wpart(l, 4 * d, 4 * d + ff), 1, 0)
             if l == 0:
-                store_perm(x1_s, c, nb, y)
+                gy = gy0_s[s.start // BLOCK : s.stop // BLOCK].reshape(size, d)
             else:
-                y4 = y.reshape(nb, NBLK, SUBL, d)
-                for b in range(nb):
-                    live = live_mask(length, c * nb + b, d)
-                    out_ref[0, :, c * nb + b] = jnp.where(live, y4[b], 0.0)
-            return 0
-
-        loop(NBLK // nb, step)
+                parts = []
+                for b in range(s.start // BLOCK, s.stop // BLOCK):
+                    live = live_mask(length, b, d)
+                    parts.append(jnp.where(live, cot_ref[0, :, b], 0.0).reshape(BLOCK, d))
+                gy = jnp.concatenate(parts, 0)
+            gmid = gy + norm_back(l, 3, mid_s[l, s], gn2)
+            gmid_s[s] = gmid
+            acc_vec(l, 2, gmid)
+            gml = gmid.astype(BF)
+            gmidl_s[s] = gml
+            gmix_s[s] = mm(gml, wout(l), 1, 0).astype(BF)
 
     def acc_vec(l, i, val, n=1):
         gv_ref[l, :, i * d : (i + n) * d] += rowsum8(val)
@@ -186,38 +271,6 @@
         me = jnp.mean(e, -1, keepdims=True)
         mx = jnp.mean(e * xh, -1, keepdims=True)
         return r * (e - me - xh * mx)
-
-    def ffn_bwd(l, nb):
-        def step(c, _):
-            s = rows(c, nb)
-            if l == 0:
-                gy = gy0_s[pl.ds(c * nb, nb)].reshape(nb * BLOCK, d)
-            else:
-                parts = []
-                for b in range(nb):
-                    live = live_mask(length, c * nb + b, d)
-                    part = jnp.where(live, cot_ref[0, :, c * nb + b], 0.0)
-                    parts.append(part.reshape(BLOCK, d))
-                gy = jnp.concatenate(parts, 0) if nb > 1 else parts[0]
-            acc_vec(l, 5, gy)
-            gyl = gy.astype(BF)
-            gy_s[s, :] = gyl
-            for f in range(ff // d):
-                wd = wpart(l, 4 * d + ff + f * d, 4 * d + ff + (f + 1) * d)
-                gup = mm(gyl, wd, 1, 1) * dact_s[l, s, f * d : (f + 1) * d].astype(F32)
-                acc_vec(l, 6 + f, gup)
-                gupl = gup.astype(BF)
-                gup_s[s, f * d : (f + 1) * d] = gupl
-            gn2 = mm(gup_s[s, :], wpart(l, 4 * d, 4 * d + ff), 1, 0)
-            gmid = gy + norm_back(l, 3, mid_s[l, s, :], gn2)
-            gmid_s[s, :] = gmid
-            acc_vec(l, 2, gmid)
-            gml = gmid.astype(BF)
-            gmidl_s[s, :] = gml
-            gmix_s[s, :] = mm(gml, wout(l), 1, 0).astype(BF)
-            return 0
-
-        loop(NBLK // nb, step)
 
     def attn_bwd(l, nb):
         def step(c, _):
@@ -258,38 +311,47 @@
 
         loop(NBLK // nb, step)
 
+    def wgrad(l, at, a, b):
+        gwt_ref[l, :, at : at + b.shape[1]] += mm(a, b, 0, 0)
+
     def wgrads(l):
-        gwt_ref[l, :, 0 : 3 * d] += mm(n1_s[l], gpk_s[...], 0, 0)
-        gwt_ref[l, :, 3 * d : 4 * d] += mm(mix_s[l], gmidl_s[...], 0, 0)
-        gwt_ref[l, :, 4 * d : 4 * d + ff] += mm(n2_s[l], gup_s[...], 0, 0)
-        gwt_ref[l, :, 4 * d + ff :] += mm(gy_s[...], act_s[l], 0, 0)
+        wgrad(l, 0, n1_s[l], gpk_s[...])
+        wgrad(l, 3 * d, mix_s[l], gmidl_s[...])
+
+    def region(step):
+        pl.when(img >= 0)(step)
 
     def between(first, step):
         if own:
             pl.when(img == 0 if first else last)(step)
 
-    for l in range(2):
-        qkv_fwd(l, NB[0])
-        if l == 0:
-            between(True, lambda: move.gather_across(1))
-        attn_fwd(l, NB[1])
-        if l == 0:
-            between(True, lambda: move.gather_diagonal(1))
-        ffn_fwd(l, NB[2])
-        if l == 0:
-            between(True, lambda: move.gather_end(1))
-    for l in (1, 0):
-        ffn_bwd(l, NB[3])
-        if l == 0:
-            between(False, lambda: move.sum_chip(1))
-        attn_bwd(l, NB[4])
-        if l == 0:
-            between(False, lambda: move.sum_across(1))
-        qkv_bwd(l, NB[5])
-        if l == 0:
-            between(False, lambda: move.sum_column(1))
-        wgrads(l)
-        between(False, lambda: move.sum_start(l))
+    region(lambda: qkv_fwd(0, NBLK))
+    between(True, lambda: move.gather_across(1))
+    region(lambda: attn_fwd(0, NBLK))
+    between(True, lambda: move.gather_diagonal(1))
+    region(lambda: mid_stage(0))
+    region(ffn_fwd0)
+    between(True, lambda: move.gather_end(1))
+    region(lambda: qkv_fwd(1, NBLK))
+    region(lambda: attn_fwd(1, NBLK))
+    region(lambda: mid_stage(1))
+    region(load_gy1)
+    region(lambda: ffn_both1(SIZE[0]))
+    region(ffn_end1)
+    region(lambda: mid_bwd(1, SIZE[1]))
+    region(lambda: attn_bwd(1, NBLK))
+    region(lambda: qkv_bwd(1, NBLK))
+    region(lambda: wgrads(1))
+    between(False, lambda: move.sum_start(1))
+    region(lambda: ffn_bwd0(SIZE[2]))
+    between(False, lambda: move.sum_chip(1))
+    region(lambda: mid_bwd(0, SIZE[3]))
+    between(False, lambda: move.sum_across(1))
+    region(lambda: attn_bwd(0, NBLK))
+    between(False, lambda: move.sum_column(1))
+    region(lambda: qkv_bwd(0, NBLK))
+    region(lambda: wgrads(0))
+    between(False, lambda: move.sum_start(0))
 
     @pl.when(last)
     def _():
@@ -302,8 +364,12 @@
             move.drain()
         else:
             for l in range(2):
-                gw_ref[l] = gwt_ref[l].T
+                gw_ref[l] = whole_grad(gwt_ref, l, 4 * d + ff)
                 gvo_ref[l] = jnp.sum(gv_ref[l], 0, keepdims=True)
+
+
+def whole_grad(gwt_ref, l, cut):
+    return jnp.concatenate([gwt_ref[l, :, :cut], 2.0 * gwt_ref[l, :, cut:]], 1).T
 
 
 MESH = pl.DeviceIdType.MESH
@@ -500,7 +566,7 @@
 
     def sum_start(self, l):
         rows, vrow, vlen = self.rows, self.vrow, self.vlen
-        g = self.gwt_ref[l].T.astype(BF)
+        g = whole_grad(self.gwt_ref, l, (rows * self.devices) // 2 + 2 * self.d).astype(BF)
         gv = jnp.sum(self.gv_ref[l], 0, keepdims=True)
         gv = jnp.concatenate([gv, jnp.zeros((7, vlen), F32)], 0)
         for i in range(self.devices):
@@ -604,7 +670,7 @@
         pltpu.VMEM((2, S, d), F32),
         pltpu.VMEM((2, S, d), BF),
         pltpu.VMEM((2, S, ff), BF),
-        pltpu.VMEM((2, S, ff), BF),
+        pltpu.VMEM((S, ff), BF),
         pltpu.VMEM((NBLK, ROWS, SUBL, d), F32),
         pltpu.VMEM((ROWS, NBLK, SUBL, d), F32),
         pltpu.VMEM((S, d), BF),

time: 166 us -> 154 us (0.928)
  Pallas kernels: 157 us -> 145 us
    pallas_call x1, Pallas kernels: 157 us -> 145 us  [compute(): pl.pallas_call(partial(kernel, dims, own, z_count), grid=(n,), in_specs=[...]
where the time goes in v5:
time: 154 us
  Pallas kernels  145 us (94%)
  local copies, waits for them, and re-layouts  8.43 us (5%)
    pallas_call x1, Pallas kernels, compute(): pl.pallas_call(partial(kernel, dims, own, z_count), grid=(n,), in_specs=[...  145 us
    unnamed x10, local copies, waits for them, and re-layouts  8.43 us

profile of v5, /device:TPU:0, one launch (start us, length us, event | category | flops | bytes accessed | tf_op | source)
XLA Modules:
  0.0 153.9 jit_solution(11149720788467680230)
XLA Ops:
  0.6 144.8 %layers.1 = (f32[4,12,12,8,256]{4,3,2,1,0:T(8,128)}, f32[4,12,12,8,256]{4,3,2,1,0:T(8,128)}, f32[2,96,256]{2,1,0:T(8,128)}, f32[2,80]{1,0:T(2,128)}) custom-call(s32[4]{0:T(128)} %refs_0_.1, f32[4,12,12,8,256]{4,3,2,1,0:T(8,128)} %bitcast.4, f32[4,12,12,8,256]{4,3,2,1,0:T(8,128)} %bitcast.5, bf16[2,96,256]{2,1,0:T(8,128)(2,1)} %refs_3_.1, bf16[2,80]{1,0:T(2,128)(2,1)} %refs_4_.1), custom_call_target="tpu_custom_call" | custom-call | tf_op jit(solution)/shard_map/layers/pallas_call | solution.py:707
  145.5 0.0 copy-start
  145.5 5.0 %copy.13 = f32[4608,256]{1,0:T(8,128)} copy(f32[4608,256]{1,0:T(8,128)} %bitcast.7) | data formatting | bytes 9437184
  150.5 0.0 copy-done
  150.5 0.0 copy-start.1
  150.5 0.0 copy-start.2
  150.5 2.2 %copy.14 = f32[4608,256]{1,0:T(8,128)} copy(f32[4608,256]{1,0:T(8,128)S(1)} %bitcast.6) | data formatting | bytes 9437184
  152.7 0.0 copy-done.1
  152.7 0.7 copy.15
  153.4 0.0 copy-done.2
  153.4 0.6 copy.16
Async XLA Ops:
  145.5 5.0 %copy-start = (f32[4,12,12,8,256]{4,3,2,1,0:T(8,128)S(1)}, f32[4,12,12,8,256]{4,3,2,1,0:T(8,128)}, u32[]{:S(2)}) copy-start(f32[4,12,12,8,256]{4,3,2,1,0:T(8,128)} %get-tuple-element.9) | copy-start | bytes 14155780
  150.5 2.2 %copy-start.1 = (f32[2,96,256]{2,1,0:T(8,128)S(1)}, f32[2,96,256]{2,1,0:T(8,128)}, u32[]{:S(2)}) copy-start(f32[2,96,256]{2,1,0:T(8,128)} %get-tuple-element.18) | copy-start | bytes 589828
  150.5 2.9 %copy-start.2 = (f32[2,80]{1,0:T(2,128)S(1)}, f32[2,80]{1,0:T(2,128)}, u32[]{:S(2)}) copy-start(f32[2,80]{1,0:T(2,128)} %get-tuple-element.19) | copy-start | bytes 1924

commit v6 on v5

--- a/solution.py
+++ b/solution.py
@@ -18,7 +18,7 @@
 BF = jnp.bfloat16
 F32 = jnp.float32
 STATIC = False
-SIZE = (288, 576, 576, 576)
+SIZE = (288, 576, 576, 576, 576)
 
 
 def mm(a, b, ca, cb):
@@ -63,11 +63,14 @@
 
     @pl.when(img == 0)
     def _():
-        gwt_ref[...] = jnp.zeros_like(gwt_ref)
-        gv_ref[...] = jnp.zeros_like(gv_ref)
+        def clear():
+            gwt_ref[...] = jnp.zeros_like(gwt_ref)
+            gv_ref[...] = jnp.zeros_like(gv_ref)
+
         if own:
-            move.gather_first()
+            move.gather_first(clear)
         else:
+            clear()
             vs_s[:, 0:1, :] = v_ref[...]
 
     def wqkv(l):
@@ -172,15 +175,17 @@
     def chunks(size):
         return [slice(r, r + size) for r in range(0, S, size)]
 
-    def ffn_fwd0():
-        l = 0
-        h = mm(n2_s[l], wup(l, 0), 1, 1)
-        for f in range(ff // d):
-            ahead = mm(n2_s[l], wup(l, f + 1), 1, 1) if f + 1 < ff // d else None
-            act, dact = gelu_parts(h + vec(l, 6 + f))
-            act_s[l, :, cols(f)] = act
-            dact_s[:, cols(f)] = dact
-            h = ahead
+    def ffn_fwd0(size):
+        l, n = 0, ff // d
+        ahead = {s.start: mm(n2_s[l, s], wup(l, 0), 1, 1) for s in chunks(size)}
+        for f in range(n):
+            for s in chunks(size):
+                h = ahead[s.start]
+                if f + 1 < n:
+                    ahead[s.start] = mm(n2_s[l, s], wup(l, f + 1), 1, 1)
+                act, dact = gelu_parts(h + vec(l, 6 + f))
+                act_s[l, s, cols(f)] = act
+                dact_s[s, cols(f)] = dact
         y = mid_s[l] + vec(l, 5) + mm(act_s[l], wpart(l, 4 * d + ff, 4 * d + 2 * ff), 1, 0)
         store_perm(x1_s, 0, NBLK, y)
 
@@ -326,11 +331,10 @@
             pl.when(img == 0 if first else last)(step)
 
     region(lambda: qkv_fwd(0, NBLK))
-    between(True, lambda: move.gather_across(1))
     region(lambda: attn_fwd(0, NBLK))
     between(True, lambda: move.gather_diagonal(1))
     region(lambda: mid_stage(0))
-    region(ffn_fwd0)
+    region(lambda: ffn_fwd0(SIZE[4]))
     between(True, lambda: move.gather_end(1))
     region(lambda: qkv_fwd(1, NBLK))
     region(lambda: attn_fwd(1, NBLK))
@@ -346,19 +350,19 @@
     region(lambda: ffn_bwd0(SIZE[2]))
     between(False, lambda: move.sum_chip(1))
     region(lambda: mid_bwd(0, SIZE[3]))
-    between(False, lambda: move.sum_across(1))
     region(lambda: attn_bwd(0, NBLK))
-    between(False, lambda: move.sum_column(1))
     region(lambda: qkv_bwd(0, NBLK))
     region(lambda: wgrads(0))
     between(False, lambda: move.sum_start(0))
+    between(False, lambda: move.sum_across(1))
 
     @pl.when(last)
     def _():
         if own:
             move.sum_chip(0)
+            move.sum_column(1)
+            move.sum_across(0)
             move.sum_end(1)
-            move.sum_across(0)
             move.sum_column(0)
             move.sum_end(0)
             move.drain()
@@ -471,8 +475,8 @@
         for k in self.near[1:]:
             self.ag_along(l, k).start()
 
-    def gather_spread(self, l):
-        for k in self.near:
+    def gather_spread(self, l, steps):
+        for k in steps:
             t = self.zz(k)
             if k:
                 self.ag_wait(l, 0, t)
@@ -515,7 +519,7 @@
             n = min(256, vlen - at)
             self.vs_s[l, 0:1, at : at + n] += wide[0:1, 0:n]
 
-    def gather_first(self):
+    def gather_first(self, meanwhile):
         barrier = pltpu.get_barrier_semaphore()
         partners = [(p, self.z) for p in (self.dp_x, self.dp_y, self.dp_c)]
         partners += [(self.dp, self.zz(k)) for k in self.near[1:]]
@@ -530,10 +534,14 @@
             self.full_s[l, me, rows : self.block, :] = jnp.concatenate([v.astype(BF), tail], 1)
         pl.semaphore_wait(barrier, len(partners))
         self.gather_along(0)
-        self.gather_spread(0)
+        self.gather_spread(0, (0,))
         self.gather_along(1)
+        self.gather_spread(1, (0,))
+        meanwhile()
+        self.gather_spread(0, self.near[1:])
+        self.gather_spread(1, self.near[1:])
         self.gather_across(0)
-        self.gather_spread(1)
+        self.gather_across(1)
         self.gather_diagonal(0)
         self.gather_end(0)
 

time: 154 us -> 148 us (0.961)
  Pallas kernels: 145 us -> 138 us
    pallas_call x1, Pallas kernels: 145 us -> 138 us  [compute(): pl.pallas_call(partial(kernel, dims, own, z_count), grid=(n,), in_specs=[...]
where the time goes in v6:
time: 148 us
  Pallas kernels  138 us (93%)
  local copies, waits for them, and re-layouts  8.43 us (6%)
    pallas_call x1, Pallas kernels, compute(): pl.pallas_call(partial(kernel, dims, own, z_count), grid=(n,), in_specs=[...  138 us
    unnamed x10, local copies, waits for them, and re-layouts  8.43 us

profile of v6, /device:TPU:0, one launch (start us, length us, event | category | flops | bytes accessed | tf_op | source)
XLA Modules:
  0.0 147.6 jit_solution(15441448426161645534)
XLA Ops:
  0.6 138.5 %layers.1 = (f32[4,12,12,8,256]{4,3,2,1,0:T(8,128)}, f32[4,12,12,8,256]{4,3,2,1,0:T(8,128)}, f32[2,96,256]{2,1,0:T(8,128)}, f32[2,80]{1,0:T(2,128)}) custom-call(s32[4]{0:T(128)} %refs_0_.1, f32[4,12,12,8,256]{4,3,2,1,0:T(8,128)} %bitcast.4, f32[4,12,12,8,256]{4,3,2,1,0:T(8,128)} %bitcast.5, bf16[2,96,256]{2,1,0:T(8,128)(2,1)} %refs_3_.1, bf16[2,80]{1,0:T(2,128)(2,1)} %refs_4_.1), custom_call_target="tpu_custom_call" | custom-call | tf_op jit(solution)/shard_map/layers/pallas_call | solution.py:715
  139.1 0.0 copy-start
  139.1 5.0 %copy.13 = f32[4608,256]{1,0:T(8,128)} copy(f32[4608,256]{1,0:T(8,128)} %bitcast.7) | data formatting | bytes 9437184
  144.1 0.0 copy-done
  144.1 0.0 copy-start.1
  144.1 0.0 copy-start.2
  144.1 2.2 %copy.14 = f32[4608,256]{1,0:T(8,128)} copy(f32[4608,256]{1,0:T(8,128)S(1)} %bitcast.6) | data formatting | bytes 9437184
  146.3 0.0 copy-done.1
  146.3 0.7 copy.15
  147.0 0.0 copy-done.2
  147.0 0.6 copy.16
Async XLA Ops:
  139.1 5.0 %copy-start = (f32[4,12,12,8,256]{4,3,2,1,0:T(8,128)S(1)}, f32[4,12,12,8,256]{4,3,2,1,0:T(8,128)}, u32[]{:S(2)}) copy-start(f32[4,12,12,8,256]{4,3,2,1,0:T(8,128)} %get-tuple-element.9) | copy-start | bytes 14155780
  144.1 2.2 %copy-start.1 = (f32[2,96,256]{2,1,0:T(8,128)S(1)}, f32[2,96,256]{2,1,0:T(8,128)}, u32[]{:S(2)}) copy-start(f32[2,96,256]{2,1,0:T(8,128)} %get-tuple-element.18) | copy-start | bytes 589828
  144.1 2.9 %copy-start.2 = (f32[2,80]{1,0:T(2,128)S(1)}, f32[2,80]{1,0:T(2,128)}, u32[]{:S(2)}) copy-start(f32[2,80]{1,0:T(2,128)} %get-tuple-element.19) | copy-start | bytes 1924

commit v7 on v6

--- a/solution.py
+++ b/solution.py
@@ -19,6 +19,7 @@
 F32 = jnp.float32
 STATIC = False
 SIZE = (288, 576, 576, 576, 576)
+NB = (4, 4, 4, 4)
 
 
 def mm(a, b, ca, cb):
@@ -111,44 +112,59 @@
         else:
             lax.fori_loop(0, n, step, 0)
 
-    def qkv_fwd(l, nb):
-        def step(c, _):
-            s = rows(c, nb)
-            xh, _r = standardize(load_x(l, c, nb))
-            n1 = (xh * vec(l, 0) + vec(l, 1)).astype(BF)
-            n1_s[l, s, :] = n1
-            pk_s[l, s, :] = mm(n1, wqkv(l), 1, 1).astype(BF)
-            return 0
-
-        loop(NBLK // nb, step)
-
     def heads_of(packed):
         return [
             tuple(packed[:, i * d + h * hw : i * d + (h + 1) * hw] for i in range(3))
             for h in range(HEADS)
         ]
 
-    def attn_fwd(l, nb):
+    def pipeline(stages, n):
+        for i in range(n + len(stages) - 1):
+            for j in reversed(range(len(stages))):
+                if 0 <= i - j < n:
+                    stages[j](i - j)
+
+    def front(l, nb):
         mask = masks[l]
-
-        def step(c, _):
-            each = [(b, h) for b in range(nb) for h in range(HEADS)]
-            qkv = []
+        qkv, scores, ps = {}, {}, {}
+
+        def each(c):
+            return [(c * nb + b, h) for b in range(nb) for h in range(HEADS)]
+
+        def normed(c):
+            xh, _r = standardize(load_x(l, c, nb))
+            n1_s[l, rows(c, nb), :] = (xh * vec(l, 0) + vec(l, 1)).astype(BF)
+
+        def project(c):
+            pk_s[l, rows(c, nb), :] = mm(n1_s[l, rows(c, nb), :], wqkv(l), 1, 1).astype(BF)
+
+        def score(c):
+            qkv[c] = []
             for b in range(nb):
-                qkv += heads_of(pk_s[l, rows(c * nb + b, 1), :])
-            scores = [mm(k, q, 1, 1) for q, k, v in qkv]
-            ps = []
-            for st in scores:
+                qkv[c] += heads_of(pk_s[l, rows(c * nb + b, 1), :])
+            scores[c] = [mm(k, q, 1, 1) for q, k, v in qkv[c]]
+
+        def soft(c):
+            ps[c] = []
+            for st, (b, h) in zip(scores.pop(c), each(c)):
                 st = jnp.where(mask, st, -1e30)
                 p = jnp.exp2((st - jnp.max(st, 0, keepdims=True)) * (qs * LOG2E))
-                ps.append((p * (1.0 / jnp.sum(p, 0, keepdims=True))).astype(BF))
-            mixed = [mm(p, v, 0, 0).astype(BF) for p, (q, k, v) in zip(ps, qkv)]
-            for (b, h), p, m in zip(each, ps, mixed):
-                pt_s[l, c * nb + b, h, :, 0:BLOCK] = p
-                mix_s[l, rows(c * nb + b, 1), h * hw : (h + 1) * hw] = m
-            return 0
-
-        loop(NBLK // nb, step)
+                p = (p * (1.0 / jnp.sum(p, 0, keepdims=True))).astype(BF)
+                pt_s[l, b, h, :, 0:BLOCK] = p
+                ps[c].append(p)
+
+        def mix(c):
+            for p, (q, k, v), (b, h) in zip(ps.pop(c), qkv.pop(c), each(c)):
+                mix_s[l, rows(b, 1), h * hw : (h + 1) * hw] = mm(p, v, 0, 0).astype(BF)
+
+        def middle(c):
+            r = rows(c, nb)
+            mid = load_x(l, c, nb) + mm(mix_s[l, r, :], wout(l), 1, 1) + vec(l, 2)
+            mid_s[l, r, :] = mid
+            xh, _r = standardize(mid)
+            n2_s[l, r, :] = (xh * vec(l, 3) + vec(l, 4)).astype(BF)
+
+        pipeline([normed, project, score, soft, mix, middle], NBLK // nb)
 
     def wup(l, f):
         return wpart(l, (4 + f) * d, (5 + f) * d)
@@ -158,12 +174,6 @@
 
     def cols(f):
         return slice(f * d, (f + 1) * d)
-
-    def mid_stage(l):
-        mid = load_x(l, 0, NBLK) + mm(mix_s[l], wout(l), 1, 1) + vec(l, 2)
-        mid_s[l] = mid
-        xh, _r = standardize(mid)
-        n2_s[l] = (xh * vec(l, 3) + vec(l, 4)).astype(BF)
 
     def gelu_parts(h):
         t = lax.erf(h * (2 ** -0.5)) + 1.0
@@ -247,24 +257,6 @@
                 if f > 0 and i == min(1, S // size - 1):
                     wgrad(l, 4 * d + (f - 1) * d, n2_s[l], gup_s[:, cols(f - 1)])
 
-    def mid_bwd(l, size):
-        for s in chunks(size):
-            gn2 = mm(gup_s[s], wpart(l, 4 * d, 4 * d + ff), 1, 0)
-            if l == 0:
-                gy = gy0_s[s.start // BLOCK : s.stop // BLOCK].reshape(size, d)
-            else:
-                parts = []
-                for b in range(s.start // BLOCK, s.stop // BLOCK):
-                    live = live_mask(length, b, d)
-                    parts.append(jnp.where(live, cot_ref[0, :, b], 0.0).reshape(BLOCK, d))
-                gy = jnp.concatenate(parts, 0)
-            gmid = gy + norm_back(l, 3, mid_s[l, s], gn2)
-            gmid_s[s] = gmid
-            acc_vec(l, 2, gmid)
-            gml = gmid.astype(BF)
-            gmidl_s[s] = gml
-            gmix_s[s] = mm(gml, wout(l), 1, 0).astype(BF)
-
     def acc_vec(l, i, val, n=1):
         gv_ref[l, :, i * d : (i + n) * d] += rowsum8(val)
 
@@ -277,44 +269,72 @@
         mx = jnp.mean(e * xh, -1, keepdims=True)
         return r * (e - me - xh * mx)
 
-    def attn_bwd(l, nb):
-        def step(c, _):
-            each = [(b, h) for b in range(nb) for h in range(HEADS)]
-            qkv, gms = [], []
-            for b in range(nb):
-                at = rows(c * nb + b, 1)
-                qkv += heads_of(pk_s[l, at, :])
-                gm = gmix_s[at, :]
-                gms += [gm[:, h * hw : (h + 1) * hw] for h in range(HEADS)]
-            pts = [pt_s[l, c * nb + b, h, :, 0:BLOCK] for b, h in each]
-            gps = [mm(v, gm, 1, 1) for (q, k, v), gm in zip(qkv, gms)]
-            gss = []
-            for pt, gp in zip(pts, gps):
+    def back(l, nb):
+        gn2, gn1, qkv, gms, pts, gps, gss = {}, {}, {}, {}, {}, {}, {}
+
+        def each(c):
+            return [(c * nb + b, h) for b in range(nb) for h in range(HEADS)]
+
+        def up(c):
+            gn2[c] = mm(gup_s[rows(c, nb), :], wpart(l, 4 * d, 4 * d + ff), 1, 0)
+
+        def middle(c):
+            r = rows(c, nb)
+            if l == 0:
+                gy = gy0_s[c * nb : (c + 1) * nb].reshape(nb * BLOCK, d)
+            else:
+                parts = []
+                for b in range(c * nb, (c + 1) * nb):
+                    live = live_mask(length, b, d)
+                    parts.append(jnp.where(live, cot_ref[0, :, b], 0.0).reshape(BLOCK, d))
+                gy = jnp.concatenate(parts, 0)
+            gmid = gy + norm_back(l, 3, mid_s[l, r, :], gn2.pop(c))
+            gmid_s[r, :] = gmid
+            acc_vec(l, 2, gmid)
+            gmidl_s[r, :] = gmid.astype(BF)
+
+        def out(c):
+            r = rows(c, nb)
+            gmix_s[r, :] = mm(gmidl_s[r, :], wout(l), 1, 0).astype(BF)
+
+        def probs(c):
+            qkv[c], gms[c] = [], []
+            for b in range(c * nb, (c + 1) * nb):
+                qkv[c] += heads_of(pk_s[l, rows(b, 1), :])
+                gm = gmix_s[rows(b, 1), :]
+                gms[c] += [gm[:, h * hw : (h + 1) * hw] for h in range(HEADS)]
+            gps[c] = [mm(v, gm, 1, 1) for (q, k, v), gm in zip(qkv[c], gms[c])]
+
+        def store(c, i, grads):
+            for (b, h), g in zip(each(c), grads):
+                gpk_s[rows(b, 1), i * d + h * hw : i * d + (h + 1) * hw] = g.astype(BF)
+
+        def soft(c):
+            pts = [pt_s[l, b, h, :, 0:BLOCK] for b, h in each(c)]
+            gss[c] = []
+            for pt, gp in zip(pts, gps.pop(c)):
                 pf = pt.astype(F32)
                 pg = pf * gp
-                gss.append(((pg - pf * jnp.sum(pg, 0, keepdims=True)) * qs).astype(BF))
-            gv = [mm(pt, gm, 1, 0).astype(BF) for pt, gm in zip(pts, gms)]
-            gk = [mm(gs, q, 1, 0).astype(BF) for gs, (q, k, v) in zip(gss, qkv)]
-            gq = [mm(gs, k, 0, 0).astype(BF) for gs, (q, k, v) in zip(gss, qkv)]
-            for n, (b, h) in enumerate(each):
-                for i, g in enumerate((gq, gk, gv)):
-                    gpk_s[rows(c * nb + b, 1), i * d + h * hw : i * d + (h + 1) * hw] = g[n]
-            return 0
-
-        loop(NBLK // nb, step)
-
-    def qkv_bwd(l, nb):
-        def step(c, _):
-            s = rows(c, nb)
-            gn1 = mm(gpk_s[s, :], wqkv(l), 1, 0)
-            gx = gmid_s[s, :] + norm_back(l, 0, load_x(l, c, nb), gn1)
+                gss[c].append(((pg - pf * jnp.sum(pg, 0, keepdims=True)) * qs).astype(BF))
+            store(c, 2, [mm(pt, gm, 1, 0) for pt, gm in zip(pts, gms.pop(c))])
+
+        def heads(c):
+            gs, both = gss.pop(c), qkv.pop(c)
+            store(c, 1, [mm(g, q, 1, 0) for g, (q, k, v) in zip(gs, both)])
+            store(c, 0, [mm(g, k, 0, 0) for g, (q, k, v) in zip(gs, both)])
+
+        def project(c):
+            gn1[c] = mm(gpk_s[rows(c, nb), :], wqkv(l), 1, 0)
+
+        def first(c):
+            r = rows(c, nb)
+            gx = gmid_s[r, :] + norm_back(l, 0, load_x(l, c, nb), gn1.pop(c))
             if l == 0:
                 gin_ref[0, pl.ds(c * nb, nb)] = gx.reshape(nb, NBLK, SUBL, d)
             else:
                 store_perm(gy0_s, c, nb, gx)
-            return 0
-
-        loop(NBLK // nb, step)
+
+        pipeline([up, middle, out, probs, soft, heads, project, first], NBLK // nb)
 
     def wgrad(l, at, a, b):
         gwt_ref[l, :, at : at + b.shape[1]] += mm(a, b, 0, 0)
@@ -330,28 +350,20 @@
         if own:
             pl.when(img == 0 if first else last)(step)
 
-    region(lambda: qkv_fwd(0, NBLK))
-    region(lambda: attn_fwd(0, NBLK))
+    region(lambda: front(0, NB[0]))
     between(True, lambda: move.gather_diagonal(1))
-    region(lambda: mid_stage(0))
     region(lambda: ffn_fwd0(SIZE[4]))
     between(True, lambda: move.gather_end(1))
-    region(lambda: qkv_fwd(1, NBLK))
-    region(lambda: attn_fwd(1, NBLK))
-    region(lambda: mid_stage(1))
+    region(lambda: front(1, NB[1]))
     region(load_gy1)
     region(lambda: ffn_both1(SIZE[0]))
     region(ffn_end1)
-    region(lambda: mid_bwd(1, SIZE[1]))
-    region(lambda: attn_bwd(1, NBLK))
-    region(lambda: qkv_bwd(1, NBLK))
+    region(lambda: back(1, NB[2]))
     region(lambda: wgrads(1))
     between(False, lambda: move.sum_start(1))
     region(lambda: ffn_bwd0(SIZE[2]))
     between(False, lambda: move.sum_chip(1))
-    region(lambda: mid_bwd(0, SIZE[3]))
-    region(lambda: attn_bwd(0, NBLK))
-    region(lambda: qkv_bwd(0, NBLK))
+    region(lambda: back(0, NB[3]))
     region(lambda: wgrads(0))
     between(False, lambda: move.sum_start(0))
     between(False, lambda: move.sum_across(1))
@@ -359,11 +371,8 @@
     @pl.when(last)
     def _():
         if own:
-            move.sum_chip(0)
-            move.sum_column(1)
-            move.sum_across(0)
+            move.sum_tail(0, lambda: move.sum_column(1))
             move.sum_end(1)
-            move.sum_column(0)
             move.sum_end(0)
             move.drain()
         else:
@@ -412,15 +421,11 @@
         self.dp_y = column(1 - y, x, self.core)
         self.dp_c = column(y, x, 1 - self.core)
         self.cut = (pl.ds(0, self.half), pl.ds(self.half, self.block - self.half))
-        near = [0]
-        for k in range(1, z_count // 2 + 1):
-            near.append(k)
-            if z_count - k != k:
-                near.append(z_count - k)
-        self.near = near
+        self.near = list(range(z_count))
+        self.order = self.near[1:] + [0]
 
     def zz(self, k):
-        return lax.rem(self.z + k, self.z_count)
+        return self.z ^ k
 
     def index(self, kind, t, core=None):
         yy, xx = self.chips[kind]
@@ -509,15 +514,16 @@
                     ref, ref, self.ag_c.at[l, s], self.ag_core.at[l, s], (self.dp_c, self.z)
                 ).wait_recv()
         vrow, vlen, rows = self.vrow, self.vlen, self.rows
-        self.vs_s[l] = jnp.zeros((8, vlen), F32)
+        tiles = [jnp.zeros((8, 128), F32)] * (vlen // 128 + 1)
         for i in range(self.devices):
             part = self.full_s[l, i, rows : self.block, 0:128].astype(F32)[0:8]
-            at = i * vrow // 128 * 128
+            at = i * vrow // 128
             wide = jnp.concatenate([part, jnp.zeros_like(part)], 1)
-            if i * vrow > at:
-                wide = pltpu.roll(wide, i * vrow - at, 1)
-            n = min(256, vlen - at)
-            self.vs_s[l, 0:1, at : at + n] += wide[0:1, 0:n]
+            if i * vrow > at * 128:
+                wide = pltpu.roll(wide, i * vrow - at * 128, 1)
+            tiles[at] += wide[:, 0:128]
+            tiles[at + 1] += wide[:, 128:256]
+        self.vs_s[l] = jnp.concatenate(tiles[:-1], 1)
 
     def gather_first(self, meanwhile):
         barrier = pltpu.get_barrier_semaphore()
@@ -591,43 +597,71 @@
         for kind in (3, 1, 2, 0):
             self.rs_core(l, kind).start()
 
+    def chip_step(self, l, k):
+        t = self.zz(k)
+        for kind, slots in ((3, (0, 1)), (1, (3,)), (2, (2,)), (0, ())):
+            i = self.index(kind, t)
+            mine, other = self.gb_s[l, i], self.sib_s[l, kind, t]
+            if kind == 0:
+                self.own_s[l, t] = mine.astype(F32) + other.astype(F32)
+            else:
+                self.gb_s[l, i] = mine + other
+            for slot in slots:
+                self.rs_across(l, slot, t).start()
+
+    def across_step(self, l, k):
+        t = self.zz(k)
+        for slot, kind, half, ref in (
+            (0, 1, 0, self.diag_top_s), (1, 2, 1, self.diag_low_s),
+        ):
+            self.rs_across(l, slot, t).wait_recv()
+            i, cut = self.index(kind, t), self.cut[half]
+            self.gb_s[l, i, cut] = self.gb_s[l, i, cut] + ref[l, t]
+            self.rs_across(l, 4 if half == 0 else 5, t).start()
+
+    def column_step(self, l, k):
+        t = self.zz(k)
+        for slot in (2, 3, 4, 5):
+            self.rs_across(l, slot, t).wait_recv()
+        total = self.own_s[l, t]
+        for a in range(2):
+            total = total + self.cols_s[l, a, t].astype(F32)
+        if k:
+            self.gb_s[l, self.index(0, t)] = total.astype(BF)
+            self.rs_along(l, k).start()
+        else:
+            self.own_s[l, t] = total
+
+    def sum_core(self, l):
+        for kind in (3, 1, 2, 0):
+            self.rs_core(l, kind).wait_recv()
+
     def sum_chip(self, l):
-        for kind, slots in ((3, (0, 1)), (1, (3,)), (2, (2,)), (0, ())):
-            self.rs_core(l, kind).wait_recv()
-            for t in range(self.z_count):
-                i = self.index(kind, t)
-                both = self.gb_s[l, i].astype(F32) + self.sib_s[l, kind, t].astype(F32)
-                if kind == 0:
-                    self.own_s[l, t] = both
-                else:
-                    self.gb_s[l, i] = both.astype(BF)
-                for slot in slots:
-                    self.rs_across(l, slot, t).start()
+        self.sum_core(l)
+        for k in self.order:
+            self.chip_step(l, k)
 
     def sum_across(self, l):
-        for t in range(self.z_count):
-            for slot, kind, half, ref in (
-                (0, 1, 0, self.diag_top_s), (1, 2, 1, self.diag_low_s),
-            ):
-                self.rs_across(l, slot, t).wait_recv()
-                i, cut = self.index(kind, t), self.cut[half]
-                both = self.gb_s[l, i, cut].astype(F32) + ref[l, t].astype(F32)
-                self.gb_s[l, i, cut] = both.astype(BF)
-                self.rs_across(l, 4 if half == 0 else 5, t).start()
+        for k in self.order:
+            self.across_step(l, k)
 
     def sum_column(self, l):
-        for k in self.near[1:] + [0]:
-            t = self.zz(k)
-            for slot in (2, 3, 4, 5):
-                self.rs_across(l, slot, t).wait_recv()
-            total = self.own_s[l, t]
-            for a in range(2):
-                total = total + self.cols_s[l, a, t].astype(F32)
-            if k:
-                self.gb_s[l, self.index(0, t)] = total.astype(BF)
-                self.rs_along(l, k).start()
-            else:
-                self.own_s[l, t] = total
+        for k in self.order:
+            self.column_step(l, k)
+
+    def sum_tail(self, l, meanwhile):
+        order = self.order
+        self.sum_core(l)
+        self.chip_step(l, order[0])
+        self.chip_step(l, order[1])
+        meanwhile()
+        for n in range(len(order) + 2):
+            if n < len(order):
+                self.across_step(l, order[n])
+            if 1 <= n <= len(order):
+                self.column_step(l, order[n - 1])
+            if n + 2 < len(order):
+                self.chip_step(l, order[n + 2])
 
     def sum_end(self, l):
         for k in self.near[1:]:
@@ -738,7 +772,7 @@
     d = inputs.shape[1]
     devices = z_count * dp_count
     ff = (matrices.shape[1] * devices - 4 * d) // 2
-    own = dp_count == 8
+    own = dp_count == 8 and z_count & (z_count - 1) == 0
     split = ("dp", "sub")
     if own:
         w, v = matrices, vectors

time: 148 us -> 144 us (0.973)
  Pallas kernels: 138 us -> 135 us
    pallas_call x1, Pallas kernels: 138 us -> 135 us  [compute(): pl.pallas_call(partial(kernel, dims, own, z_count), grid=(n,), in_specs=[...]
where the time goes in v7:
time: 144 us
  Pallas kernels  135 us (94%)
  local copies, waits for them, and re-layouts  8.43 us (6%)
    pallas_call x1, Pallas kernels, compute(): pl.pallas_call(partial(kernel, dims, own, z_count), grid=(n,), in_specs=[...  135 us
    unnamed x10, local copies, waits for them, and re-layouts  8.43 us

profile of v7, /device:TPU:0, one launch (start us, length us, event | category | flops | bytes accessed | tf_op | source)
XLA Modules:
  0.0 143.8 jit_solution(13168343298000080033)
XLA Ops:
  0.6 134.7 %layers.1 = (f32[4,12,12,8,256]{4,3,2,1,0:T(8,128)}, f32[4,12,12,8,256]{4,3,2,1,0:T(8,128)}, f32[2,96,256]{2,1,0:T(8,128)}, f32[2,80]{1,0:T(2,128)}) custom-call(s32[4]{0:T(128)} %refs_0_.1, f32[4,12,12,8,256]{4,3,2,1,0:T(8,128)} %bitcast.4, f32[4,12,12,8,256]{4,3,2,1,0:T(8,128)} %bitcast.5, bf16[2,96,256]{2,1,0:T(8,128)(2,1)} %refs_3_.1, bf16[2,80]{1,0:T(2,128)(2,1)} %refs_4_.1), custom_call_target="tpu_custom_call" | custom-call | tf_op jit(solution)/shard_map/layers/pallas_call | solution.py:749
  135.3 0.0 copy-start
  135.3 5.0 %copy.13 = f32[4608,256]{1,0:T(8,128)} copy(f32[4608,256]{1,0:T(8,128)} %bitcast.7) | data formatting | bytes 9437184
  140.3 0.0 copy-done
  140.3 0.0 copy-start.1
  140.3 0.0 copy-start.2
  140.3 2.2 %copy.14 = f32[4608,256]{1,0:T(8,128)} copy(f32[4608,256]{1,0:T(8,128)S(1)} %bitcast.6) | data formatting | bytes 9437184
  142.5 0.0 copy-done.1
  142.5 0.7 copy.15
  143.2 0.0 copy-done.2
  143.2 0.6 copy.16
Async XLA Ops:
  135.3 5.0 %copy-start = (f32[4,12,12,8,256]{4,3,2,1,0:T(8,128)S(1)}, f32[4,12,12,8,256]{4,3,2,1,0:T(8,128)}, u32[]{:S(2)}) copy-start(f32[4,12,12,8,256]{4,3,2,1,0:T(8,128)} %get-tuple-element.9) | copy-start | bytes 14155780
  140.3 2.2 %copy-start.1 = (f32[2,96,256]{2,1,0:T(8,128)S(1)}, f32[2,96,256]{2,1,0:T(8,128)}, u32[]{:S(2)}) copy-start(f32[2,96,256]{2,1,0:T(8,128)} %get-tuple-element.18) | copy-start | bytes 589828
  140.3 2.9 %copy-start.2 = (f32[2,80]{1,0:T(2,128)S(1)}, f32[2,80]{1,0:T(2,128)}, u32[]{:S(2)}) copy-start(f32[2,80]{1,0:T(2,128)} %get-tuple-element.19) | copy-start | bytes 1924

commit v8 on v7

--- a/solution.py
+++ b/solution.py
@@ -20,6 +20,7 @@
 STATIC = False
 SIZE = (288, 576, 576, 576, 576)
 NB = (4, 4, 4, 4)
+FLAGS = (True, True)
 
 
 def mm(a, b, ca, cb):
@@ -164,7 +165,26 @@
             xh, _r = standardize(mid)
             n2_s[l, r, :] = (xh * vec(l, 3) + vec(l, 4)).astype(BF)
 
-        pipeline([normed, project, score, soft, mix, middle], NBLK // nb)
+        def hidden(c):
+            r = rows(c, nb)
+            n = ff // d
+            h = mm(n2_s[l, r, :], wup(l, 0), 1, 1)
+            for f in range(n):
+                ahead = mm(n2_s[l, r, :], wup(l, f + 1), 1, 1) if f + 1 < n else None
+                act, dact = gelu_parts(h + vec(l, 6 + f))
+                act_s[l, r, cols(f)] = act
+                dact_s[r, cols(f)] = dact
+                h = ahead
+
+        def result(c):
+            r = rows(c, nb)
+            y = mm(act_s[l, r, :], wpart(l, 4 * d + ff, 4 * d + 2 * ff), 1, 0)
+            store_perm(x1_s, c, nb, y + mid_s[l, r, :] + vec(l, 5))
+
+        stages = [normed, project, score, soft, mix, middle]
+        if l == 0 and FLAGS[1]:
+            stages += [hidden, result]
+        pipeline(stages, NBLK // nb)
 
     def wup(l, f):
         return wpart(l, (4 + f) * d, (5 + f) * d)
@@ -334,7 +354,15 @@
             else:
                 store_perm(gy0_s, c, nb, gx)
 
-        pipeline([up, middle, out, probs, soft, heads, project, first], NBLK // nb)
+        def weights(c):
+            r = rows(c, nb)
+            wgrad(l, 0, n1_s[l, r, :], gpk_s[r, :])
+            wgrad(l, 3 * d, mix_s[l, r, :], gmidl_s[r, :])
+
+        stages = [up, middle, out, probs, soft, heads, project, first]
+        if FLAGS[0]:
+            stages[7] = lambda c: (first(c), weights(c))
+        pipeline(stages, NBLK // nb)
 
     def wgrad(l, at, a, b):
         gwt_ref[l, :, at : at + b.shape[1]] += mm(a, b, 0, 0)
@@ -351,20 +379,22 @@
             pl.when(img == 0 if first else last)(step)
 
     region(lambda: front(0, NB[0]))
-    between(True, lambda: move.gather_diagonal(1))
-    region(lambda: ffn_fwd0(SIZE[4]))
+    if not FLAGS[1]:
+        region(lambda: ffn_fwd0(SIZE[4]))
     between(True, lambda: move.gather_end(1))
     region(lambda: front(1, NB[1]))
     region(load_gy1)
     region(lambda: ffn_both1(SIZE[0]))
     region(ffn_end1)
     region(lambda: back(1, NB[2]))
-    region(lambda: wgrads(1))
+    if not FLAGS[0]:
+        region(lambda: wgrads(1))
     between(False, lambda: move.sum_start(1))
     region(lambda: ffn_bwd0(SIZE[2]))
     between(False, lambda: move.sum_chip(1))
     region(lambda: back(0, NB[3]))
-    region(lambda: wgrads(0))
+    if not FLAGS[0]:
+        region(lambda: wgrads(0))
     between(False, lambda: move.sum_start(0))
     between(False, lambda: move.sum_across(1))
 
@@ -420,7 +450,11 @@
         self.dp_x = column(y, 1 - x, self.core)
         self.dp_y = column(1 - y, x, self.core)
         self.dp_c = column(y, x, 1 - self.core)
-        self.cut = (pl.ds(0, self.half), pl.ds(self.half, self.block - self.half))
+        self.size = (self.block, self.rows)
+        self.cuts = (
+            (pl.ds(0, self.half), pl.ds(self.half, self.block - self.half)),
+            (pl.ds(0, self.rows // 2), pl.ds(self.rows // 2, self.rows // 2)),
+        )
         self.near = list(range(z_count))
         self.order = self.near[1:] + [0]
 
@@ -444,6 +478,10 @@
             a = e
         return jnp.concatenate(parts, 0)
 
+    def piece(self, l, i, part=None):
+        rows = pl.ds(0, self.size[l]) if part is None else self.cuts[l][part]
+        return self.full_s.at[l, i, rows, :]
+
     def remote(self, src, dst, send, recv, target):
         return pltpu.make_async_remote_copy(
             src_ref=src, dst_ref=dst, send_sem=send, recv_sem=recv,
@@ -452,7 +490,7 @@
 
     def ag_copy(self, l, kind, t, way, part=None):
         i, s = self.index(kind, t), self.slot(kind, t)
-        ref = self.full_s.at[l, i] if part is None else self.full_s.at[l, i, self.cut[part], :]
+        ref = self.piece(l, i, part)
         if way == "c":
             return self.remote(
                 ref, ref, self.ag_c.at[l, s], self.ag_core.at[l, s], (self.dp_c, self.z)
@@ -462,7 +500,7 @@
         return self.remote(ref, ref, send.at[l, s], self.ag_link.at[l, 1 if part else 0, s], target)
 
     def ag_along(self, l, k):
-        ref = self.full_s.at[l, self.index(0, self.z)]
+        ref = self.piece(l, self.index(0, self.z))
         s = self.slot(0, self.z)
         return self.remote(
             ref, ref, self.ag_z.at[l, k], self.ag_link.at[l, 0, s], (self.dp, self.zz(k))
@@ -470,7 +508,7 @@
 
     def ag_wait(self, l, kind, t, part=None):
         i, s = self.index(kind, t), self.slot(kind, t)
-        ref = self.full_s.at[l, i] if part is None else self.full_s.at[l, i, self.cut[part], :]
+        ref = self.piece(l, i, part)
         self.remote(
             ref, ref, self.ag_c.at[l, s], self.ag_link.at[l, 1 if part else 0, s],
             (self.dp_c, self.z),
@@ -509,21 +547,25 @@
         for kind in range(4):
             for t in range(self.z_count):
                 i, s = self.index(kind, t, 1 - self.core), self.slot(kind, t)
-                ref = self.full_s.at[l, i]
+                ref = self.piece(l, i)
                 self.remote(
                     ref, ref, self.ag_c.at[l, s], self.ag_core.at[l, s], (self.dp_c, self.z)
                 ).wait_recv()
+        if l == 1:
+            return
         vrow, vlen, rows = self.vrow, self.vlen, self.rows
         tiles = [jnp.zeros((8, 128), F32)] * (vlen // 128 + 1)
         for i in range(self.devices):
-            part = self.full_s[l, i, rows : self.block, 0:128].astype(F32)[0:8]
+            part = self.full_s[0, i, rows : self.block, 0:128].astype(F32)[0:8]
             at = i * vrow // 128
             wide = jnp.concatenate([part, jnp.zeros_like(part)], 1)
             if i * vrow > at * 128:
                 wide = pltpu.roll(wide, i * vrow - at * 128, 1)
             tiles[at] += wide[:, 0:128]
             tiles[at + 1] += wide[:, 128:256]
-        self.vs_s[l] = jnp.concatenate(tiles[:-1], 1)
+        both = jnp.concatenate(tiles[:-1], 1)
+        self.vs_s[0] = both
+        self.vs_s[1] = pltpu.roll(both, 7, 0)
 
     def gather_first(self, meanwhile):
         barrier = pltpu.get_barrier_semaphore()
@@ -534,10 +576,10 @@
         me, rows = self.index(0, self.z), self.rows
         for l in range(2):
             self.full_s[l, me, 0:rows] = self.w_ref[l]
-            tail = jnp.zeros((self.block - rows, self.d - self.vrow), BF)
-            v = self.v_ref[l : l + 1, :].astype(F32)
-            v = jnp.concatenate([v, jnp.zeros((self.block - rows - 1, self.vrow), F32)], 0)
-            self.full_s[l, me, rows : self.block, :] = jnp.concatenate([v.astype(BF), tail], 1)
+        tail = jnp.zeros((self.block - rows, self.d - self.vrow), BF)
+        v = self.v_ref[...].astype(F32)
+        v = jnp.concatenate([v, jnp.zeros((self.block - rows - 2, self.vrow), F32)], 0)
+        self.full_s[0, me, rows : self.block, :] = jnp.concatenate([v.astype(BF), tail], 1)
         pl.semaphore_wait(barrier, len(partners))
         self.gather_along(0)
         self.gather_spread(0, (0,))
@@ -549,63 +591,89 @@
         self.gather_across(0)
         self.gather_across(1)
         self.gather_diagonal(0)
+        self.gather_diagonal(1)
         self.gather_end(0)
 
     def rs_core(self, l, kind):
         i = self.index(kind, 0, 1 - self.core)
         return self.remote(
-            self.gb_s.at[l, pl.ds(i, self.z_count)], self.sib_s.at[l, kind],
+            self.gb_s.at[l, pl.ds(i, self.z_count), pl.ds(0, self.size[l]), :],
+            self.sib_s.at[l, kind, :, pl.ds(0, self.size[l]), :],
             self.rs_core_send.at[l, kind], self.rs_core_recv.at[l, kind], (self.dp_c, self.z),
         )
 
     def rs_across(self, l, slot, t):
+        cuts = self.cuts[l]
         kind, half, target, dst = (
-            (3, 0, self.dp_y, self.diag_top_s.at[l, t]),
-            (3, 1, self.dp_x, self.diag_low_s.at[l, t]),
-            (2, 0, self.dp_y, self.cols_s.at[l, 0, t, self.cut[0], :]),
-            (1, 1, self.dp_x, self.cols_s.at[l, 0, t, self.cut[1], :]),
-            (1, 0, self.dp_x, self.cols_s.at[l, 1, t, self.cut[0], :]),
-            (2, 1, self.dp_y, self.cols_s.at[l, 1, t, self.cut[1], :]),
+            (3, 0, self.dp_y, self.diag_top_s.at[l, t, pl.ds(0, cuts[0].size), :]),
+            (3, 1, self.dp_x, self.diag_low_s.at[l, t, pl.ds(0, cuts[1].size), :]),
+            (2, 0, self.dp_y, self.cols_s.at[l, 0, t, cuts[0], :]),
+            (1, 1, self.dp_x, self.cols_s.at[l, 0, t, cuts[1], :]),
+            (1, 0, self.dp_x, self.cols_s.at[l, 1, t, cuts[0], :]),
+            (2, 1, self.dp_y, self.cols_s.at[l, 1, t, cuts[1], :]),
         )[slot]
         return self.remote(
-            self.gb_s.at[l, self.index(kind, t), self.cut[half], :], dst,
+            self.gb_s.at[l, self.index(kind, t), cuts[half], :], dst,
             self.rs_send.at[l, slot, t], self.rs_recv.at[l, slot, t], (target, self.z),
         )
 
     def rs_along(self, l, k):
         return self.remote(
-            self.gb_s.at[l, self.index(0, self.zz(k))], self.zr_s.at[l, k - 1],
+            self.gb_s.at[l, self.index(0, self.zz(k)), pl.ds(0, self.size[l]), :],
+            self.zr_s.at[l, k - 1, pl.ds(0, self.size[l]), :],
             self.rs_z_send.at[l, k], self.rs_z_recv.at[l, k], (self.dp, self.zz(k)),
         )
 
     def sum_start(self, l):
-        rows, vrow, vlen = self.rows, self.vrow, self.vlen
-        g = whole_grad(self.gwt_ref, l, (rows * self.devices) // 2 + 2 * self.d).astype(BF)
-        gv = jnp.sum(self.gv_ref[l], 0, keepdims=True)
-        gv = jnp.concatenate([gv, jnp.zeros((7, vlen), F32)], 0)
-        for i in range(self.devices):
-            self.gb_s[l, i, 0:rows] = g[i * rows : (i + 1) * rows]
-            at = i * vrow // 128 * 128
-            n = min(256, vlen - at)
-            wide = gv[:, at : at + n]
-            if n < 256:
-                wide = jnp.concatenate([wide, jnp.zeros_like(wide)], 1)
-            if i * vrow > at:
-                wide = pltpu.roll(wide, 256 - (i * vrow - at), 1)
-            wide = jnp.concatenate([wide, jnp.zeros_like(wide)], 0)
-            self.gb_s[l, i, rows : self.block] = wide.astype(BF)
-        for kind in (3, 1, 2, 0):
-            self.rs_core(l, kind).start()
+        rows, vrow, vlen, zc = self.rows, self.vrow, self.vlen, self.z_count
+        cut = (rows * self.devices) // 2 + 2 * self.d
+        gv = [jnp.sum(self.gv_ref[a], 0, keepdims=True) for a in range(2)]
+        gv = jnp.concatenate(gv + [jnp.zeros((6, vlen), F32)], 0)
+        for g in range(8):
+            lo, hi = g * zc * rows, (g + 1) * zc * rows
+            mid = min(max(lo, cut), hi)
+            part = []
+            if lo < mid:
+                part.append(self.gwt_ref[l, :, lo:mid])
+            if mid < hi:
+                part.append(2.0 * self.gwt_ref[l, :, mid:hi])
+            part = jnp.concatenate(part, 1).T.astype(BF)
+            for j in range(zc):
+                i = g * zc + j
+                self.gb_s[l, i, 0:rows] = part[j * rows : (j + 1) * rows]
+                if l == 1:
+                    continue
+                at = i * vrow // 128 * 128
+                n = min(256, vlen - at)
+                wide = gv[:, at : at + n]
+                if n < 256:
+                    wide = jnp.concatenate([wide, jnp.zeros_like(wide)], 1)
+                if i * vrow > at:
+                    wide = pltpu.roll(wide, 256 - (i * vrow - at), 1)
+                wide = jnp.concatenate([wide, jnp.zeros_like(wide)], 0)
+                self.gb_s[l, i, rows : self.block] = wide.astype(BF)
+            yy, xx, cc = g // 4, g // 2 % 2, g % 2
+            kind = 2 * jnp.abs(self.y - yy) + jnp.abs(self.x - xx)
+
+            @pl.when(self.core == 1 - cc)
+            def _():
+                self.remote(
+                    self.gb_s.at[l, pl.ds(g * zc, zc), pl.ds(0, self.size[l]), :],
+                    self.sib_s.at[l, kind, :, pl.ds(0, self.size[l]), :],
+                    self.rs_core_send.at[l, kind], self.rs_core_recv.at[l, kind],
+                    (self.dp_c, self.z),
+                ).start()
 
     def chip_step(self, l, k):
         t = self.zz(k)
         for kind, slots in ((3, (0, 1)), (1, (3,)), (2, (2,)), (0, ())):
             i = self.index(kind, t)
-            mine, other = self.gb_s[l, i], self.sib_s[l, kind, t]
+            size = self.size[l]
+            mine, other = self.gb_s[l, i, 0:size], self.sib_s[l, kind, t, 0:size]
             if kind == 0:
-                self.own_s[l, t] = mine.astype(F32) + other.astype(F32)
+                self.own_s[l, t, 0:size] = mine.astype(F32) + other.astype(F32)
             else:
-                self.gb_s[l, i] = mine + other
+                self.gb_s[l, i, 0:size] = mine + other
             for slot in slots:
                 self.rs_across(l, slot, t).start()
 
@@ -615,22 +683,23 @@
             (0, 1, 0, self.diag_top_s), (1, 2, 1, self.diag_low_s),
         ):
             self.rs_across(l, slot, t).wait_recv()
-            i, cut = self.index(kind, t), self.cut[half]
-            self.gb_s[l, i, cut] = self.gb_s[l, i, cut] + ref[l, t]
+            i, cut = self.index(kind, t), self.cuts[l][half]
+            self.gb_s[l, i, cut] = self.gb_s[l, i, cut] + ref[l, t, 0 : cut.size]
             self.rs_across(l, 4 if half == 0 else 5, t).start()
 
     def column_step(self, l, k):
         t = self.zz(k)
         for slot in (2, 3, 4, 5):
             self.rs_across(l, slot, t).wait_recv()
-        total = self.own_s[l, t]
+        size = self.size[l]
+        total = self.own_s[l, t, 0:size]
         for a in range(2):
-            total = total + self.cols_s[l, a, t].astype(F32)
+            total = total + self.cols_s[l, a, t, 0:size].astype(F32)
         if k:
-            self.gb_s[l, self.index(0, t)] = total.astype(BF)
+            self.gb_s[l, self.index(0, t), 0:size] = total.astype(BF)
             self.rs_along(l, k).start()
         else:
-            self.own_s[l, t] = total
+            self.own_s[l, t, 0:size] = total
 
     def sum_core(self, l):
         for kind in (3, 1, 2, 0):
@@ -666,11 +735,13 @@
     def sum_end(self, l):
         for k in self.near[1:]:
             self.rs_along(l, k).wait_recv()
-        total = self.own_s[l, self.z]
+        size = self.size[l]
+        total = self.own_s[l, self.z, 0:size]
         for k in self.near[1:]:
-            total = total + self.zr_s[l, k - 1].astype(F32)
+            total = total + self.zr_s[l, k - 1, 0:size].astype(F32)
         self.gw_ref[l] = total[0 : self.rows]
-        self.gvo_ref[l : l + 1, :] = total[self.rows : self.rows + 1, 0 : self.vrow]
+        if l == 0:
+            self.gvo_ref[...] = total[self.rows : self.rows + 2, 0 : self.vrow]
 
     def drain(self):
         for l in range(2):

time: 144 us -> 142 us (0.986)
  Pallas kernels: 135 us -> 133 us
    pallas_call x1, Pallas kernels: 135 us -> 133 us  [compute(): pl.pallas_call(partial(kernel, dims, own, z_count), grid=(n,), in_specs=[...]
where the time goes in v8:
time: 142 us
  Pallas kernels  133 us (94%)
  local copies, waits for them, and re-layouts  8.43 us (6%)
    pallas_call x1, Pallas kernels, compute(): pl.pallas_call(partial(kernel, dims, own, z_count), grid=(n,), in_specs=[...  133 us
    unnamed x10, local copies, waits for them, and re-layouts  8.43 us

profile of v8, /device:TPU:0, one launch (start us, length us, event | category | flops | bytes accessed | tf_op | source)
XLA Modules:
  0.0 142.1 jit_solution(1449677095431740973)
XLA Ops:
  0.6 133.0 %layers.1 = (f32[4,12,12,8,256]{4,3,2,1,0:T(8,128)}, f32[4,12,12,8,256]{4,3,2,1,0:T(8,128)}, f32[2,96,256]{2,1,0:T(8,128)}, f32[2,80]{1,0:T(2,128)}) custom-call(s32[4]{0:T(128)} %refs_0_.1, f32[4,12,12,8,256]{4,3,2,1,0:T(8,128)} %bitcast.4, f32[4,12,12,8,256]{4,3,2,1,0:T(8,128)} %bitcast.5, bf16[2,96,256]{2,1,0:T(8,128)(2,1)} %refs_3_.1, bf16[2,80]{1,0:T(2,128)(2,1)} %refs_4_.1), custom_call_target="tpu_custom_call" | custom-call | tf_op jit(solution)/shard_map/layers/pallas_call | solution.py:820
  133.7 0.0 copy-start
  133.7 5.0 %copy.13 = f32[4608,256]{1,0:T(8,128)} copy(f32[4608,256]{1,0:T(8,128)} %bitcast.7) | data formatting | bytes 9437184
  138.7 0.0 copy-done
  138.7 0.0 copy-start.1
  138.7 0.0 copy-start.2
  138.7 2.2 %copy.14 = f32[4608,256]{1,0:T(8,128)} copy(f32[4608,256]{1,0:T(8,128)S(1)} %bitcast.6) | data formatting | bytes 9437184
  140.9 0.0 copy-done.1
  140.9 0.7 copy.15
  141.5 0.0 copy-done.2
  141.5 0.6 copy.16
Async XLA Ops:
  133.7 5.0 %copy-start = (f32[4,12,12,8,256]{4,3,2,1,0:T(8,128)S(1)}, f32[4,12,12,8,256]{4,3,2,1,0:T(8,128)}, u32[]{:S(2)}) copy-start(f32[4,12,12,8,256]{4,3,2,1,0:T(8,128)} %get-tuple-element.9) | copy-start | bytes 14155780
  138.7 2.2 %copy-start.1 = (f32[2,96,256]{2,1,0:T(8,128)S(1)}, f32[2,96,256]{2,1,0:T(8,128)}, u32[]{:S(2)}) copy-start(f32[2,96,256]{2,1,0:T(8,128)} %get-tuple-element.18) | copy-start | bytes 589828
  138.7 2.9 %copy-start.2 = (f32[2,80]{1,0:T(2,128)S(1)}, f32[2,80]{1,0:T(2,128)}, u32[]{:S(2)}) copy-start(f32[2,80]{1,0:T(2,128)} %get-tuple-element.19) | copy-start | bytes 1924

commit v9 on v8

--- a/solution.py
+++ b/solution.py
@@ -37,10 +37,10 @@
     return jnp.sum(v.reshape(v.shape[0] // 8, 8, v.shape[1]), axis=0)
 
 
-def live_mask(length, slab, width):
-    row = lax.broadcasted_iota(jnp.int32, (ROWS, SUBL, width), 0)
-    col = lax.broadcasted_iota(jnp.int32, (ROWS, SUBL, width), 1)
-    return row * COLS + col + slab * SUBL < length
+def keep_live(length, slab, val):
+    col = lax.broadcasted_iota(jnp.int32, (SUBL, val.shape[2]), 0)
+    left = length - slab * SUBL
+    return jnp.stack([jnp.where(col < left - r * COLS, val[r], 0.0) for r in range(ROWS)])
 
 
 def kernel(dims, own, z_count, *refs):
@@ -221,8 +221,7 @@
 
     def load_gy1():
         for b in range(NBLK):
-            live = live_mask(length, b, d)
-            part = jnp.where(live, cot_ref[0, :, b], 0.0).reshape(BLOCK, d)
+            part = keep_live(length, b, cot_ref[0, :, b]).reshape(BLOCK, d)
             acc_vec(1, 5, part)
             gy_s[b * BLOCK : (b + 1) * BLOCK] = (0.5 * part).astype(BF)
 
@@ -254,7 +253,7 @@
         y = mid_s[l] + vec(l, 5) + mm(act_s[l], wpart(l, 4 * d + ff, 4 * d + 2 * ff), 1, 0)
         y4 = y.reshape(NBLK, NBLK, SUBL, d)
         for b in range(NBLK):
-            out_ref[0, :, b] = jnp.where(live_mask(length, b, d), y4[b], 0.0)
+            out_ref[0, :, b] = keep_live(length, b, y4[b])
 
     def ffn_bwd0(size):
         l, n = 0, ff // d
@@ -305,8 +304,7 @@
             else:
                 parts = []
                 for b in range(c * nb, (c + 1) * nb):
-                    live = live_mask(length, b, d)
-                    parts.append(jnp.where(live, cot_ref[0, :, b], 0.0).reshape(BLOCK, d))
+                    parts.append(keep_live(length, b, cot_ref[0, :, b]).reshape(BLOCK, d))
                 gy = jnp.concatenate(parts, 0)
             gmid = gy + norm_back(l, 3, mid_s[l, r, :], gn2.pop(c))
             gmid_s[r, :] = gmid

time: 142 us -> 142 us (level)
  no operation moved by 1% of the time
where the time goes in v9:
time: 142 us
  Pallas kernels  133 us (94%)
  local copies, waits for them, and re-layouts  8.43 us (6%)
    pallas_call x1, Pallas kernels, compute(): pl.pallas_call(partial(kernel, dims, own, z_count), grid=(n,), in_specs=[...  133 us
    unnamed x10, local copies, waits for them, and re-layouts  8.43 us

profile of v9, /device:TPU:0, one launch (start us, length us, event | category | flops | bytes accessed | tf_op | source)
XLA Modules:
  0.0 142.0 jit_solution(16886339997188240850)
XLA Ops:
  0.6 132.9 %layers.1 = (f32[4,12,12,8,256]{4,3,2,1,0:T(8,128)}, f32[4,12,12,8,256]{4,3,2,1,0:T(8,128)}, f32[2,96,256]{2,1,0:T(8,128)}, f32[2,80]{1,0:T(2,128)}) custom-call(s32[4]{0:T(128)} %refs_0_.1, f32[4,12,12,8,256]{4,3,2,1,0:T(8,128)} %bitcast.4, f32[4,12,12,8,256]{4,3,2,1,0:T(8,128)} %bitcast.5, bf16[2,96,256]{2,1,0:T(8,128)(2,1)} %refs_3_.1, bf16[2,80]{1,0:T(2,128)(2,1)} %refs_4_.1), custom_call_target="tpu_custom_call" | custom-call | tf_op jit(solution)/shard_map/layers/pallas_call | solution.py:818
  133.5 0.0 copy-start
  133.5 5.0 %copy.13 = f32[4608,256]{1,0:T(8,128)} copy(f32[4608,256]{1,0:T(8,128)} %bitcast.7) | data formatting | bytes 9437184
  138.5 0.0 copy-done
  138.5 0.0 copy-start.1
  138.5 0.0 copy-start.2
  138.5 2.2 %copy.14 = f32[4608,256]{1,0:T(8,128)} copy(f32[4608,256]{1,0:T(8,128)S(1)} %bitcast.6) | data formatting | bytes 9437184
  140.7 0.0 copy-done.1
  140.7 0.7 copy.15
  141.4 0.0 copy-done.2
  141.4 0.6 copy.16
Async XLA Ops:
  133.5 5.0 %copy-start = (f32[4,12,12,8,256]{4,3,2,1,0:T(8,128)S(1)}, f32[4,12,12,8,256]{4,3,2,1,0:T(8,128)}, u32[]{:S(2)}) copy-start(f32[4,12,12,8,256]{4,3,2,1,0:T(8,128)} %get-tuple-element.9) | copy-start | bytes 14155780
  138.5 2.2 %copy-start.1 = (f32[2,96,256]{2,1,0:T(8,128)S(1)}, f32[2,96,256]{2,1,0:T(8,128)}, u32[]{:S(2)}) copy-start(f32[2,96,256]{2,1,0:T(8,128)} %get-tuple-element.18) | copy-start | bytes 589828
  138.5 2.9 %copy-start.2 = (f32[2,80]{1,0:T(2,128)S(1)}, f32[2,80]{1,0:T(2,128)}, u32[]{:S(2)}) copy-start(f32[2,80]{1,0:T(2,128)} %get-tuple-element.19) | copy-start | bytes 1924
